TPU v7x, 32 devices: a whole 2x2x4 slice. The times are simulated.
32 devices in a mesh: dp: 8 (over y, x, core), tensor: 4 (over z).
Axes of the slice: x: 2, y: 2, z: 4, core: 2. Of those that a mesh axis runs over, the one named last changes fastest.
Arguments:
- token_ids: int32 [2, 8192], P(None, 'dp'), may hold values from 0 to 50287
- lengths: int32 [2, 8], P(None, 'dp'), may hold values from 170 to 1024, as said below
- loss_pos: int32 [2, 2048], P(None, 'dp'), may hold values from 0 to 1023
- targets: int32 [2, 2048], P(None, 'dp'), may hold values from 0 to 50287
- embed: float32 [12572, 4096], P('tensor', 'dp'), may hold values from -0.375 to 0.375
- embed_m: float32 [12572, 4096], P('tensor', 'dp'), may hold values from -0.001953125 to 0.001953125
- embed_v: float32 [12572, 4096], P('tensor', 'dp'), may hold values from 1.5456417e-08 to 6.1825666e-08
- w_zx: float32 [2, 1024, 2, 2048], P(None, 'dp', None, 'tensor'), may hold values from -0.1875 to 0.1875
- w_zx_m: float32 [2, 1024, 2, 2048], P(None, 'dp', None, 'tensor'), may hold values from -0.001953125 to 0.001953125
- w_zx_v: float32 [2, 1024, 2, 2048], P(None, 'dp', None, 'tensor'), may hold values from 1.5456417e-08 to 6.1825666e-08
- w_bcdt: float32 [2, 1024, 288], P(None, 'dp'), may hold values from -0.1875 to 0.1875
- w_bcdt_m: float32 [2, 1024, 288], P(None, 'dp'), may hold values from -0.001953125 to 0.001953125
- w_bcdt_v: float32 [2, 1024, 288], P(None, 'dp'), may hold values from 1.5456417e-08 to 6.1825666e-08
- w_out: float32 [2, 1024, 2048], P(None, 'dp', 'tensor'), may hold values from -0.125 to 0.125
- w_out_m: float32 [2, 1024, 2048], P(None, 'dp', 'tensor'), may hold values from -0.001953125 to 0.001953125
- w_out_v: float32 [2, 1024, 2048], P(None, 'dp', 'tensor'), may hold values from 1.5456417e-08 to 6.1825666e-08
- channel: float32 [2, 6, 2048], P(None, None, 'tensor'), may hold values from -1 to 1.8
- channel_m: float32 [2, 6, 2048], P(None, None, 'tensor'), may hold values from -0.0078125 to 0.0078125
- channel_v: float32 [2, 6, 2048], P(None, None, 'tensor'), may hold values from 2.4730267e-07 to 9.892107e-07
- per_head: float32 [2, 3, 32], P(None, None, 'tensor'), may hold values from -4.5 to 2.8
- per_head_m: float32 [2, 3, 32], P(None, None, 'tensor'), may hold values from -0.0078125 to 0.0078125
- per_head_v: float32 [2, 3, 32], P(None, None, 'tensor'), may hold values from 2.4730267e-07 to 9.892107e-07
- bc_conv: float32 [2, 5, 256], replicated, may hold values from -1 to 1
- bc_conv_m: float32 [2, 5, 256], replicated, may hold values from -0.0078125 to 0.0078125
- bc_conv_v: float32 [2, 5, 256], replicated, may hold values from 2.4730267e-07 to 9.892107e-07
- gains: float32 [3, 1024], replicated, may hold values from 0.4 to 1.8
- gains_m: float32 [3, 1024], replicated, may hold values from -0.0078125 to 0.0078125
- gains_v: float32 [3, 1024], replicated, may hold values from 2.4730267e-07 to 9.892107e-07
Outputs:
- loss_sum: float32 [], replicated
- loss_count: float32 [], replicated
- grad_norm: float32 [], replicated
- group_norms: float32 [2, 14], replicated
- embed_new: float32 [12572, 4096], P('tensor', 'dp')
- embed_m_new: float32 [12572, 4096], P('tensor', 'dp')
- embed_v_new: float32 [12572, 4096], P('tensor', 'dp')
- w_zx_new: float32 [2, 1024, 2, 2048], P(None, 'dp', None, 'tensor')
- w_zx_m_new: float32 [2, 1024, 2, 2048], P(None, 'dp', None, 'tensor')
- w_zx_v_new: float32 [2, 1024, 2, 2048], P(None, 'dp', None, 'tensor')
- w_bcdt_new: float32 [2, 1024, 288], P(None, 'dp')
- w_bcdt_m_new: float32 [2, 1024, 288], P(None, 'dp')
- w_bcdt_v_new: float32 [2, 1024, 288], P(None, 'dp')
- w_out_new: float32 [2, 1024, 2048], P(None, 'dp', 'tensor')
- w_out_m_new: float32 [2, 1024, 2048], P(None, 'dp', 'tensor')
- w_out_v_new: float32 [2, 1024, 2048], P(None, 'dp', 'tensor')
- channel_new: float32 [2, 6, 2048], P(None, None, 'tensor')
- channel_m_new: float32 [2, 6, 2048], P(None, None, 'tensor')
- channel_v_new: float32 [2, 6, 2048], P(None, None, 'tensor')
- per_head_new: float32 [2, 3, 32], P(None, None, 'tensor')
- per_head_m_new: float32 [2, 3, 32], P(None, None, 'tensor')
- per_head_v_new: float32 [2, 3, 32], P(None, None, 'tensor')
- bc_conv_new: float32 [2, 5, 256], replicated
- bc_conv_m_new: float32 [2, 5, 256], replicated
- bc_conv_v_new: float32 [2, 5, 256], replicated
- gains_new: float32 [3, 1024], replicated
- gains_m_new: float32 [3, 1024], replicated
- gains_v_new: float32 [3, 1024], replicated
Inputs may be any that keep to these rules, and one draw needn't show every extreme that they name: Positions at or past a sequence's length are padding; the lengths of each micro-batch sum to exactly 4776.
All inputs are finite; a program needn't handle non-finite values.
Results may differ from a plain program's by a relative error of at most 0.025.
Values may be sent and summed in bfloat16 or wider, within the bound.
No kernel may reach another device: no remote copies, remote signals or barrier semaphores. Data moves between devices by JAX's collectives and lax.ppermute only.
A program may use at most 448 MiB of HBM per device.

v0:
```python
import jax
import jax.numpy as jnp
from jax import lax
from jax.sharding import PartitionSpec as P

D = 1024
INNER = 2048
HEADS = 32
HDIM = 64
STATE = 128
CONV = 4
SPAN = 256
LAYERS = 2
MICRO = 2
STEP = 5


precise = lax.Precision.HIGHEST
norm_eps = 1e-05
adam_eps = 1e-06
clip_limit = 1.0
first_decay = 0.5
second_decay = 0.5
learn_rate = 0.3
weight_decay = 0.01


def merged(shard, axis, combine):
    everything = jax.tree.map(lambda part: lax.all_gather(part, axis), shard)
    leading = jax.tree.map(lambda part: part[0], everything)

    def turn(k, so_far):
        return combine(so_far, jax.tree.map(lambda part: part[k], everything))

    return lax.fori_loop(1, lax.axis_size(axis), turn, leading)


def rms_scale(values, weights):
    return (
        values * lax.rsqrt(jnp.mean(values * values, axis=-1, keepdims=True) + norm_eps) * weights
    )


def causal_conv(signal, kernel, offset):
    width = kernel.shape[0]
    count = signal.shape[0]
    padded = jnp.pad(signal, ((width - 1, 0), (0, 0)))
    result = offset + padded[:count] * kernel[0]
    for shift_at in range(1, width):
        result = result + padded[shift_at : shift_at + count] * kernel[shift_at]
    return result


def ssd_scan(inputs, step_dt, decay, keys_b, reads_c):
    length, heads, width = inputs.shape
    blocks = length // SPAN
    scaled = (inputs * step_dt[:, :, None]).reshape(blocks, SPAN, heads, width)
    summed = jnp.cumsum(decay.reshape(blocks, SPAN, heads), axis=1)
    keys_q = keys_b.reshape(blocks, SPAN, -1)
    reads_q = reads_c.reshape(blocks, SPAN, -1)
    causal = (jnp.arange(SPAN)[:, None] >= jnp.arange(SPAN)[None, :])[None, :, :, None]
    spread = summed[:, :, None, :] - summed[:, None, :, :]
    fading = jnp.where(causal, jnp.exp(jnp.where(causal, spread, 0.0)), 0.0)
    scores = jnp.einsum("btn,bsn->bts", reads_q, keys_q, precision=precise)
    within = jnp.einsum("bts,btsh,bshp->bthp", scores, fading, scaled, precision=precise)
    to_end = jnp.exp(summed[:, -1:, :] - summed)
    states = jnp.einsum("bsn,bsh,bshp->bhnp", keys_q, to_end, scaled, precision=precise)

    def advance(state, pair):
        fresh, total = pair
        return (state * jnp.exp(total)[:, None, None] + fresh, state)

    _, entering = lax.scan(advance, jnp.zeros_like(states[0]), (states, summed[:, -1, :]))
    across = jnp.einsum("btn,bth,bhnp->bthp", reads_q, jnp.exp(summed), entering, precision=precise)
    return (within + across).reshape(length, heads, width)


def ssd_mixer(gate_in, x_raw, bc_raw, dt_raw, channel, per_head, bc_conv):
    length = gate_in.shape[0]
    heads = per_head.shape[1]
    x_conv = jax.nn.silu(causal_conv(x_raw, channel[:CONV], channel[CONV]))
    bc_out = jax.nn.silu(causal_conv(bc_raw, bc_conv[:CONV], bc_conv[CONV]))
    step_dt = jax.nn.softplus(dt_raw + per_head[0])
    decay = -jnp.exp(per_head[1]) * step_dt
    inputs = x_conv.reshape(length, heads, HDIM)
    mixed = (
        ssd_scan(inputs, step_dt, decay, bc_out[:, :STATE], bc_out[:, STATE:])
        + per_head[2][None, :, None] * inputs
    )
    return mixed.reshape(length, -1) * jax.nn.silu(gate_in)


def rows_gather(values):
    return lax.all_gather(values, "tensor", axis=0, tiled=True)


def rows_sum(values):
    return lax.psum_scatter(values, "tensor", scatter_dimension=0, tiled=True)


def inner_total(values):
    return lax.psum(values, "tensor")


def shard_gather(embed, w_zx, w_bcdt, w_out):
    return (
        lax.all_gather(embed.astype(jnp.bfloat16), "dp", axis=1, tiled=True),
        lax.all_gather(w_zx.astype(jnp.bfloat16), "dp", axis=1, tiled=True),
        lax.all_gather(w_bcdt.astype(jnp.bfloat16), "dp", axis=1, tiled=True),
        lax.all_gather(w_out.astype(jnp.bfloat16), "dp", axis=1, tiled=True),
    )


def reduce_end(local, vocab_rows):
    grad_table, grad_zx, grad_bcdt, grad_out, grad_gains, grad_channel, grad_head, grad_bc_conv = (
        local
    )
    grad_bcdt, grad_bc_conv, grad_gains = (
        lax.psum(grad_bcdt.astype(jnp.bfloat16), "tensor").astype(jnp.float32),
        lax.psum(grad_bc_conv.astype(jnp.bfloat16), "tensor").astype(jnp.float32),
        lax.psum(grad_gains.astype(jnp.bfloat16), "tensor").astype(jnp.float32),
    )
    grad_lines = grad_table.reshape(vocab_rows // 4, 4 * D)
    grad_lines, grad_zx, grad_bcdt, grad_out = (
        lax.psum_scatter(
            grad_lines.astype(jnp.bfloat16), "dp", scatter_dimension=1, tiled=True
        ).astype(jnp.float32),
        lax.psum_scatter(
            grad_zx.astype(jnp.bfloat16), "dp", scatter_dimension=1, tiled=True
        ).astype(jnp.float32),
        lax.psum_scatter(
            grad_bcdt.astype(jnp.bfloat16), "dp", scatter_dimension=1, tiled=True
        ).astype(jnp.float32),
        lax.psum_scatter(
            grad_out.astype(jnp.bfloat16), "dp", scatter_dimension=1, tiled=True
        ).astype(jnp.float32),
    )
    grad_channel, grad_head, grad_bc_conv, grad_gains = (
        lax.psum(grad_channel.astype(jnp.bfloat16), "dp").astype(jnp.float32),
        lax.psum(grad_head.astype(jnp.bfloat16), "dp").astype(jnp.float32),
        lax.psum(grad_bc_conv.astype(jnp.bfloat16), "dp").astype(jnp.float32),
        lax.psum(grad_gains.astype(jnp.bfloat16), "dp").astype(jnp.float32),
    )
    return (
        grad_lines,
        grad_zx,
        grad_bcdt,
        grad_out,
        grad_channel,
        grad_head,
        grad_bc_conv,
        grad_gains,
    )


def contract(left, right, left_dim, right_dim):
    return lax.dot_general(
        left, right, (((left_dim,), (right_dim,)), ((), ())), preferred_element_type=jnp.float32
    )


def layer_front(resid, matrices, smalls):
    w_zx, w_bcdt, w_out = matrices
    gain, channel, per_head, bc_conv = smalls
    normed_own = rms_scale(resid, gain).astype(jnp.bfloat16)
    normed = rows_gather(normed_own)
    zx = jnp.einsum("td,dki->tki", normed, w_zx, preferred_element_type=jnp.float32)
    bcdt = jnp.dot(normed, w_bcdt, preferred_element_type=jnp.float32)
    heads = per_head.shape[1]
    dt_raw = lax.dynamic_slice_in_dim(bcdt, 2 * STATE + lax.axis_index("tensor") * heads, heads, 1)
    mixer_args = (zx[:, 0], zx[:, 1], bcdt[:, : 2 * STATE], dt_raw, channel, per_head, bc_conv)
    gated = ssd_mixer(
        mixer_args[0],
        mixer_args[1],
        mixer_args[2],
        mixer_args[3],
        mixer_args[4],
        mixer_args[5],
        mixer_args[6],
    )
    inverse = lax.rsqrt(inner_total(jnp.sum(gated * gated, axis=1)) / INNER + norm_eps)
    scaled = (gated * inverse[:, None] * channel[CONV + 1]).astype(jnp.bfloat16)
    return (normed_own, normed, mixer_args, gated, inverse, scaled)


def layer_forward(resid, matrices, smalls):
    scaled = layer_front(resid, matrices, smalls)[5]
    return resid + rows_sum(contract(scaled, matrices[2], 1, 1))


def layer_backward(resid, grad_out, matrices, smalls):
    w_zx, w_bcdt, w_out = matrices
    gain, channel, per_head, bc_conv = smalls
    normed_own, normed, mixer_args, gated, inverse, scaled = layer_front(resid, matrices, smalls)
    grad_rows = rows_gather(grad_out.astype(jnp.bfloat16))
    grad_w_out = contract(grad_rows, scaled, 0, 0)
    grad_scaled = contract(grad_rows, w_out, 1, 0)
    norm_gain = channel[CONV + 1]
    along = inner_total(jnp.sum(grad_scaled * norm_gain * gated, axis=1))
    grad_gated = (
        inverse[:, None] * norm_gain * grad_scaled - gated * (inverse**3 * along / INNER)[:, None]
    )
    _, pull = jax.vjp(
        ssd_mixer,
        mixer_args[0],
        mixer_args[1],
        mixer_args[2],
        mixer_args[3],
        mixer_args[4],
        mixer_args[5],
        mixer_args[6],
    )
    grad_z, grad_x, grad_bc, grad_dt, grad_channel, grad_head, grad_bc_conv = pull(grad_gated)
    grad_channel = grad_channel.at[CONV + 1].add(
        jnp.sum(grad_scaled * gated * inverse[:, None], axis=0)
    )
    grad_zx = jnp.stack([grad_z, grad_x], axis=1).astype(jnp.bfloat16)
    heads = per_head.shape[1]
    grad_dt_all = lax.dynamic_update_slice_in_dim(
        jnp.zeros((grad_dt.shape[0], HEADS), jnp.float32),
        grad_dt,
        lax.axis_index("tensor") * heads,
        1,
    )
    grad_bcdt_part = jnp.concatenate([grad_bc, grad_dt_all], axis=1)
    grad_normed_part = jnp.einsum("tki,dki->td", grad_zx, w_zx, preferred_element_type=jnp.float32)
    grad_normed, grad_bcdt = rows_sum((grad_normed_part, grad_bcdt_part))
    grad_bcdt = grad_bcdt.astype(jnp.bfloat16)
    grad_normed = grad_normed + contract(grad_bcdt, w_bcdt, 1, 1)
    grad_w_zx = jnp.einsum("td,tki->dki", normed, grad_zx, preferred_element_type=jnp.float32)
    grad_w_bcdt = contract(normed_own, grad_bcdt, 0, 0)
    _, pull_norm = jax.vjp(rms_scale, resid, gain)
    grad_resid, grad_gain = pull_norm(grad_normed)
    return (
        grad_out + grad_resid,
        (grad_w_zx, grad_w_bcdt, grad_w_out),
        (grad_gain, grad_channel, grad_head, grad_bc_conv),
    )


def lse_merge(first, second):
    top = jnp.maximum(first[0], second[0])
    return (
        top,
        first[1] * jnp.exp(first[0] - top) + second[1] * jnp.exp(second[0] - top),
        first[2] + second[2],
    )


def vocab_forward(resid, table, gain, positions, target_row, length):
    final = rows_gather(rms_scale(resid, gain).astype(jnp.bfloat16))
    chosen = jnp.take(final, positions, axis=0)
    logits = contract(chosen, table, 1, 1)
    vocab_rows = table.shape[0]
    local_target = target_row - lax.axis_index("tensor") * vocab_rows
    target_hit = jnp.arange(vocab_rows)[None, :] == local_target[:, None]
    highest = jnp.max(logits, axis=1)
    pieces = (
        highest,
        jnp.sum(jnp.exp(logits - highest[:, None]), axis=1),
        jnp.sum(jnp.where(target_hit, logits, 0.0), axis=1),
    )
    top_all, total_all, picked = merged(pieces, "tensor", lse_merge)
    log_total = top_all + jnp.log(total_all)
    counted = (positions < length).astype(jnp.float32)
    grad_logits = (
        counted[:, None] * (jnp.exp(logits - log_total[:, None]) - target_hit.astype(jnp.float32))
    ).astype(jnp.bfloat16)
    grad_table = contract(grad_logits, chosen, 0, 0)
    return (jnp.sum(counted * (log_total - picked)), jnp.sum(counted), grad_logits, grad_table)


def vocab_backward(resid, gain, positions, grad_logits, table):
    chosen_grad = jnp.dot(grad_logits, table, preferred_element_type=jnp.float32)
    all_rows = resid.shape[0] * lax.axis_size("tensor")
    placed = jnp.zeros((all_rows, resid.shape[1]), jnp.float32).at[positions].add(chosen_grad)
    _, pull_norm = jax.vjp(rms_scale, resid, gain)
    return pull_norm(rows_sum(placed))


def adapt(weight, first, second, grad):
    first_new = first_decay * first + (1.0 - first_decay) * grad
    second_new = second_decay * second + (1.0 - second_decay) * grad * grad
    update = (
        first_new
        / (1.0 - first_decay**STEP)
        / (jnp.sqrt(second_new / (1.0 - second_decay**STEP)) + adam_eps)
        + weight_decay * weight
    )
    return (first_new, second_new, update)


def group_squares(values, stacked):
    if stacked:
        return jnp.sum(values * values, axis=tuple(range(1, values.ndim)))
    return jnp.sum(values * values)[None]


def body(
    token_ids,
    lengths,
    loss_pos,
    targets,
    embed,
    embed_m,
    embed_v,
    w_zx,
    w_zx_m,
    w_zx_v,
    w_bcdt,
    w_bcdt_m,
    w_bcdt_v,
    w_out,
    w_out_m,
    w_out_v,
    channel,
    channel_m,
    channel_v,
    per_head,
    per_head_m,
    per_head_v,
    bc_conv,
    bc_conv_m,
    bc_conv_v,
    gains,
    gains_m,
    gains_v,
):
    n_tensor = lax.axis_size("tensor")
    n_data = lax.axis_size("dp")
    vocab_rows = embed.shape[0] * 4
    gathered = shard_gather(embed, w_zx, w_bcdt, w_out)
    local = (
        jnp.zeros((vocab_rows, D), jnp.float32),
        jnp.zeros((LAYERS, D) + w_zx.shape[2:], jnp.float32),
        jnp.zeros((LAYERS, D, w_bcdt.shape[2]), jnp.float32),
        jnp.zeros((LAYERS, D, w_out.shape[2]), jnp.float32),
        jnp.zeros_like(gains),
        jnp.zeros_like(channel),
        jnp.zeros_like(per_head),
        jnp.zeros_like(bc_conv),
    )
    owned = None
    loss_sum = jnp.zeros((), jnp.float32)
    loss_count = jnp.zeros((), jnp.float32)
    for micro in range(MICRO):
        (
            grad_table,
            grad_zx,
            grad_bcdt,
            grad_out,
            grad_gains,
            grad_channel,
            grad_head,
            grad_bc_conv,
        ) = local
        table = gathered[0].reshape(vocab_rows, D)
        local_ids = token_ids[micro] - lax.axis_index("tensor") * vocab_rows
        inside = (local_ids >= 0) & (local_ids < vocab_rows)
        safe_ids = jnp.clip(local_ids, 0, vocab_rows - 1)
        resid = rows_sum(
            jnp.where(inside[:, None], jnp.take(table, safe_ids, axis=0).astype(jnp.float32), 0.0)
        )
        kept = []
        for depth in range(LAYERS):
            kept.append(resid)
            matrices = (gathered[1][depth], gathered[2][depth], gathered[3][depth])
            resid = layer_forward(
                resid, matrices, (gains[depth], channel[depth], per_head[depth], bc_conv[depth])
            )
        loss_part, count_part, grad_logits, head_table = vocab_forward(
            resid, table, gains[LAYERS], loss_pos[micro], targets[micro], lengths[micro, 0]
        )
        loss_sum = loss_sum + loss_part
        loss_count = loss_count + count_part
        table = gathered[0].reshape(vocab_rows, D)
        grad_resid, grad_final = vocab_backward(
            resid, gains[LAYERS], loss_pos[micro], grad_logits, table
        )
        grad_gains = grad_gains.at[LAYERS].add(grad_final)
        for depth in reversed(range(LAYERS)):
            matrices = (gathered[1][depth], gathered[2][depth], gathered[3][depth])
            grad_resid, matrix_grads, small_grads = layer_backward(
                kept[depth],
                grad_resid,
                matrices,
                (gains[depth], channel[depth], per_head[depth], bc_conv[depth]),
            )
            grad_zx = grad_zx.at[depth].add(matrix_grads[0])
            grad_bcdt = grad_bcdt.at[depth].add(matrix_grads[1])
            grad_out = grad_out.at[depth].add(matrix_grads[2])
            grad_gains = grad_gains.at[depth].add(small_grads[0])
            grad_channel = grad_channel.at[depth].add(small_grads[1])
            grad_head = grad_head.at[depth].add(small_grads[2])
            grad_bc_conv = grad_bc_conv.at[depth].add(small_grads[3])
        grad_first = rows_gather(grad_resid.astype(jnp.bfloat16))
        grad_table = grad_table + head_table
        grad_table = grad_table.at[safe_ids].add(
            jnp.where(inside[:, None], grad_first.astype(jnp.float32), 0.0)
        )
        local = (
            grad_table,
            grad_zx,
            grad_bcdt,
            grad_out,
            grad_gains,
            grad_channel,
            grad_head,
            grad_bc_conv,
        )
    owned = reduce_end(local, vocab_rows)
    grad_table, grad_zx, grad_bcdt, grad_out, grad_channel, grad_head, grad_bc_conv, grad_gains = (
        owned
    )
    everyone = n_tensor * n_data
    kinds = (
        (embed, embed_m, embed_v, grad_table, False, 1),
        (w_zx, w_zx_m, w_zx_v, grad_zx, True, 1),
        (w_bcdt, w_bcdt_m, w_bcdt_v, grad_bcdt, True, n_tensor),
        (w_out, w_out_m, w_out_v, grad_out, True, 1),
        (channel, channel_m, channel_v, grad_channel, True, n_data),
        (per_head, per_head_m, per_head_v, grad_head, True, n_data),
        (bc_conv, bc_conv_m, bc_conv_v, grad_bc_conv, True, everyone),
        (gains, gains_m, gains_v, grad_gains, False, everyone),
    )
    grad_sq = jnp.concatenate([group_squares(kind[3], kind[4]) / kind[5] for kind in kinds])
    weight_sq = jnp.concatenate([group_squares(kind[0], kind[4]) / kind[5] for kind in kinds])
    grad_sq, weight_sq, totals = lax.psum(
        (grad_sq, weight_sq, jnp.stack([loss_sum, loss_count]) / n_tensor), ("dp", "tensor")
    )
    grad_norm = jnp.sqrt(jnp.sum(grad_sq))
    scale = jnp.minimum(1.0, clip_limit / grad_norm)
    moved = [adapt(kind[0], kind[1], kind[2], kind[3] * scale) for kind in kinds]
    step_sq = jnp.concatenate(
        [group_squares(change[2], kind[4]) / kind[5] for change, kind in zip(moved, kinds)]
    )
    step_sq = lax.psum(step_sq, ("dp", "tensor"))
    weight_norm = jnp.sqrt(weight_sq)
    step_norm = jnp.sqrt(step_sq)
    trust_all = weight_norm / step_norm
    results = []
    offset = 0
    for kind, change in zip(kinds, moved):
        weight = kind[0]
        if kind[4]:
            factor = trust_all[offset : offset + weight.shape[0]].reshape(
                (weight.shape[0],) + (1,) * (weight.ndim - 1)
            )
            offset = offset + weight.shape[0]
        else:
            factor = trust_all[offset]
            offset = offset + 1
        results += [weight - learn_rate * factor * change[2], change[0], change[1]]
    group_norms = jnp.stack([weight_norm, step_norm])
    return (
        totals[0],
        totals[1],
        grad_norm,
        group_norms,
        results[0],
        results[1],
        results[2],
        results[3],
        results[4],
        results[5],
        results[6],
        results[7],
        results[8],
        results[9],
        results[10],
        results[11],
        results[12],
        results[13],
        results[14],
        results[15],
        results[16],
        results[17],
        results[18],
        results[19],
        results[20],
        results[21],
        results[22],
        results[23],
    )


def solution(mesh):
    in_specs = (
        P(None, "dp"),
        P(None, "dp"),
        P(None, "dp"),
        P(None, "dp"),
        P("tensor", "dp"),
        P("tensor", "dp"),
        P("tensor", "dp"),
        P(None, "dp", None, "tensor"),
        P(None, "dp", None, "tensor"),
        P(None, "dp", None, "tensor"),
        P(None, "dp", None),
        P(None, "dp", None),
        P(None, "dp", None),
        P(None, "dp", "tensor"),
        P(None, "dp", "tensor"),
        P(None, "dp", "tensor"),
        P(None, None, "tensor"),
        P(None, None, "tensor"),
        P(None, None, "tensor"),
        P(None, None, "tensor"),
        P(None, None, "tensor"),
        P(None, None, "tensor"),
        P(),
        P(),
        P(),
        P(),
        P(),
        P(),
    )
    out_specs = (
        P(),
        P(),
        P(),
        P(),
        P("tensor", "dp"),
        P("tensor", "dp"),
        P("tensor", "dp"),
        P(None, "dp", None, "tensor"),
        P(None, "dp", None, "tensor"),
        P(None, "dp", None, "tensor"),
        P(None, "dp", None),
        P(None, "dp", None),
        P(None, "dp", None),
        P(None, "dp", "tensor"),
        P(None, "dp", "tensor"),
        P(None, "dp", "tensor"),
        P(None, None, "tensor"),
        P(None, None, "tensor"),
        P(None, None, "tensor"),
        P(None, None, "tensor"),
        P(None, None, "tensor"),
        P(None, None, "tensor"),
        P(),
        P(),
        P(),
        P(),
        P(),
        P(),
    )
    return jax.shard_map(body, mesh=mesh, in_specs=in_specs, out_specs=out_specs, check_vma=False)
```

profile of v0, /device:TPU:0, one launch (start us, length us, event | category | flops | bytes accessed | tf_op | source)
XLA Modules:
  0.0 3086.5 jit_solution(3433903649638819367)
XLA Ops:
  13.6 134.4 %all-gather.29.cloned.1.call-done = bf16[3143,4096]{1,0:T(8,128)(2,1)} async-done(((bf16[3143,512]{1,0:T(8,128)(2,1)}), bf16[3143,4096]{1,0:T(8,128)(2,1)}) %all-gather.29.cloned.1.call-update) | async-done | bytes 25747472 | tf_op jit(solution)/shard_map/all_gather | solution.py:107
  147.9 40.7 %reshape.2394 = bf16[12572,1024]{1,0:T(8,128)(2,1)} reshape(bf16[3143,4096]{1,0:T(8,128)(2,1)} %all-gather.29.cloned.1.call-done) | data formatting | bytes 51494912 | tf_op jit(solution)/shard_map/reshape | solution.py:357
  188.6 16.6 gather_fusion.2
  207.9 17.4 gather_fusion
  230.2 54.5 %reduce-scatter.29.cloned.1.call-done = f32[256,1024]{1,0:T(8,128)} async-done(((f32[1024,1024]{1,0:T(8,128)}), f32[256,1024]{1,0:T(8,128)}) %reduce-scatter.29.cloned.1.call-update) | async-done | bytes 1048592 | tf_op jit(solution)/shard_map/reduce_scatter | solution.py:98
  286.2 78.8 %reduce-scatter.23.cloned.1.call-done = f32[256,1024]{1,0:T(8,128)} async-done(((f32[1024,1024]{1,0:T(8,128)}), f32[256,1024]{1,0:T(8,128)}) %reduce-scatter.23.cloned.1.call-update) | async-done | bytes 1048592 | tf_op jit(solution)/shard_map/reduce_scatter | solution.py:98
  374.5 17.6 all-gather.33.cloned.1.call-done
  392.0 48.0 %all-gather.31.cloned.1.call-done = bf16[1024,1024]{1,0:T(8,128)(2,1)} async-done(((bf16[256,1024]{1,0:T(8,128)(2,1)}), bf16[1024,1024]{1,0:T(8,128)(2,1)}) %all-gather.31.cloned.1.call-update) | async-done | bytes 2097168 | tf_op jit(solution)/shard_map/all_gather | solution.py:94
  444.6 42.1 %all-gather.43.cloned.1.call-done = bf16[1024,1024]{1,0:T(8,128)(2,1)} async-done(((bf16[256,1024]{1,0:T(8,128)(2,1)}), bf16[1024,1024]{1,0:T(8,128)(2,1)}) %all-gather.43.cloned.1.call-update) | async-done | bytes 2097168 | tf_op jit(solution)/shard_map/all_gather | solution.py:94
  494.8 29.8 all-gather.35.cloned.1.call-done
  566.2 18.9 while.290
  693.1 74.1 %reduce-scatter.31.cloned.1.call-done = f32[256,1024]{1,0:T(8,128)} async-done(((f32[1024,1024]{1,0:T(8,128)}), f32[256,1024]{1,0:T(8,128)}) %reduce-scatter.31.cloned.1.call-update) | async-done | bytes 1048592 | tf_op jit(solution)/shard_map/reduce_scatter | solution.py:98
  770.8 46.4 %all-gather.45.cloned.1.call-done = bf16[1024,1024]{1,0:T(8,128)(2,1)} async-done(((bf16[256,1024]{1,0:T(8,128)(2,1)}), bf16[1024,1024]{1,0:T(8,128)(2,1)}) %all-gather.45.cloned.1.call-update) | async-done | bytes 2097168 | tf_op jit(solution)/shard_map/all_gather | solution.py:94
  850.9 15.2 while.293
  917.5 69.8 %reduce-scatter.33.cloned.1.call-done = f32[256,1024]{1,0:T(8,128)} async-done(((f32[1024,1024]{1,0:T(8,128)}), f32[256,1024]{1,0:T(8,128)}) %reduce-scatter.33.cloned.1.call-update) | async-done | bytes 1048592 | tf_op jit(solution)/shard_map/reduce_scatter | solution.py:98
  993.8 73.0 %reduce-scatter.25.cloned.1.call-done = f32[256,1024]{1,0:T(8,128)} async-done(((f32[1024,1024]{1,0:T(8,128)}), f32[256,1024]{1,0:T(8,128)}) %reduce-scatter.25.cloned.1.call-update) | async-done | bytes 1048592 | tf_op jit(solution)/shard_map/reduce_scatter | solution.py:98
  1070.4 44.6 %all-gather.47.cloned.1.call-done = bf16[1024,1024]{1,0:T(8,128)(2,1)} async-done(((bf16[256,1024]{1,0:T(8,128)(2,1)}), bf16[1024,1024]{1,0:T(8,128)(2,1)}) %all-gather.47.cloned.1.call-update) | async-done | bytes 2097168 | tf_op jit(solution)/shard_map/all_gather | solution.py:94
  1118.4 15.4 fusion.633
  1168.4 15.7 fusion.579
  1194.6 13.3 while.298
  1247.0 17.5 reduce-scatter.45.cloned.1.call-done
  1386.4 21.0 while.299
  1416.1 13.6 fusion.79
  1511.1 15.3 fusion.634
  1562.3 15.8 fusion.578
  1601.3 75.6 %reduce-scatter.35.cloned.1.call-done = f32[256,1024]{1,0:T(8,128)} async-done(((f32[1024,1024]{1,0:T(8,128)}), f32[256,1024]{1,0:T(8,128)}) %reduce-scatter.35.cloned.1.call-update) | async-done | bytes 1048592 | tf_op jit(solution)/shard_map/reduce_scatter | solution.py:98
  1685.4 19.0 while.300
  1740.4 16.2 while.294
  1835.6 20.7 while.295
  1889.6 18.7 fusion.81
  1984.8 16.1 while.296
  2044.8 23.5 while.301
  2170.0 20.7 while.297
  2205.1 14.2 fusion.77
  2333.1 64.2 %reduce-scatter.41.cloned.1.call-done = f32[256,1024]{1,0:T(8,128)} async-done(((f32[1024,1024]{1,0:T(8,128)}), f32[256,1024]{1,0:T(8,128)}) %reduce-scatter.41.cloned.1.call-update) | async-done | bytes 1048592 | tf_op jit(solution)/shard_map/reduce_scatter | solution.py:98
  2399.2 78.1 %reduce-scatter.51.cloned.1.call-done = f32[256,1024]{1,0:T(8,128)} async-done(((f32[1024,1024]{1,0:T(8,128)}), f32[256,1024]{1,0:T(8,128)}) %reduce-scatter.51.cloned.1.call-update) | async-done | bytes 1048592 | tf_op jit(solution)/shard_map/reduce_scatter | solution.py:98
  2534.9 25.1 fusion.464
  2560.1 39.7 %convolution_add_fusion = f32[12572,1024]{1,0:T(8,128)} fusion(f32[12572,1024]{1,0:T(8,128)} %fusion.464, bf16[256,1024]{1,0:T(8,128)(2,1)S(1)} %copy-done.167, pred[256]{0:T(512)(128)(4,1)S(1)} %copy-done.399, f32[256,12572]{0,1:T(8,128)} %get-tuple-element.3148, f32[256]{0:T(256)S(1)} %copy-done.325, f32[256]{0:T(256)S(1)} %copy-done.356, ...), kind=kOutput, calls=%fused_computation.104 | convolution fusion | flops 6623795200 | bytes 116391168 | tf_op jit(solution)/shard_map/dot_general | solution.py:157
  2603.7 43.8 %scatter_fusion = f32[12572,1024]{1,0:T(8,128)} fusion(f32[12572,1024]{1,0:T(8,128)} %convolution_add_fusion, s32[1024]{0:T(1024)S(1)} %bitcast.1350, f32[1024,1024]{1,0:T(8,128)} %convert_select_fusion.1), kind=kCustom, calls=%fused_computation.5 | custom fusion | flops 1048576 | bytes 12587008 | tf_op jit(solution)/shard_map/scatter-add | solution.py:398
  2651.6 43.2 %scatter_fusion.1 = f32[12572,1024]{1,0:T(8,128)} fusion(f32[12572,1024]{1,0:T(8,128)} %scatter_fusion, s32[1024]{0:T(1024)S(1)} %bitcast.1349, f32[1024,1024]{1,0:T(8,128)} %convert_select_fusion), kind=kCustom, calls=%fused_computation.7 | custom fusion | flops 1048576 | bytes 12587008 | tf_op jit(solution)/shard_map/scatter-add | solution.py:398
  2694.8 27.2 convert_element_type.241
  2722.0 40.7 %convert_element_type.242 = bf16[3143,4096]{1,0:T(8,128)(2,1)} reshape(bf16[12572,1024]{1,0:T(8,128)(2,1)} %convert_element_type.241) | data formatting | bytes 51494912 | tf_op jit(solution)/shard_map/convert_element_type | solution.py:126
  2784.9 18.7 all-reduce.122
  2803.6 24.0 all-reduce.121
  2829.7 95.5 %reduce-scatter.55.cloned.1.call-done = bf16[3143,512]{1,0:T(8,128)(2,1)} async-done(((bf16[3143,4096]{1,0:T(8,128)(2,1)}), bf16[3143,512]{1,0:T(8,128)(2,1)}) %reduce-scatter.55.cloned.1.call-update) | async-done | bytes 3218448 | tf_op jit(solution)/shard_map/reduce_scatter | solution.py:125
  2931.8 39.8 %psum.161 = f32[14]{0:T(128)S(1)} all-reduce(f32[14]{0:T(128)} %concatenate.99), channel_id=1, replica_groups=mesh['dp'=8,'tensor'=4] {'dp','tensor'}, use_global_device_ids=true, to_apply=%region_216.220 | all-reduce | flops 14 | bytes 112 | tf_op jit(solution)/shard_map/psum | solution.py:428
  2983.0 13.6 multiply_reduce_fusion.1
  3003.6 41.4 %all-reduce.117 = (f32[2]{0:T(128)S(1)}, f32[14]{0:T(128)S(1)}, f32[14]{0:T(128)S(1)}) all-reduce(f32[2]{0:T(128)} %maximum_multiply_fusion, f32[14]{0:T(128)S(1)} %concatenate.101, f32[14]{0:T(128)} %concatenate.100), channel_id=1, replica_groups=mesh['dp'=8,'tensor'=4] {'dp','tensor'}, use_global_device_ids=true, to_apply=%region_50.53 | all-reduce | flops 30 | bytes 240 | tf_op jit(solution)/shard_map/psum | solution.py:428
  (1884 shorter events, 1477.5 us)
Async XLA Ops:
  7.2 140.7 %all-gather.29.cloned.1.call-start = ((), (), s32[]{:S(2)}) async-start(), calls=%async_computation.20 | async-start | bytes 28975104 | tf_op jit(solution)/shard_map/all_gather | solution.py:107
  12.2 272.6 %reduce-scatter.29.cloned.1.call-start = ((), (), s32[]{:S(2)}) async-start(), calls=%async_computation.30 | async-start | bytes 5242880 | tf_op jit(solution)/shard_map/reduce_scatter | solution.py:98
  12.9 192.3 %copy-start.351 = (pred[1024]{0:T(1024)(128)(4,1)}, pred[1024]{0:T(1024)(128)(4,1)S(1)}, u32[]{:S(2)}) copy-start(pred[1024]{0:T(1024)(128)(4,1)S(1)} %get-tuple-element.2649) | copy-start | bytes 3076
  12.9 212.4 %copy-start.353 = (pred[1024]{0:T(1024)(128)(4,1)}, pred[1024]{0:T(1024)(128)(4,1)S(1)}, u32[]{:S(2)}) copy-start(pred[1024]{0:T(1024)(128)(4,1)S(1)} %get-tuple-element.2650) | copy-start | bytes 3076
  207.9 157.2 %reduce-scatter.23.cloned.1.call-start = ((), (), s32[]{:S(2)}) async-start(), calls=%async_computation.21 | async-start | bytes 5242880 | tf_op jit(solution)/shard_map/reduce_scatter | solution.py:98
  227.9 164.1 %all-gather.33.cloned.1.call-start = ((), (), s32[]{:S(2)}) async-start(), calls=%async_computation.23 | async-start | bytes 1327104 | tf_op jit(solution)/shard_map/all_gather | solution.py:109
  229.6 210.4 %all-gather.31.cloned.1.call-start = ((), (), s32[]{:S(2)}) async-start(), calls=%async_computation.22 | async-start | bytes 2621440 | tf_op jit(solution)/shard_map/all_gather | solution.py:94
  230.2 838.1 %copy-start.241 = (f32[1,1024]{1,0:T(1,128)}, f32[1,1024]{1,0:T(1,128)S(1)}, u32[]{:S(2)}) copy-start(f32[1,1024]{1,0:T(1,128)S(1)} %get-tuple-element.3069) | copy-start | bytes 12292
  369.1 117.6 %all-gather.43.cloned.1.call-start = ((), (), s32[]{:S(2)}) async-start(), calls=%async_computation.31 | async-start | bytes 2621440 | tf_op jit(solution)/shard_map/all_gather | solution.py:94
  369.7 154.9 %all-gather.35.cloned.1.call-start = ((), (), s32[]{:S(2)}) async-start(), calls=%async_computation.24 | async-start | bytes 4718592 | tf_op jit(solution)/shard_map/all_gather | solution.py:108
  370.7 317.1 %all-gather.37.cloned.1.call-start = ((), (), s32[]{:S(2)}) async-start(), calls=%async_computation.25 | async-start | bytes 2359296 | tf_op jit(solution)/shard_map/all_gather | solution.py:110
  371.5 395.6 %reduce-scatter.31.cloned.1.call-start = ((), (), s32[]{:S(2)}) async-start(), calls=%async_computation.32 | async-start | bytes 5242880 | tf_op jit(solution)/shard_map/reduce_scatter | solution.py:98
  373.7 538.4 %copy-start.258 = (f32[1,1,512]{2,0,1:T(1,128)}, f32[1,1,512]{2,0,1:T(1,128)S(1)}, u32[]{:S(2)}) copy-start(f32[1,1,512]{2,0,1:T(1,128)S(1)} %get-tuple-element.3061) | copy-start | bytes 6148
  374.5 295.1 %copy-start.270 = (f32[512]{0:T(512)}, f32[512]{0:T(512)S(1)}, u32[]{:S(2)}) copy-start(f32[512]{0:T(512)S(1)} %mul.2952) | copy-start | bytes 6148
  693.0 124.2 %all-gather.45.cloned.1.call-start = ((), (), s32[]{:S(2)}) async-start(), calls=%async_computation.33 | async-start | bytes 2621440 | tf_op jit(solution)/shard_map/all_gather | solution.py:94
  770.6 216.8 %reduce-scatter.33.cloned.1.call-start = ((), (), s32[]{:S(2)}) async-start(), calls=%async_computation.34 | async-start | bytes 5242880 | tf_op jit(solution)/shard_map/reduce_scatter | solution.py:98
  840.4 350.7 %copy-start.7 = (f32[4,256,8,64]{1,0,3,2:T(4,128)}, f32[4,256,8,64]{1,0,3,2:T(4,128)S(1)}, u32[]{:S(2)}) copy-start(f32[4,256,8,64]{1,0,3,2:T(4,128)S(1)} %reshape.2421) | copy-start | bytes 6291460
  906.7 451.8 %copy-start.249 = (f32[1024]{0:T(1024)}, f32[1024]{0:T(1024)S(1)}, u32[]{:S(2)}) copy-start(f32[1024]{0:T(1024)S(1)} %add_rsqrt_fusion) | copy-start | bytes 12292
  912.0 154.8 %reduce-scatter.25.cloned.1.call-start = ((), (), s32[]{:S(2)}) async-start(), calls=%async_computation.26 | async-start | bytes 5242880 | tf_op jit(solution)/shard_map/reduce_scatter | solution.py:98
  917.5 197.4 %all-gather.47.cloned.1.call-start = ((), (), s32[]{:S(2)}) async-start(), calls=%async_computation.35 | async-start | bytes 2621440 | tf_op jit(solution)/shard_map/all_gather | solution.py:94
  988.8 277.8 %copy-start.278 = (f32[256]{0:T(256)}, f32[256]{0:T(256)S(1)}, u32[]{:S(2)}) copy-start(f32[256]{0:T(256)S(1)} %fusion.552) | copy-start | bytes 3076
  991.4 222.8 %all-gather.39.cloned.1.call-start = ((), (), s32[]{:S(2)}) async-start(), calls=%async_computation.27 | async-start | bytes 2621440 | tf_op jit(solution)/shard_map/all_gather | solution.py:94
  1070.3 194.2 %reduce-scatter.45.cloned.1.call-start = ((), (), s32[]{:S(2)}) async-start(), calls=%async_computation.44 | async-start | bytes 5242880 | tf_op jit(solution)/shard_map/reduce_scatter | solution.py:98
  1189.1 126.1 %all-gather.55.cloned.1.call-start = ((), (), s32[]{:S(2)}) async-start(), calls=%async_computation.45 | async-start | bytes 2621440 | tf_op jit(solution)/shard_map/all_gather | solution.py:94
  1268.5 170.9 %reduce-scatter.27.cloned.1.call-start = ((), (), s32[]{:S(2)}) async-start(), calls=%async_computation.28 | async-start | bytes 5242880 | tf_op jit(solution)/shard_map/reduce_scatter | solution.py:98
  1335.3 172.3 %all-gather.41.cloned.1.call-start = ((), (), s32[]{:S(2)}) async-start(), calls=%async_computation.29 | async-start | bytes 2621440 | tf_op jit(solution)/shard_map/all_gather | solution.py:94
  1441.3 238.1 %copy-start.276 = (f32[256]{0:T(256)}, f32[256]{0:T(256)S(1)}, u32[]{:S(2)}) copy-start(f32[256]{0:T(256)S(1)} %fusion.549) | copy-start | bytes 3076
  1444.0 144.5 %reduce-scatter.49.cloned.1.call-start = ((), (), s32[]{:S(2)}) async-start(), calls=%async_computation.47 | async-start | bytes 1474560 | tf_op jit(solution)/shard_map/reduce_scatter | solution.py:98
  1477.3 120.0 %reduce-scatter.47.cloned.1.call-start = ((), (), s32[]{:S(2)}) async-start(), calls=%async_computation.46 | async-start | bytes 5242880 | tf_op jit(solution)/shard_map/reduce_scatter | solution.py:98
  1506.3 170.7 %reduce-scatter.35.cloned.1.call-start = ((), (), s32[]{:S(2)}) async-start(), calls=%async_computation.36 | async-start | bytes 5242880 | tf_op jit(solution)/shard_map/reduce_scatter | solution.py:98
  1583.2 201.1 %all-gather.57.cloned.1.call-start = ((), (), s32[]{:S(2)}) async-start(), calls=%async_computation.48 | async-start | bytes 2621440 | tf_op jit(solution)/shard_map/all_gather | solution.py:94
  1683.7 106.5 %all-gather.49.cloned.1.call-start = ((), (), s32[]{:S(2)}) async-start(), calls=%async_computation.37 | async-start | bytes 2621440 | tf_op jit(solution)/shard_map/all_gather | solution.py:94
  1738.6 329.7 %reduce-scatter.39.cloned.1.call-start = ((), (), s32[]{:S(2)}) async-start(), calls=%async_computation.39 | async-start | bytes 1474560 | tf_op jit(solution)/shard_map/reduce_scatter | solution.py:98
  1948.7 119.6 %reduce-scatter.37.cloned.1.call-start = ((), (), s32[]{:S(2)}) async-start(), calls=%async_computation.38 | async-start | bytes 5242880 | tf_op jit(solution)/shard_map/reduce_scatter | solution.py:98
  1983.2 143.8 %all-gather.51.cloned.1.call-start = ((), (), s32[]{:S(2)}) async-start(), calls=%async_computation.40 | async-start | bytes 2621440 | tf_op jit(solution)/shard_map/all_gather | solution.py:94
  2074.0 249.8 %reduce-scatter.43.cloned.1.call-start = ((), (), s32[]{:S(2)}) async-start(), calls=%async_computation.42 | async-start | bytes 1474560 | tf_op jit(solution)/shard_map/reduce_scatter | solution.py:98
  2259.5 67.0 %reduce-scatter.53.cloned.1.call-start = ((), (), s32[]{:S(2)}) async-start(), calls=%async_computation.50 | async-start | bytes 1474560 | tf_op jit(solution)/shard_map/reduce_scatter | solution.py:98
  2285.1 112.1 %reduce-scatter.41.cloned.1.call-start = ((), (), s32[]{:S(2)}) async-start(), calls=%async_computation.41 | async-start | bytes 5242880 | tf_op jit(solution)/shard_map/reduce_scatter | solution.py:98
  2312.6 164.7 %reduce-scatter.51.cloned.1.call-start = ((), (), s32[]{:S(2)}) async-start(), calls=%async_computation.49 | async-start | bytes 5242880 | tf_op jit(solution)/shard_map/reduce_scatter | solution.py:98
  2322.3 196.2 %reduce-scatter.61.cloned.1.call-start = ((), (), s32[]{:S(2)}) async-start(), calls=%async_computation.56 | async-start | bytes 1474560
  2332.8 266.9 %all-gather.53.cloned.1.call-start = ((), (), s32[]{:S(2)}) async-start(), calls=%async_computation.43 | async-start | bytes 2621440 | tf_op jit(solution)/shard_map/all_gather | solution.py:94
  2483.4 164.2 %all-gather.59.cloned.1.call-start = ((), (), s32[]{:S(2)}) async-start(), calls=%async_computation.51 | async-start | bytes 2621440 | tf_op jit(solution)/shard_map/all_gather | solution.py:94
  2483.9 296.1 %reduce-scatter.59.cloned.1.call-start = ((), (), s32[]{:S(2)}) async-start(), calls=%async_computation.54 | async-start | bytes 2359296 | tf_op jit(solution)/shard_map/reduce_scatter | solution.py:134
  2496.4 284.9 %all-reduce.125.cloned.1.call-start = ((), (), s32[]{:S(2)}) async-start(), calls=%async_computation.55 | async-start | bytes 294912 | tf_op jit(solution)/shard_map/psum | solution.py:119
  2520.4 262.6 %reduce-scatter.57.cloned.1.call-start = ((), (), s32[]{:S(2)}) async-start(), calls=%async_computation.53 | async-start | bytes 4718592 | tf_op jit(solution)/shard_map/reduce_scatter | solution.py:128
  2534.0 391.2 %reduce-scatter.55.cloned.1.call-start = ((), (), s32[]{:S(2)}) async-start(), calls=%async_computation.52 | async-start | bytes 28975104 | tf_op jit(solution)/shard_map/reduce_scatter | solution.py:125
  2781.2 193.6 %copy-start.163 = (f32[2,128,288]{1,2,0:T(8,128)S(1)}, f32[2,128,288]{1,2,0:T(8,128)}, u32[]{:S(2)}) copy-start(f32[2,128,288]{1,2,0:T(8,128)} %param.139) | copy-start | bytes 884740
  2781.3 193.5 %copy-start.223 = (bf16[2,128,288]{1,2,0:T(8,128)(2,1)S(1)}, bf16[2,128,288]{1,2,0:T(8,128)(2,1)}, u32[]{:S(2)}) copy-start(bf16[2,128,288]{1,2,0:T(8,128)(2,1)} %all-reduce.125.cloned.1.call-done) | copy-start | bytes 442372
  (402 other events, 9207.6 us)
Sparse Core Ops, SparseCore 0:
  12.3 135.5 all-gather.28
  208.0 76.7 reduce-scatter.28
  287.8 77.2 reduce-scatter.22
  367.4 24.6 all-gather.32
  394.0 45.9 all-gather.30
  442.0 44.6 all-gather.42
  489.2 35.4 all-gather.34
  527.1 27.8 all-gather.36
  693.1 73.9 reduce-scatter.30
  770.7 46.4 all-gather.44
  912.1 75.1 reduce-scatter.32
  989.5 77.2 reduce-scatter.24
  1068.5 46.4 all-gather.46
  1116.4 44.7 all-gather.38
  1189.2 75.2 reduce-scatter.44
  1268.6 46.4 all-gather.54
  1335.5 75.2 reduce-scatter.26
  1444.1 44.3 all-gather.40
  1490.9 27.8 reduce-scatter.48
  1521.6 75.6 reduce-scatter.46
  1599.6 77.2 reduce-scatter.34
  1683.8 46.6 all-gather.56
  1738.7 46.4 all-gather.48
  1948.8 27.5 reduce-scatter.38
  1983.3 75.1 reduce-scatter.36
  2074.1 44.3 all-gather.50
  2259.7 28.9 reduce-scatter.42
  2290.9 27.8 reduce-scatter.52
  2321.7 75.4 reduce-scatter.40
  2400.0 77.2 reduce-scatter.50
  2480.6 37.8 reduce-scatter.60
  2520.6 45.8 all-gather.52
  2568.5 44.6 all-gather.58
  2617.1 39.9 reduce-scatter.58
  2660.1 34.3 all-reduce.124
  2698.2 51.3 reduce-scatter.56
  2763.2 161.9 reduce-scatter.54
where the time goes:
time: 3110 us; the launch traced here: 3090 us
  waiting for transfers between devices  1070 us (34%)
  matrix products  639 us (21%)
  other arithmetic  569 us (18%)
  local copies, waits for them, and re-layouts  534 us (17%)
  blocking collectives  229 us (7%)
    reduce_scatter x16, waiting for transfers between devices, rows_sum(): return lax.psum_scatter(values, 'tensor', scatter_dimension=0, tiled=True)  595 us
    all_gather x12, waiting for transfers between devices, rows_gather(): return lax.all_gather(values, 'tensor', axis=0, tiled=True)  192 us
    dot_general x16, matrix products, ssd_scan(): jnp.einsum('bts,btsh,bshp->bthp', scores, fading, scaled, precision=precise)  189 us
    dot_general x24, matrix products, contract(): lax.dot_general(left, right, (((left_dim,), (right_dim,)), ((), ())), pre...  163 us
    all_gather x1, waiting for transfers between devices, shard_gather(): lax.all_gather(embed.astype(jnp.bfloat16), 'dp', axis=1, tiled=True)  134 us
    reduce_scatter x1, waiting for transfers between devices, reduce_end(): lax.psum_scatter(grad_lines.astype(jnp.bfloat16), 'dp', scatter_dimension...  95.5 us
    scatter-add x2, other arithmetic, body(): grad_table.at[safe_ids]  87 us
    dot_general x16, matrix products, ssd_scan(): jnp.einsum('bsn,bsh,bshp->bhnp', keys_q, to_end, scaled, precision=precise)  83.8 us
  transfers between devices with their start and end apart: 37, of which 20 were waited for; matrix products, arithmetic and copies ran while one was open for 38% of the time, Pallas kernels for 0%

commit v1 on v0

v1 whole, which is shorter than its diff:
```python
import functools

import jax
import jax.numpy as jnp
from jax import lax
from jax.experimental import pallas as pl
from jax.experimental.pallas import tpu as pltpu
from jax.sharding import Mesh
from jax.sharding import PartitionSpec as P

D = 1024
INNER = 2048
HEADS = 32
HDIM = 64
STATE = 128
CONV = 4
LAYERS = 2
MICRO = 2
STEP = 5

BLOCK = 128
HALO = 16
WIDTH = 512
GROUPS = INNER // WIDTH
LANES = 128
TILE = 640
CLASSES = 4
PAST = 1 << 11

norm_eps = 1e-05
adam_eps = 1e-06
clip_limit = 1.0
first_decay = 0.5
second_decay = 0.5
learn_rate = 0.3
weight_decay = 0.01

f32 = jnp.float32
bf16 = jnp.bfloat16
full = lax.Precision.HIGHEST
DP = ("chip", "core")
VMEM_BYTES = 58 * 1024 * 1024


def dot(left, right, left_dim, right_dim, precision=None):
    return lax.dot_general(
        left,
        right,
        (((left_dim,), (right_dim,)), ((), ())),
        precision=precision,
        preferred_element_type=f32,
    )


def nn(left, right, precision=None):
    return dot(left, right, 1, 0, precision)


def nt(left, right, precision=None):
    return dot(left, right, 1, 1, precision)


def tn(left, right, precision=None):
    return dot(left, right, 0, 0, precision)


def sigmoid(v):
    return 1.0 / (1.0 + jnp.exp(-v))


def softplus(v):
    return jnp.maximum(v, 0.0) + jnp.log1p(jnp.exp(-jnp.abs(v)))


def iota(shape, axis):
    return lax.broadcasted_iota(jnp.int32, shape, axis)


def call(kernel, grid, in_specs, out_specs, out_shape, scratch, prefetch=0, flops=0, bytes_moved=0):
    return pl.pallas_call(
        kernel,
        grid_spec=pltpu.PrefetchScalarGridSpec(
            num_scalar_prefetch=prefetch,
            grid=grid,
            in_specs=in_specs,
            out_specs=out_specs,
            scratch_shapes=scratch,
        ),
        out_shape=out_shape,
        compiler_params=pltpu.CompilerParams(
            vmem_limit_bytes=VMEM_BYTES, dimension_semantics=("arbitrary",) * len(grid)
        ),
        cost_estimate=pl.CostEstimate(
            flops=flops, bytes_accessed=bytes_moved, transcendentals=0
        ),
    )


def whole(shape):
    return pl.BlockSpec(shape, lambda *_: (0,) * len(shape))


def packed_zx(packed):
    rows = D // packed.shape[0]
    return pl.BlockSpec((packed.shape[0], rows, D), lambda g: (0, g, 0))


def unpacked_out(ref, low, rows):
    lines = ref[:, low : low + rows // 2, :]
    both = jnp.concatenate([lines[:, :, :WIDTH], lines[:, :, WIDTH:]], axis=1)
    return both.reshape(D, WIDTH)


def columns(rows, width=WIDTH, at=0):
    return pl.BlockSpec((rows, width), lambda g: (0, g + at))


def struct(shape, dtype=f32):
    return jax.ShapeDtypeStruct(shape, dtype)


def conv_rows(ref, taps, rows, low, width):
    result = taps[CONV : CONV + 1, :]
    for j in range(CONV):
        start = HALO - CONV + 1 + j
        result = result + ref[start : start + rows, low : low + width] * taps[j : j + 1, :]
    return result


def triangle():
    return iota((BLOCK, BLOCK), 0) >= iota((BLOCK, BLOCK), 1)


def spread(group):
    head = iota((LANES, WIDTH), 0)
    lane = iota((LANES, WIDTH), 1)
    return (head == group * (WIDTH // HDIM) + lane // HDIM).astype(f32)


def small_parts(rows, bcdt, headp, bcv, s_b, s_c, s_dt, s_cum, s_cumt, s_g):
    pre = conv_rows(bcdt, bcv, rows, 0, 2 * STATE)
    bc = (pre * sigmoid(pre)).astype(bf16)
    s_b[...] = bc[:, :STATE]
    s_c[...] = bc[:, STATE:]
    dt = softplus(bcdt[HALO:, 2 * STATE :] + headp[0:1, :])
    s_dt[...] = dt
    decay = headp[1:2, :] * dt
    keep = triangle()
    lower = keep.astype(f32)
    for b in range(rows // BLOCK):
        r = slice(b * BLOCK, (b + 1) * BLOCK)
        cum = nn(lower, decay[r], full)
        s_cum[r, :] = cum
        s_cumt[:, r] = cum.T
        s_g[b] = jnp.where(keep, nt(bc[r, STATE:], bc[r, :STATE]), 0.0)


def head_rows(s_cumt, group, r):
    heads = WIDTH // HDIM
    return s_cumt[pl.ds(pl.multiple_of(group * heads, heads), heads), r]


def fading(cum_e, cum_rows, head):
    column = cum_e[:, head * HDIM : head * HDIM + 1]
    return jnp.exp(jnp.minimum(column - cum_rows[head : head + 1, :], 0.0))


def one_head(values, j):
    first = iota(values.shape, 1) < HDIM
    return jnp.where(first if j == 0 else jnp.logical_not(first), values, 0.0).astype(bf16)


def small_scratch(rows):
    return [
        pltpu.VMEM((rows, STATE), bf16),
        pltpu.VMEM((rows, STATE), bf16),
        pltpu.VMEM((rows, LANES), f32),
        pltpu.VMEM((rows, LANES), f32),
        pltpu.VMEM((LANES, rows), f32),
        pltpu.VMEM((rows // BLOCK, BLOCK, BLOCK), f32),
    ]


def scan_kernel(
    nx, w_zx, wb, chan, headp, bcv,
    y_o, gate_o, xraw_o, st_o, bcdt_o, c_o, ecf_o,
    s_b, s_c, s_dt, s_cum, s_cumt, s_g,
):
    rows = y_o.shape[0]
    group = pl.program_id(0)

    @pl.when(group == 0)
    def _():
        bcdt_o[...] = nn(nx[...], wb[...])
        small_parts(rows, bcdt_o, headp, bcv, s_b, s_c, s_dt, s_cum, s_cumt, s_g)
        c_o[...] = s_c[...]
        run = jnp.zeros((1, LANES), f32)
        for b in range(rows // BLOCK):
            r = slice(b * BLOCK, (b + 1) * BLOCK)
            ecf_o[r, :] = jnp.exp(s_cum[r, :] + run)
            run = run + s_cum[(b + 1) * BLOCK - 1 : (b + 1) * BLOCK, :]

    both = w_zx[...].reshape(D, 2 * WIDTH)
    gate_o[...] = nn(nx[HALO:, :], both[:, :WIDTH])
    xraw_o[...] = nn(nx[...], both[:, WIDTH:])
    pre = conv_rows(xraw_o, chan, rows, 0, WIDTH)
    xc = pre * sigmoid(pre)
    expand = spread(group)
    u = xc * nn(s_dt[...], expand, full)
    skip = nn(headp[...], expand, full)[2:3, :]
    state = jnp.zeros((STATE, WIDTH), f32)
    for b in range(rows // BLOCK):
        r = slice(b * BLOCK, (b + 1) * BLOCK)
        cum_e = nn(s_cum[r, :], expand, full)
        total = cum_e[BLOCK - 1 : BLOCK, :]
        keys, reads = s_b[r, :], s_c[r, :]
        y = jnp.exp(cum_e) * nn(reads, state.astype(bf16)) + skip * xc[r]
        cum_rows = head_rows(s_cumt, group, r)
        pieces = []
        for pair in range(WIDTH // LANES):
            both = u[r, pair * LANES : (pair + 1) * LANES]
            piece = jnp.zeros((BLOCK, LANES), f32)
            for j in range(2):
                weights = (fading(cum_e, cum_rows, 2 * pair + j) * s_g[b]).astype(bf16)
                piece = piece + nn(weights, one_head(both, j))
            pieces.append(piece)
        y_o[r, :] = y + jnp.concatenate(pieces, axis=1)
        fresh = tn(keys, (u[r] * jnp.exp(total - cum_e)).astype(bf16))
        state = state * jnp.exp(total) + fresh
    st_o[...] = state


def scan_front(nx, packed, wb, chan, headp, bcv):
    ext = nx.shape[0]
    rows = ext - HALO
    return call(
        scan_kernel,
        (GROUPS,),
        [
            whole((ext, D)),
            packed_zx(packed),
            whole(wb.shape),
            columns(8),
            whole((8, LANES)),
            whole((8, 2 * STATE)),
        ],
        [
            columns(rows),
            columns(rows),
            columns(ext),
            columns(STATE),
            whole((ext, 384)),
            whole((rows, STATE)),
            whole((rows, LANES)),
        ],
        [
            struct((rows, INNER)),
            struct((rows, INNER)),
            struct((ext, INNER)),
            struct((STATE, INNER)),
            struct((ext, 384)),
            struct((rows, STATE), bf16),
            struct((rows, LANES)),
        ],
        small_scratch(rows),
        flops=2 * ext * D * 2 * INNER,
        bytes_moved=2 * D * 2 * INNER + 12 * rows * INNER,
    )(nx, packed, wb, chan, headp, bcv)


def join_kernel(
    y, gate, c, ecf, st, chan, wout, resid, yf_o, scaled_o, inv_o, res_o, s_gated, s_square
):
    group = pl.program_id(0)
    ecf_e = nn(ecf[...], spread(group), full)
    yf = y[...] + ecf_e * nn(c[...], st[...].astype(bf16))
    yf_o[...] = yf
    gated = yf * (gate[...] * sigmoid(gate[...]))
    s_gated[group] = gated
    part = jnp.broadcast_to(jnp.sum(gated * gated, axis=1, keepdims=True), s_square.shape)

    @pl.when(group == 0)
    def _():
        s_square[...] = part

    @pl.when(group > 0)
    def _():
        s_square[...] += part

    @pl.when(group == GROUPS - 1)
    def _():
        inverse = lax.rsqrt(s_square[...] / INNER + norm_eps)
        inv_o[...] = inverse
        res = resid[...]
        for q in range(GROUPS):
            at = slice(q * WIDTH, (q + 1) * WIDTH)
            scaled = (s_gated[q] * inverse[:, :1] * chan[CONV + 1 : CONV + 2, at]).astype(bf16)
            scaled_o[:, at] = scaled
            height = D // wout.shape[0]
            res = res + nt(scaled, unpacked_out(wout, q * height // 2, height))
        res_o[...] = res


def scan_join(y, gate, c, ecf, st, chan, packed, resid):
    rows = y.shape[0]
    height = D // packed.shape[0]
    return call(
        join_kernel,
        (GROUPS,),
        [
            columns(rows),
            columns(rows),
            whole((rows, STATE)),
            whole((rows, LANES)),
            columns(STATE),
            whole((8, INNER)),
            pl.BlockSpec((packed.shape[0], 2 * height, D), lambda g: (0, 2, 0)),
            whole((rows, D)),
        ],
        [columns(rows), whole((rows, INNER)), whole((rows, LANES)), whole((rows, D))],
        [
            struct((rows, INNER)),
            struct((rows, INNER), bf16),
            struct((rows, LANES)),
            struct((rows, D)),
        ],
        [pltpu.VMEM((GROUPS, rows, WIDTH), f32), pltpu.VMEM((rows, LANES), f32)],
        flops=2 * rows * D * INNER,
        bytes_moved=2 * D * INNER + 14 * rows * INNER,
    )(y, gate, c, ecf, st, chan, packed, resid)


def unjoin_kernel(
    dout, wout, y, gate, inv, c, ecf, chan, dy_o, dgate_o, dgain_o, ds_o, s_scaled, s_along
):
    phase = pl.program_id(0)
    group = pl.program_id(1)
    gain = chan[CONV + 1 : CONV + 2, :]
    raw = gate[...]
    sig = sigmoid(raw)
    opened = raw * sig
    gated = y[...] * opened
    inverse = inv[:, :1]

    @pl.when(phase == 0)
    def _():
        dscaled = nn(dout[...], unpacked_out(wout, 0, D // wout.shape[0]))
        s_scaled[group] = dscaled
        part = jnp.sum(dscaled * gain * gated, axis=1, keepdims=True)
        part = jnp.broadcast_to(part, s_along.shape)

        @pl.when(group == 0)
        def _():
            s_along[...] = part

        @pl.when(group > 0)
        def _():
            s_along[...] += part

    @pl.when(phase == 1)
    def _():
        dscaled = s_scaled[group]
        pulled = inverse * inverse * inverse * s_along[:, :1] / INNER
        dgated = inverse * gain * dscaled - gated * pulled
        dgain = jnp.sum(dscaled * gated * inverse, axis=0, keepdims=True)
        dgain_o[...] = jnp.broadcast_to(dgain, dgain_o.shape)
        dy = dgated * opened
        dy_o[...] = dy
        dgate_o[...] = (dgated * y[...] * (sig * (1.0 + raw * (1.0 - sig)))).astype(bf16)
        ecf_e = nn(ecf[...], spread(group), full)
        ds_o[...] = tn(c[...], (ecf_e * dy).astype(bf16))


def scan_unjoin(dout, packed, y, gate, inv, c, ecf, chan):
    rows = y.shape[0]
    shares = packed.shape[0]

    def both(height):
        return pl.BlockSpec((height, WIDTH), lambda p, g: (0, g))

    def second(height):
        return pl.BlockSpec((height, WIDTH), lambda p, g: (0, g * p))

    return call(
        unjoin_kernel,
        (2, GROUPS),
        [
            whole((rows, D)),
            pl.BlockSpec(
                (shares, D // shares // 2, D),
                lambda p, g: (0, 2 * GROUPS + jnp.where(p == 0, g, GROUPS - 1), 0),
            ),
            both(rows),
            both(rows),
            whole((rows, LANES)),
            whole((rows, STATE)),
            whole((rows, LANES)),
            both(8),
        ],
        [second(rows), second(rows), second(8), second(STATE)],
        [
            struct((rows, INNER)),
            struct((rows, INNER), bf16),
            struct((8, INNER)),
            struct((STATE, INNER)),
        ],
        [pltpu.VMEM((GROUPS, rows, WIDTH), f32), pltpu.VMEM((rows, LANES), f32)],
        flops=2 * rows * D * INNER,
        bytes_moved=2 * D * INNER + 22 * rows * INNER,
    )(dout, packed, y, gate, inv, c, ecf, chan)


def head_sums(values, expand):
    if values.shape[0] == 1:
        return nt(jnp.broadcast_to(values, (8, values.shape[1])), expand, full)[0:1, :]
    return nt(values, expand, full)


def conv_back(ref, taps, pad, rows, low, width, taps_o, main, halo):
    grads = [jnp.sum(pad[HALO : HALO + rows, :] * ref[HALO - 3 + j : HALO - 3 + j + rows,
             low : low + width], axis=0, keepdims=True) for j in range(CONV)]
    grads.append(jnp.sum(pad[HALO : HALO + rows, :], axis=0, keepdims=True))
    taps_o[...] = jnp.concatenate(grads + [jnp.zeros((3, width), f32)], axis=0)
    total = jnp.zeros((HALO + rows, width), f32)
    for j in range(CONV):
        shift = CONV - 1 - j
        total = total + pad[shift : shift + HALO + rows, :] * taps[j : j + 1, :]
    halo(total[:HALO])
    main(total[HALO:])


def back_kernel(
    xraw, dy, bcdt, st, dst, chan, headp, bcv,
    dx_o, tail_o, halo_o, dchan_o, dbc_o, dbch_o, dheadp_o, dbcv_o,
    s_b, s_c, s_dt, s_cum, s_cumt, s_g,
    s_db, s_dc, s_dcum, s_ddt, s_dtot, s_dg, s_skip, s_pad, s_state, s_bcpad,
):
    rows = dy.shape[0]
    blocks = rows // BLOCK
    group = pl.program_id(0)

    @pl.when(group == 0)
    def _():
        small_parts(rows, bcdt, headp, bcv, s_b, s_c, s_dt, s_cum, s_cumt, s_g)
        for ref in (s_db, s_dc, s_dcum, s_ddt, s_dtot, s_dg, s_skip, s_pad, s_bcpad):
            ref[...] = jnp.zeros(ref.shape, f32)

    pre = conv_rows(xraw, chan, rows, 0, WIDTH)
    sig = sigmoid(pre)
    xc = pre * sig
    expand = spread(group)
    dt_e = nn(s_dt[...], expand, full)
    u = xc * dt_e
    skip = nn(headp[...], expand, full)[2:3, :]
    state = st[...]
    for b in range(blocks):
        r = slice(b * BLOCK, (b + 1) * BLOCK)
        s_state[b] = state
        if b < blocks - 1:
            cum_e = nn(s_cum[r, :], expand, full)
            total = cum_e[BLOCK - 1 : BLOCK, :]
            fresh = tn(s_b[r, :], (u[r] * jnp.exp(total - cum_e)).astype(bf16))
            state = state * jnp.exp(total) + fresh
    dstate = dst[...]
    dskip = jnp.zeros((1, WIDTH), f32)
    for b in reversed(range(blocks)):
        r = slice(b * BLOCK, (b + 1) * BLOCK)
        cum_e = nn(s_cum[r, :], expand, full)
        total = cum_e[BLOCK - 1 : BLOCK, :]
        keys, reads = s_b[r, :], s_c[r, :]
        to_here, to_end, passed = jnp.exp(cum_e), jnp.exp(total - cum_e), jnp.exp(total)
        u_b, dy_b = u[r], dy[r, :]
        u_low, dy_low = u_b.astype(bf16), dy_b.astype(bf16)
        state_low, dstate_low = s_state[b].astype(bf16), dstate.astype(bf16)
        faded = (dy_b * to_here).astype(bf16)
        y_across = to_here * nn(reads, state_low)
        s_dc[r, :] += nt(faded, state_low)
        du_across = to_end * nn(keys, dstate_low)
        s_db[r, :] += nt((u_b * to_end).astype(bf16), dstate_low)
        cum_rows = head_rows(s_cumt, group, r)
        y_pieces, du_pieces = [], []
        dscores = jnp.zeros((BLOCK, BLOCK), f32)
        for pair in range(WIDTH // LANES):
            at = slice(pair * LANES, (pair + 1) * LANES)
            y_piece = jnp.zeros((BLOCK, LANES), f32)
            du_piece = jnp.zeros((BLOCK, LANES), f32)
            for j in range(2):
                fade = fading(cum_e, cum_rows, 2 * pair + j)
                weights = (fade * s_g[b]).astype(bf16)
                dy_head = one_head(dy_b[:, at], j)
                y_piece = y_piece + nn(weights, one_head(u_b[:, at], j))
                du_piece = du_piece + tn(weights, dy_head)
                dscores = dscores + nt(dy_head, u_low[:, at]) * fade
            y_pieces.append(y_piece)
            du_pieces.append(du_piece)
        y_within = jnp.concatenate(y_pieces, axis=1)
        du_within = jnp.concatenate(du_pieces, axis=1)
        s_dg[b] += dscores
        du = du_within + du_across
        moved = u_b * du_across
        dcum = dy_low.astype(f32) * y_within + dy_b * y_across
        dcum = dcum - u_low.astype(f32) * du_within - moved
        s_dcum[r, :] += head_sums(dcum, expand)
        dtotal = jnp.sum(moved, axis=0, keepdims=True)
        dtotal = dtotal + passed * jnp.sum(s_state[b] * dstate, axis=0, keepdims=True)
        s_dtot[b : b + 1, :] += head_sums(dtotal, expand)
        s_ddt[r, :] += head_sums(du * xc[r], expand)
        dskip = dskip + jnp.sum(dy_b * xc[r], axis=0, keepdims=True)
        dxc = du * dt_e[r] + skip * dy_b
        s_pad[HALO + b * BLOCK : HALO + (b + 1) * BLOCK, :] = dxc * (
            sig[r] * (1.0 + pre[r] * (1.0 - sig[r]))
        )
        dstate = passed * dstate + tn(reads, faded)
    s_skip[0:1, :] += head_sums(dskip, expand)

    def put_main(values):
        dx_o[...] = values.astype(bf16)
        tail_o[...] = values[rows - HALO :]

    def put_halo(values):
        halo_o[...] = values

    conv_back(xraw, chan, s_pad, rows, 0, WIDTH, dchan_o, put_main, put_halo)

    @pl.when(group == GROUPS - 1)
    def _():
        keep = triangle()
        upper = (iota((BLOCK, BLOCK), 0) <= iota((BLOCK, BLOCK), 1)).astype(f32)
        rate = headp[1:2, :]
        bias_sum = jnp.zeros((1, LANES), f32)
        rate_sum = jnp.zeros((1, LANES), f32)
        for b in range(blocks):
            r = slice(b * BLOCK, (b + 1) * BLOCK)
            dscores = jnp.where(keep, s_dg[b], 0.0).astype(bf16)
            s_dc[r, :] += nn(dscores, s_b[r, :])
            s_db[r, :] += tn(dscores, s_c[r, :])
            da = nn(upper, s_dcum[r, :], full) + s_dtot[b : b + 1, :]
            ddt = s_ddt[r, :] + da * rate
            rate_sum = rate_sum + jnp.sum(da * (rate * s_dt[r, :]), axis=0, keepdims=True)
            raw = bcdt[HALO + b * BLOCK : HALO + (b + 1) * BLOCK, 2 * STATE :] + headp[0:1, :]
            ddt = ddt * sigmoid(raw)
            bias_sum = bias_sum + jnp.sum(ddt, axis=0, keepdims=True)
            dbc_o[r, 2 * STATE :] = ddt
        dheadp_o[...] = jnp.concatenate(
            [bias_sum, rate_sum, s_skip[0:1, :], jnp.zeros((5, LANES), f32)], axis=0
        )
        bc_pre = conv_rows(bcdt, bcv, rows, 0, 2 * STATE)
        bc_sig = sigmoid(bc_pre)
        turn = bc_sig * (1.0 + bc_pre * (1.0 - bc_sig))
        s_bcpad[HALO : HALO + rows, :STATE] = s_db[...] * turn[:, :STATE]
        s_bcpad[HALO : HALO + rows, STATE:] = s_dc[...] * turn[:, STATE:]

        def put_bc(values):
            dbc_o[:, : 2 * STATE] = values

        def put_bc_halo(values):
            dbch_o[...] = values

        conv_back(bcdt, bcv, s_bcpad, rows, 0, 2 * STATE, dbcv_o, put_bc, put_bc_halo)


def scan_back(xraw, dy, bcdt, st, dst, chan, headp, bcv):
    rows = dy.shape[0]
    ext = rows + HALO
    blocks = rows // BLOCK
    return call(
        back_kernel,
        (GROUPS,),
        [
            columns(ext),
            columns(rows),
            whole((ext, 384)),
            columns(STATE),
            columns(STATE),
            columns(8),
            whole((8, LANES)),
            whole((8, 2 * STATE)),
        ],
        [
            columns(rows),
            columns(HALO),
            columns(HALO),
            columns(8),
            whole((rows, 384)),
            whole((HALO, 2 * STATE)),
            whole((8, LANES)),
            whole((8, 2 * STATE)),
        ],
        [
            struct((rows, INNER), bf16),
            struct((HALO, INNER)),
            struct((HALO, INNER)),
            struct((8, INNER)),
            struct((rows, 384)),
            struct((HALO, 2 * STATE)),
            struct((8, LANES)),
            struct((8, 2 * STATE)),
        ],
        small_scratch(rows)
        + [
            pltpu.VMEM((rows, STATE), f32),
            pltpu.VMEM((rows, STATE), f32),
            pltpu.VMEM((rows, LANES), f32),
            pltpu.VMEM((rows, LANES), f32),
            pltpu.VMEM((8, LANES), f32),
            pltpu.VMEM((blocks, BLOCK, BLOCK), f32),
            pltpu.VMEM((8, LANES), f32),
            pltpu.VMEM((rows + 2 * HALO, WIDTH), f32),
            pltpu.VMEM((blocks, STATE, WIDTH), f32),
            pltpu.VMEM((rows + 2 * HALO, 2 * STATE), f32),
        ],
        flops=20 * rows * INNER * STATE,
        bytes_moved=12 * rows * INNER,
    )(xraw, dy, bcdt, st, dst, chan, headp, bcv)


SHARE = 3 * WIDTH + LANES


def grads_kernel(
    normed, dout, dgate, dx, tail, back, dbcdt, bc_back, scaled, w_zx, wb, resid, dresid, gain,
    packed_o, dres_o, dgain_o, s_bc, s_sum,
):
    rows = normed.shape[0]
    group = pl.program_id(0)
    edge = slice(rows - HALO, rows)

    @pl.when(group == 0)
    def _():
        s_bc[GROUPS - 1] = jnp.zeros((rows, LANES), bf16)
        for q in range(3):
            at = slice(q * LANES, (q + 1) * LANES)
            s_bc[q] = dbcdt[:, at].astype(bf16)
            if q < 2:
                s_bc[q, edge, :] = (dbcdt[edge, at] + bc_back[:, at]).astype(bf16)
        total = nt(s_bc[0], wb[:, :LANES])
        total = total + nt(s_bc[1], wb[:, LANES : 2 * LANES])
        s_sum[...] = total + nt(s_bc[2], wb[:, 2 * LANES :])

    fixed = (tail[...] + back[...]).astype(bf16)
    dzx = jnp.concatenate(
        [dgate[...], jnp.concatenate([dx[: rows - HALO, :], fixed], axis=0)], axis=1
    )
    s_sum[...] += nt(dzx, w_zx[...].reshape(D, 2 * WIDTH))
    packed_o[:, : 2 * WIDTH] = tn(normed[...], dzx).astype(bf16)
    packed_o[:, 2 * WIDTH : 3 * WIDTH] = tn(dout[...], scaled[...]).astype(bf16)
    packed_o[:, 3 * WIDTH :] = tn(normed[...], s_bc[group]).astype(bf16)

    @pl.when(group == GROUPS - 1)
    def _():
        values, grad, weight = resid[...], s_sum[...], gain[0:1, :]
        inverse = lax.rsqrt(jnp.mean(values * values, axis=1, keepdims=True) + norm_eps)
        along = jnp.mean(grad * weight * values, axis=1, keepdims=True)
        pulled = inverse * inverse * inverse * along
        dres_o[...] = dresid[...] + inverse * weight * grad - values * pulled
        dgain = jnp.sum(grad * values * inverse, axis=0, keepdims=True)
        dgain_o[...] = jnp.broadcast_to(dgain, dgain_o.shape)


def layer_grads(
    normed, dout, dgate, dx, tail, back, dbcdt, bc_back, scaled, packed, wb, resid, dresid, gain
):
    rows = normed.shape[0]
    return call(
        grads_kernel,
        (GROUPS,),
        [
            whole((rows, D)),
            whole((rows, D)),
            columns(rows),
            columns(rows),
            columns(HALO),
            columns(HALO),
            whole((rows, 384)),
            whole((HALO, 2 * STATE)),
            columns(rows),
            packed_zx(packed),
            whole(wb.shape),
            whole((rows, D)),
            whole((rows, D)),
            whole((8, D)),
        ],
        [columns(D, SHARE), whole((rows, D)), whole((8, D))],
        [struct((D, GROUPS * SHARE), bf16), struct((rows, D)), struct((8, D))],
        [pltpu.VMEM((GROUPS, rows, LANES), bf16), pltpu.VMEM((rows, D), f32)],
        flops=10 * rows * D * INNER,
        bytes_moved=26 * D * INNER,
    )(normed, dout, dgate, dx, tail, back, dbcdt, bc_back, scaled, packed, wb, resid, dresid, gain)


def lookup_kernel(keys, starts, table, out, s_rows):
    cls = pl.program_id(0)
    parts, lines, width = table.shape[1:]

    @pl.when(cls == 0)
    def _():
        s_rows[...] = jnp.zeros(s_rows.shape, f32)

    place = iota((16, width), 0)

    def turn(i, carry):
        key = keys[i]
        at = key & (PAST - 1)
        line = (key >> 11) - cls * lines
        base = pl.multiple_of((line >> 4) << 4, 16)
        found = []
        for part in range(parts):
            tile = table[0, part, pl.ds(base, 16), :].astype(f32)
            found.append(
                jnp.sum(jnp.where(place == (line & 15), tile, 0.0), axis=0, keepdims=True)
            )
        s_rows[pl.ds(at, 1), :] = jnp.concatenate(found, axis=1)
        return carry

    lax.fori_loop(starts[cls], starts[cls + 1], turn, 0)

    @pl.when(cls == CLASSES - 1)
    def _():
        out[...] = s_rows[...].astype(bf16)


def lookup(keys, starts, table):
    count = keys.shape[0]
    return call(
        lookup_kernel,
        (CLASSES,),
        [pl.BlockSpec((1,) + table.shape[1:], lambda c, *_: (c, 0, 0, 0))],
        whole((count, D)),
        struct((count, D), bf16),
        [pltpu.VMEM((count, D), f32)],
        prefetch=2,
        bytes_moved=2 * table.size,
    )(keys, starts, table)


def scatter_kernel(keys, starts, table, rows, out, s_rows, s_sum):
    cls = pl.program_id(0)
    piece = pl.program_id(1)
    parts, lines, width = table.shape[1:]

    @pl.when((cls == 0) & (piece == 0))
    def _():
        wide = rows[...].astype(f32)
        for p in range(s_rows.shape[0]):
            s_rows[p] = wide[:, p * WIDTH : (p + 1) * WIDTH]

    for part in range(parts):
        s_sum[:, part * width : (part + 1) * width] = table[0, part].astype(f32)

    def turn(i, carry):
        key = keys[i]
        at = key & (PAST - 1)
        line = (key >> 11) - cls * lines
        s_sum[pl.ds(line, 1), :] += s_rows[piece, pl.ds(at, 1), :]
        return carry

    lax.fori_loop(starts[cls], starts[cls + 1], turn, 0)
    for part in range(parts):
        out[0, part] = s_sum[:, part * width : (part + 1) * width].astype(bf16)


def scatter(keys, starts, table, rows):
    count = keys.shape[0]
    lines, width = table.shape[2:]
    spec = pl.BlockSpec((1, WIDTH // width, lines, width), lambda c, p, *_: (c, p, 0, 0))
    return call(
        scatter_kernel,
        (CLASSES, D // WIDTH),
        [spec, whole((count, D))],
        spec,
        struct(table.shape, bf16),
        [pltpu.VMEM((D // WIDTH, count, WIDTH), f32), pltpu.VMEM((lines, WIDTH), f32)],
        prefetch=2,
        bytes_moved=4 * table.size,
    )(keys, starts, table, rows)


def tile_logits(table, chosen, real):
    parts, height, width = table.shape[1:]
    result = nt(table[0, 0], chosen[:, :width])
    for part in range(1, parts):
        result = result + nt(table[0, part], chosen[:, part * width : (part + 1) * width])
    line = pl.program_id(1) * height + iota(result.shape, 0)
    return jnp.where(line < real, result, -1e30)


def tile_hit(table, lines, wanted):
    height = table.shape[2]
    first = pl.program_id(0) * lines + pl.program_id(1) * height
    return first + iota((height, wanted.shape[1]), 0) == wanted[0:1, :]


def measure_kernel(real, lines, table, chosen, wanted, out, s_stats):
    logits = tile_logits(table, chosen, real)
    hit = tile_hit(table, lines, wanted)
    first = (pl.program_id(0) == 0) & (pl.program_id(1) == 0)

    @pl.when(first)
    def _():
        s_stats[0:1, :] = jnp.full((1, s_stats.shape[1]), -1e30, f32)
        s_stats[1:8, :] = jnp.zeros((7, s_stats.shape[1]), f32)

    old = s_stats[0:1, :]
    top = jnp.maximum(old, jnp.max(logits, axis=0, keepdims=True))
    total = s_stats[1:2, :] * jnp.exp(old - top)
    s_stats[1:2, :] = total + jnp.sum(jnp.exp(logits - top), axis=0, keepdims=True)
    s_stats[2:3, :] += jnp.sum(jnp.where(hit, logits, 0.0), axis=0, keepdims=True)
    s_stats[0:1, :] = top
    out[...] = s_stats[...]


def table_spec(table):
    parts, width = table.shape[1], table.shape[3]
    return pl.BlockSpec((1, parts, TILE, width), lambda c, i: (c, 0, i, 0))


def vocab_measure(table, chosen, wanted, real):
    count = chosen.shape[0]
    lines = table.shape[2]
    return call(
        functools.partial(measure_kernel, real, lines),
        (CLASSES, lines // TILE),
        [table_spec(table), whole((count, D)), whole((8, count))],
        whole((8, count)),
        struct((8, count)),
        [pltpu.VMEM((8, count), f32)],
        flops=2 * count * table.size,
        bytes_moved=2 * table.size,
    )(table, chosen, wanted)


def vocab_kernel(real, lines, table, chosen, wanted, stats, dtable, dchosen, s_sum):
    logits = tile_logits(table, chosen, real)
    hit = tile_hit(table, lines, wanted)
    soft = jnp.exp(logits - stats[0:1, :])
    dlogits = (stats[1:2, :] * (soft - jnp.where(hit, 1.0, 0.0))).astype(bf16)
    step = pl.program_id(0) * pl.num_programs(1) + pl.program_id(1)
    parts, width = table.shape[1], table.shape[3]

    @pl.when(step == 0)
    def _():
        s_sum[...] = jnp.zeros(s_sum.shape, f32)

    for part in range(parts):
        at = slice(part * width, (part + 1) * width)
        dtable[0, part] = nn(dlogits, chosen[:, at]).astype(bf16)
        s_sum[:, at] += tn(dlogits, table[0, part])

    @pl.when(step == CLASSES * pl.num_programs(1) - 1)
    def _():
        dchosen[...] = s_sum[...].astype(bf16)


def vocab_back(table, chosen, wanted, stats, real):
    count = chosen.shape[0]
    lines = table.shape[2]
    return call(
        functools.partial(vocab_kernel, real, lines),
        (CLASSES, lines // TILE),
        [table_spec(table), whole((count, D)), whole((8, count)), whole((8, count))],
        [table_spec(table), whole((count, D))],
        [struct(table.shape, bf16), struct((count, D), bf16)],
        [pltpu.VMEM((count, D), f32)],
        flops=6 * count * table.size,
        bytes_moved=4 * table.size,
    )(table, chosen, wanted, stats)


def shifted(values, axis, by):
    n = lax.axis_size(axis)
    return lax.ppermute(values, axis, [(i, (i + by) % n) for i in range(n)])


def swapped(values):
    return lax.ppermute(values, "core", [(0, 1), (1, 0)])


def to_later(values):
    return lax.ppermute(values, "core", [(0, 1)])


def to_earlier(values):
    return lax.ppermute(values, "core", [(1, 0)])


def everywhere(values, axes, combine=jnp.add):
    for axis in axes:
        reach = 1
        while reach < lax.axis_size(axis):
            n = lax.axis_size(axis)
            other = lax.ppermute(values, axis, [(i, i ^ reach) for i in range(n)])
            values = combine(values, other)
            reach *= 2
    return values


def around(values, axis):
    n = lax.axis_size(axis)
    return jnp.stack([values] + [shifted(values, axis, by) for by in range(1, n)])


def sum_back(blocks, axis):
    n = lax.axis_size(axis)
    result = blocks[0].astype(f32)
    for by in range(1, n):
        result = result + shifted(blocks[by], axis, -by).astype(f32)
    return result


def inverse_rms(values):
    return lax.rsqrt(jnp.mean(values * values, axis=-1, keepdims=True) + norm_eps)


def rms_back(grad, values, gain):
    inverse = inverse_rms(values)
    along = jnp.mean(grad * gain * values, axis=-1, keepdims=True)
    dvalues = inverse * gain * grad - values * (inverse * inverse * inverse * along)
    return (dvalues, jnp.sum(grad * values * inverse, axis=0))


def in_order(blocks, axis):
    n = blocks.shape[axis]
    z = lax.axis_index("tensor")
    taken = [lax.dynamic_index_in_dim(blocks, (z - q) % n, axis, False) for q in range(n)]
    return jnp.stack(taken, axis=axis)


def turn_heads(bcdt):
    rows = bcdt.shape[0]
    steps = bcdt[:, 2 * STATE : 2 * STATE + HEADS].reshape(rows, GROUPS, -1)
    steps = in_order(steps, 1).reshape(rows, HEADS)
    return jnp.concatenate([bcdt[:, : 2 * STATE], steps, bcdt[:, 2 * STATE + HEADS :]], axis=1)


def pack_layer(w_zx, w_bcdt, w_out):
    rows = w_zx.shape[0]
    zx = w_zx.reshape(rows, -1)
    out = jnp.concatenate([w_out[: rows // 2], w_out[rows // 2 :]], axis=1)
    own = jnp.concatenate([zx, out], axis=0).astype(bf16)
    blocks = around(own, "tensor")
    zx = blocks[:, :rows].reshape(-1, D)
    out = blocks[:, rows:].reshape(-1, D)
    lines = -(-rows // 48) * 16
    bcdt = jnp.pad(w_bcdt.astype(bf16), ((0, 3 * lines - rows), (0, LANES - HEADS)))
    bcdt = jnp.pad(bcdt[:, : 2 * STATE + HEADS].reshape(3, lines, -1), ((0, 0), (0, 0), (0, 32)))
    bcdt = jnp.concatenate([bcdt[0], bcdt[1], bcdt[2]], axis=1)
    bcdt = jnp.pad(bcdt, ((0, 0), (0, D - bcdt.shape[1])))
    return jnp.concatenate([zx, out, bcdt], axis=0)


def unpack_bcdt(packed):
    rows = D // packed.shape[0]
    lines = -(-rows // 48) * 16
    width = 2 * STATE + HEADS + 32
    part = packed[:, GROUPS * (rows + rows // 2) :]
    part = jnp.concatenate([part[:, :, i * width : (i + 1) * width] for i in range(3)], axis=1)
    part = part[:, :rows].reshape(D, width)
    return turn_heads(jnp.pad(part, ((0, 0), (0, 2 * STATE + LANES - width))))


def reduce_layer(packed):
    n_tensor = lax.axis_size("tensor")
    mine = lax.psum_scatter(packed, DP, scatter_dimension=0, tiled=True)
    shares = [mine[:, j * SHARE : (j + 1) * SHARE] for j in range(n_tensor)]
    bcdt = turn_heads(jnp.concatenate([share[:, 3 * WIDTH :] for share in shares[:3]], axis=1))
    blocks = []
    for by in range(n_tensor):
        block = jnp.concatenate([shares[-by][:, : 3 * WIDTH], bcdt], axis=1)
        blocks.append(block if by == 0 else shifted(block, "tensor", by))
    blocks = [block.astype(f32) for block in blocks]
    even = functools.reduce(jnp.add, blocks[0::2])
    odd = functools.reduce(jnp.add, blocks[1::2])
    total = even + odd
    return (
        total[:, : 2 * WIDTH].reshape(-1, 2, WIDTH),
        total[:, 2 * WIDTH : 3 * WIDTH],
        total[:, 3 * WIDTH : 3 * WIDTH + 2 * STATE + HEADS],
    )


def layer_forward(resid, gain, packed, wb, smalls):
    chan, headp, bcv = smalls
    normed = (resid * inverse_rms(resid) * gain).astype(bf16)
    nx = jnp.concatenate([to_later(normed[-HALO:]), normed], axis=0)
    y, gate, xraw, st, bcdt, c, ecf = scan_front(nx, packed, wb, chan, headp, bcv)
    before = to_later(st)
    y, scaled, inverse, out = scan_join(y, gate, c, ecf, before, chan, packed, resid)
    return out, (resid, normed, y, gate, xraw, before, bcdt, c, ecf, scaled, inverse)


def layer_backward(dresid, kept, gain, packed, wb, smalls):
    resid, normed, y, gate, xraw, before, bcdt, c, ecf, scaled, inverse = kept
    chan, headp, bcv = smalls
    dout = dresid.astype(bf16)
    dy, dgate, dgain, dstart = scan_unjoin(dout, packed, y, gate, inverse, c, ecf, chan)
    after = to_earlier(dstart)
    dx, tail, halo, dchan, dbcdt, bc_halo, dheadp, dbcv = scan_back(
        xraw, dy, bcdt, before, after, chan, headp, bcv
    )
    back, bc_back = to_earlier(halo), to_earlier(bc_halo)
    gain_rows = jnp.broadcast_to(gain[None, :], (8, D))
    grads, dresid, dnorm_gain = layer_grads(
        normed, dout, dgate, dx, tail, back, dbcdt, bc_back,
        scaled, packed, wb, resid, dresid, gain_rows,
    )
    dchan = jnp.concatenate([dchan[: CONV + 1], dgain[:1]], axis=0)
    smalls = (dnorm_gain[0], dchan, dheadp[:3, :HEADS], dbcv[: CONV + 1])
    return dresid, reduce_layer(grads), smalls


def lse_merge(first, second):
    top = jnp.maximum(first[0], second[0])
    total = first[1] * jnp.exp(first[0] - top) + second[1] * jnp.exp(second[0] - top)
    return jnp.stack([top, total, first[2] + second[2]])


def adapt(weight, first, second, grad):
    first_new = first_decay * first + (1.0 - first_decay) * grad
    second_new = second_decay * second + (1.0 - second_decay) * grad * grad
    update = (
        first_new
        / (1.0 - first_decay**STEP)
        / (jnp.sqrt(second_new / (1.0 - second_decay**STEP)) + adam_eps)
        + weight_decay * weight
    )
    return (first_new, second_new, update)


def group_squares(values, stacked):
    if stacked:
        return jnp.sum(values * values, axis=tuple(range(1, values.ndim)))
    return jnp.sum(values * values)[None]


def body(
    token_ids, lengths, loss_pos, targets,
    embed, embed_m, embed_v,
    w_zx, w_zx_m, w_zx_v,
    w_bcdt, w_bcdt_m, w_bcdt_v,
    w_out, w_out_m, w_out_v,
    channel, channel_m, channel_v,
    per_head, per_head_m, per_head_v,
    bc_conv, bc_conv_m, bc_conv_v,
    gains, gains_m, gains_v,
):
    n_tensor = lax.axis_size("tensor")
    n_data = lax.axis_size("chip") * lax.axis_size("core")
    core = lax.axis_index("core")
    z = lax.axis_index("tensor")
    seq = token_ids.shape[1]
    rows = seq // 2
    scored = loss_pos.shape[1]
    half = scored // 2
    lines = embed.shape[0]
    padded = -(-lines // TILE) * TILE
    vocab = lines * CLASSES

    own_meta = jnp.concatenate([token_ids, loss_pos, targets, lengths], axis=1)
    other_meta = swapped(own_meta)
    meta = jnp.where(
        core == 0,
        jnp.stack([own_meta, other_meta], axis=1),
        jnp.stack([other_meta, own_meta], axis=1),
    ).reshape(n_tensor, -1)
    meta = jnp.stack(
        [
            lax.dynamic_index_in_dim(meta, (z - j) % n_tensor, 0, keepdims=False)
            for j in range(n_tensor)
        ]
    )
    ids = lax.dynamic_slice_in_dim(meta, core * rows, rows, 1)
    length = meta[:, seq + 2 * scored :]
    live = core * rows + jnp.arange(rows)[None, :] < length
    positions = lax.dynamic_slice_in_dim(meta, seq + core * half, half, 1)
    wanted = lax.dynamic_slice_in_dim(meta, seq + scored + core * half, half, 1)
    own_positions = meta[0, seq : seq + scored]

    def place(indices):
        local = indices - z * vocab
        return (local & 3) * padded + (local >> 2), (local >= 0) & (local < vocab)

    key, inside = place(ids)
    count = n_tensor * rows
    key = jnp.where(inside & live, key, CLASSES * padded).reshape(count)
    key = key * PAST + jnp.arange(count)
    rank = jnp.sum((key[None, :] < key[:, None]).astype(jnp.int32), axis=1)
    keys = jnp.sum(jnp.where(rank[None, :] == jnp.arange(count)[:, None], key[None, :], 0), axis=1)
    edges = jnp.arange(8) * (padded * PAST)
    starts = jnp.sum((key[None, :] < edges[:, None]).astype(jnp.int32), axis=1)

    low = jnp.pad(embed.astype(bf16), ((0, padded - lines), (0, 0)))
    table = lax.all_gather(low, DP).reshape(CLASSES, n_data // CLASSES, padded, -1)
    shares = [pack_layer(w_zx[i], w_bcdt[i], w_out[i]) for i in range(LAYERS)]
    packed = [lax.all_gather(share, DP) for share in shares]
    inner = INNER // n_tensor
    heads = HEADS // n_tensor
    small = jnp.concatenate([channel, jnp.pad(per_head, ((0, 0), (0, 0), (0, inner - heads)))], 1)
    small = around(small, "tensor")
    channel_all = small[:, :, : CONV + 2].transpose(1, 2, 0, 3).reshape(LAYERS, CONV + 2, INNER)
    head_all = small[:, :, CONV + 2 :, :heads].transpose(1, 2, 0, 3).reshape(LAYERS, 3, HEADS)
    smalls = []
    for depth in range(LAYERS):
        headp = jnp.stack([head_all[depth, 0], -jnp.exp(head_all[depth, 1]), head_all[depth, 2]])
        smalls.append(
            (
                jnp.pad(channel_all[depth], ((0, 2), (0, 0))),
                jnp.pad(headp, ((0, 5), (0, LANES - HEADS))),
                jnp.pad(bc_conv[depth], ((0, 3), (0, 0))),
            )
        )

    found = lookup(keys, starts, table)
    resid = sum_back(found.reshape(n_tensor, rows, D), "tensor")
    w_small = [unpack_bcdt(packed[depth]) for depth in range(LAYERS)]
    kept = []
    for depth in range(LAYERS):
        resid, saved = layer_forward(
            resid, gains[depth], packed[depth], w_small[depth], smalls[depth]
        )
        kept.append(saved)

    final = (resid * inverse_rms(resid) * gains[LAYERS]).astype(bf16)
    other = swapped(final)
    both = jnp.concatenate(
        [jnp.where(core == 0, final, other), jnp.where(core == 0, other, final)], axis=0
    )
    pick = (positions[0][:, None] == jnp.arange(seq)[None, :]).astype(bf16)
    chosen = around(nn(pick, both).astype(bf16), "tensor").reshape(n_tensor * half, D)
    want, known = place(wanted)
    want = jnp.where(known, want, -1).reshape(1, -1)
    want = jnp.broadcast_to(want, (8, n_tensor * half))
    stats = vocab_measure(table, chosen, want, lines)[:3]
    stats = stats.reshape(3, n_tensor, half)

    ordered = everywhere(in_order(stats, 1), ("tensor",), lse_merge)
    stats = in_order(ordered, 1).reshape(3, -1)
    log_total = stats[0] + jnp.log(stats[1])
    counted = (positions < length).astype(f32).reshape(-1)
    losses = (counted * (log_total - stats[2])).reshape(n_tensor, half).sum(axis=1)
    loss_sum = jnp.sum(in_order(losses, 0))
    loss_count = jnp.sum(counted)
    info = jnp.pad(jnp.stack([log_total, counted]), ((0, 6), (0, 0)))
    dtable, dchosen = vocab_back(table, chosen, want, info, lines)
    dpicked = sum_back(dchosen.reshape(n_tensor, half, D), "tensor").astype(bf16)
    other = swapped(dpicked)
    dpicked = jnp.concatenate(
        [jnp.where(core == 0, dpicked, other), jnp.where(core == 0, other, dpicked)], axis=0
    )
    spots = (core * rows + jnp.arange(rows)[:, None] == own_positions[None, :]).astype(bf16)
    dresid, dfinal_gain = rms_back(nn(spots, dpicked), resid, gains[LAYERS])

    grads = [None] * LAYERS
    small_grads = [None] * LAYERS
    for depth in reversed(range(LAYERS)):
        dresid, grads[depth], small_grads[depth] = layer_backward(
            dresid, kept[depth], gains[depth], packed[depth], w_small[depth], smalls[depth]
        )

    arrived = around(dresid.astype(bf16), "tensor").reshape(count, D)
    dtable = scatter(keys, starts, dtable, arrived)
    dtable = dtable.reshape(n_data, padded, -1)
    grad_table = lax.psum_scatter(dtable, DP, scatter_dimension=0)[:lines].astype(f32)

    grad_zx, grad_out, grad_bcdt = (jnp.stack(parts) for parts in zip(*grads))
    grad_gains = jnp.stack([small_grads[depth][0] for depth in range(LAYERS)] + [dfinal_gain])
    grad_channel = jnp.stack([part[1] for part in small_grads])
    grad_channel = in_order(grad_channel.reshape(LAYERS, CONV + 2, n_tensor, inner), 2)
    grad_channel = grad_channel.reshape(LAYERS, CONV + 2, INNER)
    grad_head = jnp.stack([part[2] for part in small_grads])
    grad_head = in_order(grad_head.reshape(LAYERS, 3, n_tensor, heads), 2)
    grad_bc_conv = jnp.stack([part[3] for part in small_grads])
    flat = jnp.concatenate(
        [
            grad_gains.reshape(-1, LANES),
            grad_channel.reshape(-1, LANES),
            grad_bc_conv.reshape(-1, LANES),
            jnp.pad(grad_head.reshape(LAYERS * 3, HEADS), ((0, 0), (0, LANES - HEADS))),
        ]
    )
    flat = everywhere(flat, ("core", "tensor", "chip"))
    sizes = [grad.size // LANES for grad in (grad_gains, grad_channel, grad_bc_conv)]
    edges = [sizes[0], sizes[0] + sizes[1], sum(sizes)]
    grad_gains = flat[: edges[0]].reshape(grad_gains.shape)
    grad_channel = flat[edges[0] : edges[1]].reshape(grad_channel.shape)
    grad_bc_conv = flat[edges[1] : edges[2]].reshape(grad_bc_conv.shape)
    grad_head = flat[edges[2] :, :HEADS].reshape(LAYERS, 3, HEADS)
    grad_channel = lax.dynamic_slice_in_dim(grad_channel, z * inner, inner, 2)
    grad_head = lax.dynamic_slice_in_dim(grad_head, z * heads, heads, 2)

    everyone = n_tensor * n_data
    kinds = (
        (embed, embed_m, embed_v, grad_table, False, 1),
        (w_zx, w_zx_m, w_zx_v, grad_zx, True, 1),
        (w_bcdt, w_bcdt_m, w_bcdt_v, grad_bcdt, True, n_tensor),
        (w_out, w_out_m, w_out_v, grad_out, True, 1),
        (channel, channel_m, channel_v, grad_channel, True, n_data),
        (per_head, per_head_m, per_head_v, grad_head, True, n_data),
        (bc_conv, bc_conv_m, bc_conv_v, grad_bc_conv, True, everyone),
        (gains, gains_m, gains_v, grad_gains, False, everyone),
    )
    grad_sq = jnp.concatenate([group_squares(kind[3], kind[4]) / kind[5] for kind in kinds])
    weight_sq = jnp.concatenate([group_squares(kind[0], kind[4]) / kind[5] for kind in kinds])
    groups = grad_sq.shape[0]
    totals = jnp.concatenate(
        [grad_sq, weight_sq, jnp.stack([loss_sum, loss_count]) / n_tensor]
    )
    totals = everywhere(jnp.pad(totals, (0, LANES - totals.shape[0])), ("core", "tensor", "chip"))
    grad_sq, weight_sq = totals[:groups], totals[groups : 2 * groups]
    grad_norm = jnp.sqrt(jnp.sum(grad_sq))
    scale = jnp.minimum(1.0, clip_limit / grad_norm)
    moved = [adapt(kind[0], kind[1], kind[2], kind[3] * scale) for kind in kinds]
    step_sq = jnp.concatenate(
        [group_squares(change[2], kind[4]) / kind[5] for change, kind in zip(moved, kinds)]
    )
    step_sq = everywhere(jnp.pad(step_sq, (0, LANES - groups)), ("core", "tensor", "chip"))[:groups]
    weight_norm = jnp.sqrt(weight_sq)
    step_norm = jnp.sqrt(step_sq)
    trust_all = weight_norm / step_norm
    results = []
    offset = 0
    for kind, change in zip(kinds, moved):
        weight = kind[0]
        if kind[4]:
            factor = trust_all[offset : offset + weight.shape[0]].reshape(
                (weight.shape[0],) + (1,) * (weight.ndim - 1)
            )
            offset = offset + weight.shape[0]
        else:
            factor = trust_all[offset]
            offset = offset + 1
        results += [weight - learn_rate * factor * change[2], change[0], change[1]]
    group_norms = jnp.stack([weight_norm, step_norm])
    return (totals[2 * groups], totals[2 * groups + 1], grad_norm, group_norms, *results)


def solution(mesh):
    devices = mesh.devices.reshape(-1, 2, mesh.shape["tensor"])
    inside = Mesh(devices, ("chip", "core", "tensor"))
    by_data = P(None, DP)
    embed = (P("tensor", DP),) * 3
    w_zx = (P(None, DP, None, "tensor"),) * 3
    w_bcdt = (P(None, DP, None),) * 3
    w_out = (P(None, DP, "tensor"),) * 3
    by_tensor = (P(None, None, "tensor"),) * 6
    copied = (P(),) * 6
    states = embed + w_zx + w_bcdt + w_out + by_tensor + copied
    return jax.shard_map(
        body,
        mesh=inside,
        in_specs=(by_data,) * 4 + states,
        out_specs=(P(),) * 4 + states,
        check_vma=False,
    )
```

time: 3110 us -> 1160 us (0.37)
  waiting for transfers between devices: 1070 us -> 432 us
  matrix products: 639 us -> 1.29 us
  other arithmetic: 569 us -> 107 us
  local copies, waits for them, and re-layouts: 534 us -> 79.2 us
  Pallas kernels: 0 us -> 391 us
  blocking collectives: 229 us -> 0 us
  starting transfers between devices: 3.13 us -> 115 us
    reduce_scatter x19 -> x3, waiting for transfers between devices: 690 us -> 33.9 us  [the longest x1 33.9 us: body(): lax.psum_scatter(dtable, DP, scatter_dimension=0)[:lines].astype(f32)]
    dot_general x98 -> x2, matrix products: 631 us -> 1.29 us  [dot(): lax.dot_general(left, right, (((left_dim,), (right_dim,)), ((), ())), pre...]
    pallas_call x0 -> x14, Pallas kernels: none -> 391 us  [the longest x2 99.6 us: scan_back(): call(back_kernel, (GROUPS,), [columns(ext), columns(rows), whole((ext, 38...]
    ppermute x0 -> x57, waiting for transfers between devices: none -> 297 us  [the longest x27 250 us: shifted(): return lax.ppermute(values, axis, [(i, (i + by) % n) for i in range(n)])]
    all_gather x16 -> x3, waiting for transfers between devices: 374 us -> 101 us  [the longest x2 59.1 us: body(): packed = [lax.all_gather(share, DP) for share in shares]]
    reshape x73 -> x11, local copies, waits for them, and re-layouts: 198 us -> 0.8 us  [the longest x4 0.58 us: turn_heads(): steps = in_order(steps, 1).reshape(rows, HEADS)]
    psum x9 -> x0, blocking collectives: 175 us -> none  [the longest x2 81.2 us: body(): lax.psum((grad_sq, weight_sq, jnp.stack([loss_sum, loss_count]) / n_tenso...]
    reduce_sum x57 -> x7, other arithmetic: 147 us -> 12 us  [the longest x3 6.44 us: inverse_rms(): jnp.mean(values * values, axis=-1, keepdims=True) + norm_eps]
  transfers between devices with their start and end apart: 37 -> 63, of which waited for: 20 -> 40; matrix products, arithmetic and copies ran while one was open for 38% -> 7% of each run, Pallas kernels for 0% -> 14%
where the time goes in v1:
time: 1160 us; the launch traced here: 1150 us
  waiting for transfers between devices  432 us (37%)
  Pallas kernels  391 us (34%)
  starting transfers between devices  115 us (10%)
  other arithmetic  107 us (9%)
  local copies, waits for them, and re-layouts  79.2 us (7%)
  between operations  24.1 us (2%)
    ppermute x27, waiting for transfers between devices, shifted(): return lax.ppermute(values, axis, [(i, (i + by) % n) for i in range(n)])  250 us
    pallas_call x2, Pallas kernels, scan_back(): call(back_kernel, (GROUPS,), [columns(ext), columns(rows), whole((ext, 38...  99.6 us
    pallas_call x1, Pallas kernels, vocab_back(): call(functools.partial(vocab_kernel, real, lines), (CLASSES, lines // TIL...  59.2 us
    all_gather x2, waiting for transfers between devices, body(): packed = [lax.all_gather(share, DP) for share in shares]  59.1 us
    ppermute x17, starting transfers between devices, everywhere(): other = lax.ppermute(values, axis, [(i, i ^ reach) for i in range(n)])  50.6 us
    pallas_call x2, Pallas kernels, scan_front(): call(scan_kernel, (GROUPS,), [whole((ext, D)), packed_zx(packed), whole(w...  49.9 us
    ppermute x27, starting transfers between devices, shifted(): return lax.ppermute(values, axis, [(i, (i + by) % n) for i in range(n)])  47.3 us
    pallas_call x2, Pallas kernels, layer_grads(): call(grads_kernel, (GROUPS,), [whole((rows, D)), whole((rows, D)), column...  43.9 us
  transfers between devices with their start and end apart: 63, of which 40 were waited for; matrix products, arithmetic and copies ran while one was open for 7% of the time, Pallas kernels for 14%

profile of v1, /device:TPU:0, one launch (start us, length us, event | category | flops | bytes accessed | tf_op | source)
XLA Modules:
  0.0 1149.0 jit_solution(2486629627679988952)
XLA Ops:
  7.2 6.9 multiply_reduce_fusion.1
  17.8 5.1 collective-permute-start.7
  24.5 7.9 collective-permute-done.7
  32.5 9.4 collective-permute-done.5
  41.9 14.6 %collective-permute-done.6 = bf16[192,1024]{1,0:T(8,128)(2,1)S(1)} collective-permute-done((bf16[192,1024]{1,0:T(8,128)(2,1)S(1)}, bf16[192,1024]{1,0:T(8,128)(2,1)S(1)}, u32[]{:S(2)}, u32[]{:S(2)}) %collective-permute-start.6) | collective-permute-done | bytes 393248 | tf_op jit(solution)/shard_map/ppermute | solution.py:871
  62.4 9.8 collective-permute-done.13
  72.2 14.9 %collective-permute-done.14 = bf16[192,1024]{1,0:T(8,128)(2,1)S(1)} collective-permute-done((bf16[192,1024]{1,0:T(8,128)(2,1)S(1)}, bf16[192,1024]{1,0:T(8,128)(2,1)S(1)}, u32[]{:S(2)}, u32[]{:S(2)}) %collective-permute-start.14) | collective-permute-done | bytes 393248 | tf_op jit(solution)/shard_map/ppermute | solution.py:871
  88.9 8.1 collective-permute-start.8
  107.0 41.8 %all-gather.7.cloned.1.call-done = bf16[25600,512]{1,0:T(8,128)(2,1)} async-done(((bf16[3200,512]{1,0:T(8,128)(2,1)}), bf16[25600,512]{1,0:T(8,128)(2,1)}) %all-gather.7.cloned.1.call-update) | async-done | bytes 26214416 | tf_op jit(solution)/shard_map/all_gather | solution.py:1092
  148.8 15.9 %shard_map.483 = bf16[2048,1024]{1,0:T(8,128)(2,1)} custom-call(s32[2048]{0:T(1024)} %select_reduce_fusion.keys, s32[8]{0:T(128)} %convert_reduce_fusion.1.starts, bf16[4,2,3200,512]{3,2,1,0:T(8,128)(2,1)} %bitcast.187), custom_call_target="tpu_custom_call" | custom-call | bytes 26214400 | tf_op jit(solution)/shard_map/pallas_call | solution.py:724
  164.7 3.6 fusion.76
  168.3 6.7 collective-permute-start.1
  176.3 50.4 %all-gather.9.cloned.1.call-done = bf16[6528,1024]{1,0:T(8,128)(2,1)} async-done(((bf16[816,1024]{1,0:T(8,128)(2,1)}), bf16[6528,1024]{1,0:T(8,128)(2,1)}) %all-gather.9.cloned.1.call-update) | async-done | bytes 13369360 | tf_op jit(solution)/shard_map/all_gather | solution.py:1094
  229.5 29.2 %collective-permute-done.2 = bf16[512,1024]{1,0:T(8,128)(2,1)S(1)} collective-permute-done((bf16[512,1024]{1,0:T(8,128)(2,1)}, bf16[512,1024]{1,0:T(8,128)(2,1)S(1)}, u32[]{:S(2)}, u32[]{:S(2)}) %collective-permute-start.2) | collective-permute-done | bytes 1048608 | tf_op jit(solution)/shard_map/ppermute | solution.py:871
  266.1 25.0 %shard_map.484 = (f32[512,2048]{1,0:T(8,128)}, f32[512,2048]{1,0:T(8,128)}, f32[528,2048]{1,0:T(8,128)}, f32[128,2048]{1,0:T(8,128)}, f32[528,384]{1,0:T(8,128)}...) custom-call(bf16[528,1024]{1,0:T(8,128)(2,1)} %pad_maximum_fusion.5.nx, bf16[8,816,1024]{2,1,0:T(8,128)(2,1)} %bitcast.178, ...), custom_call_target="tpu_custom_call" | custom-call | flops 4429185024 | bytes 20971520 | tf_op jit(solution)/shard_map/pallas_call | solution.py:236
  295.4 8.7 all-gather.11.cloned.1.call-done
  307.9 15.0 %shard_map.485 = (f32[512,2048]{1,0:T(8,128)}, bf16[512,2048]{1,0:T(8,128)(2,1)}, f32[512,128]{1,0:T(8,128)}, f32[512,1024]{1,0:T(8,128)}) custom-call(f32[512,2048]{1,0:T(8,128)} %get-tuple-element.82.y, f32[512,2048]{1,0:T(8,128)} %get-tuple-element.83.gate, bf16[512,128]{1,0:T(8,128)(2,1)} %get-tuple-element.84.c, f32[512,128]{1,0:T(8,128)} %get-tuple-element.85.ecf, ...), custom_call_target="tpu_custom_call" | custom-call | flops 2147483648 | bytes 18874368 | tf_op jit(solution)/shard_map/pallas_call | solution.py:307
  329.8 24.9 %shard_map.486 = (f32[512,2048]{1,0:T(8,128)}, f32[512,2048]{1,0:T(8,128)}, f32[528,2048]{1,0:T(8,128)}, f32[128,2048]{1,0:T(8,128)}, f32[528,384]{1,0:T(8,128)}...) custom-call(bf16[528,1024]{1,0:T(8,128)(2,1)} %pad_maximum_fusion.6.nx, bf16[8,816,1024]{2,1,0:T(8,128)(2,1)} %bitcast.183, ...), custom_call_target="tpu_custom_call" | custom-call | flops 4429185024 | bytes 20971520 | tf_op jit(solution)/shard_map/pallas_call | solution.py:236
  360.1 15.0 %shard_map.487 = (f32[512,2048]{1,0:T(8,128)}, bf16[512,2048]{1,0:T(8,128)(2,1)}, f32[512,128]{1,0:T(8,128)}, f32[512,1024]{1,0:T(8,128)}) custom-call(f32[512,2048]{1,0:T(8,128)} %get-tuple-element.88.y, f32[512,2048]{1,0:T(8,128)} %get-tuple-element.89.gate, bf16[512,128]{1,0:T(8,128)(2,1)} %get-tuple-element.90.c, f32[512,128]{1,0:T(8,128)} %get-tuple-element.91.ecf, ...), custom_call_target="tpu_custom_call" | custom-call | flops 2147483648 | bytes 18874368 | tf_op jit(solution)/shard_map/pallas_call | solution.py:307
  388.0 5.7 collective-permute-done.18
  393.8 10.7 collective-permute-done.19
  406.1 28.3 %shard_map.488 = f32[8,512]{1,0:T(8,128)} custom-call(bf16[4,2,3200,512]{3,2,1,0:T(8,128)(2,1)} %bitcast.188, bf16[512,1024]{1,0:T(8,128)(2,1)} %bitcast.217, s32[8,512]{1,0:T(8,128)} %broadcast_in_dim.36.wanted), custom_call_target="tpu_custom_call" | custom-call | flops 13421772800 | bytes 26214400 | tf_op jit(solution)/shard_map/pallas_call | solution.py:820
  435.2 6.2 collective-permute-start.21
  448.9 59.2 %shard_map.489 = (bf16[4,2,3200,512]{3,2,1,0:T(8,128)(2,1)}, bf16[512,1024]{1,0:T(8,128)(2,1)}) custom-call(bf16[4,2,3200,512]{3,2,1,0:T(8,128)(2,1)} %bitcast.189, bf16[512,1024]{1,0:T(8,128)(2,1)} %bitcast.218, s32[8,512]{1,0:T(8,128)} %broadcast_in_dim.36.wanted, f32[8,512]{1,0:T(8,128)} %select_maximum_fusion.1.stats), custom_call_target="tpu_custom_call" | custom-call | flops 40265318400 | bytes 52428800 | tf_op jit(solution)/shard_map/pallas_call | solution.py:857
  512.9 6.1 collective-permute-done.23
  519.0 14.6 %collective-permute-done.24 = bf16[128,1024]{1,0:T(8,128)(2,1)S(1)} collective-permute-done((bf16[128,1024]{1,0:T(8,128)(2,1)S(1)}, bf16[128,1024]{1,0:T(8,128)(2,1)S(1)}, u32[]{:S(2)}, u32[]{:S(2)}) %collective-permute-start.24) | collective-permute-done | bytes 262176 | tf_op jit(solution)/shard_map/ppermute | solution.py:871
  539.3 18.0 %shard_map.490 = (f32[512,2048]{1,0:T(8,128)}, bf16[512,2048]{1,0:T(8,128)(2,1)}, f32[8,2048]{1,0:T(8,128)}, f32[128,2048]{1,0:T(8,128)}) custom-call(bf16[512,1024]{1,0:T(8,128)(2,1)} %get-tuple-element.253.dout, bf16[8,816,1024]{2,1,0:T(8,128)(2,1)} %bitcast.185, f32[512,2048]{1,0:T(8,128)} %get-tuple-element.96.y, f32[512,2048]{1,0:T(8,128)} %get-tuple-element.89.gate, ...), custom_call_target="tpu_custom_call" | custom-call | flops 2147483648 | bytes 27262976 | tf_op jit(solution)/shard_map/pallas_call | solution.py:384
  558.6 3.5 collective-permute-done.27.dst
  563.0 49.9 %shard_map.491 = (bf16[512,2048]{1,0:T(8,128)(2,1)}, f32[16,2048]{1,0:T(8,128)}, f32[16,2048]{1,0:T(8,128)}, f32[8,2048]{1,0:T(8,128)}, f32[512,384]{1,0:T(8,128...) custom-call(f32[528,2048]{1,0:T(8,128)} %get-tuple-element.99.xraw, f32[512,2048]{1,0:T(8,128)} %get-tuple-element.100.dy, ...), custom_call_target="tpu_custom_call" | custom-call | flops 2684354560 | bytes 12582912 | tf_op jit(solution)/shard_map/pallas_call | solution.py:566
  618.2 21.9 %shard_map.492 = (bf16[1024,6656]{1,0:T(8,128)(2,1)}, f32[512,1024]{1,0:T(8,128)}, f32[8,1024]{1,0:T(8,128)}) custom-call(bf16[512,1024]{1,0:T(8,128)(2,1)} %copy-done.16, bf16[512,1024]{1,0:T(8,128)(2,1)} %get-tuple-element.253.dout, bf16[512,2048]{1,0:T(8,128)(2,1)} %get-tuple-element.98.dgate, bf16[512,2048]{1,0:T(8,128)(2,1)} %get-tuple-element.103.dx, ...), custom_call_target="tpu_custom_call" | custom-call | flops 10737418240 | bytes 54525952 | tf_op jit(solution)/shard_map/pallas_call | solution.py:664
  642.8 20.3 %shard_map.493 = (f32[512,2048]{1,0:T(8,128)}, bf16[512,2048]{1,0:T(8,128)(2,1)}, f32[8,2048]{1,0:T(8,128)}, f32[128,2048]{1,0:T(8,128)}) custom-call(bf16[512,1024]{1,0:T(8,128)(2,1)} %convert_element_type.167.dout, bf16[8,816,1024]{2,1,0:T(8,128)(2,1)} %bitcast.180, f32[512,2048]{1,0:T(8,128)} %get-tuple-element.110.y, ...), custom_call_target="tpu_custom_call" | custom-call | flops 2147483648 | bytes 27262976 | tf_op jit(solution)/shard_map/pallas_call | solution.py:384
  668.8 49.7 %shard_map.494 = (bf16[512,2048]{1,0:T(8,128)(2,1)}, f32[16,2048]{1,0:T(8,128)}, f32[16,2048]{1,0:T(8,128)}, f32[8,2048]{1,0:T(8,128)}, f32[512,384]{1,0:T(8,128...) custom-call(f32[528,2048]{1,0:T(8,128)} %get-tuple-element.113.xraw, ...), custom_call_target="tpu_custom_call" | custom-call | flops 2684354560 | bytes 12582912 | tf_op jit(solution)/shard_map/pallas_call | solution.py:566
  723.8 22.0 %shard_map.495 = (bf16[1024,6656]{1,0:T(8,128)(2,1)}, f32[512,1024]{1,0:T(8,128)}, f32[8,1024]{1,0:T(8,128)}) custom-call(bf16[512,1024]{1,0:T(8,128)(2,1)} %copy-done.15, bf16[512,1024]{1,0:T(8,128)(2,1)} %convert_element_type.167.dout, bf16[512,2048]{1,0:T(8,128)(2,1)} %get-tuple-element.112.dgate, bf16[512,2048]{1,0:T(8,128)(2,1)} %get-tuple-element.117.dx, ...), custom_call_target="tpu_custom_call" | custom-call | flops 10737418240 | bytes 54525952 | tf_op jit(solution)/shard_map/pallas_call | solution.py:664
  752.3 23.2 %collective-permute-done.33 = bf16[512,1024]{1,0:T(8,128)(2,1)S(1)} collective-permute-done((bf16[512,1024]{1,0:T(8,128)(2,1)S(1)}, bf16[512,1024]{1,0:T(8,128)(2,1)S(1)}, u32[]{:S(2)}, u32[]{:S(2)}) %collective-permute-start.33) | collective-permute-done | bytes 1048608 | tf_op jit(solution)/shard_map/ppermute | solution.py:871
  775.5 44.0 %collective-permute-done.34 = bf16[512,1024]{1,0:T(8,128)(2,1)S(1)} collective-permute-done((bf16[512,1024]{1,0:T(8,128)(2,1)S(1)}, bf16[512,1024]{1,0:T(8,128)(2,1)S(1)}, u32[]{:S(2)}, u32[]{:S(2)}) %collective-permute-start.34) | collective-permute-done | bytes 1048608 | tf_op jit(solution)/shard_map/ppermute | solution.py:871
  821.8 26.0 %shard_map.496 = bf16[4,2,3200,512]{3,2,1,0:T(8,128)(2,1)} custom-call(s32[2048]{0:T(1024)} %select_reduce_fusion.keys, s32[8]{0:T(128)} %convert_reduce_fusion.1.starts, bf16[4,2,3200,512]{3,2,1,0:T(8,128)(2,1)} %get-tuple-element.94.table, bf16[2048,1024]{1,0:T(8,128)(2,1)} %bitcast.190), custom_call_target="tpu_custom_call" | custom-call | bytes 52428800 | tf_op jit(solution)/shard_map/pallas_call | solution.py:766
  854.9 20.9 %collective-permute-start.43 = (f32[242,128]{1,0:T(8,128)S(1)}, f32[242,128]{1,0:T(8,128)S(1)}, u32[]{:S(2)}, u32[]{:S(2)}) collective-permute-start(f32[242,128]{1,0:T(8,128)S(1)} %fusion.62), channel_id=1, source_target_pairs={{0,1},{1,0},{2,3},{3,2},{4,5},{5,4},{6,7},{7,6},{8,9},{9,8},{10,11... | collective-permute-start | bytes 371720 | tf_op jit(solution)/shard_map/ppermute | solution.py:891
  879.8 3.9 collective-permute-start.44
  884.4 5.5 collective-permute-done.44
  889.8 5.3 collective-permute-start.45
  915.6 3.5 collective-permute-start.40
  928.6 40.2 %collective-permute-done.39 = bf16[128,1920]{1,0:T(8,128)(2,1)} collective-permute-done((bf16[128,1920]{1,0:T(8,128)(2,1)}, bf16[128,1920]{1,0:T(8,128)(2,1)}, u32[]{:S(2)}, u32[]{:S(2)}) %collective-permute-start.39) | collective-permute-done | bytes 491552 | tf_op jit(solution)/shard_map/ppermute | solution.py:871
  971.9 19.8 %collective-permute-done.36 = bf16[128,1920]{1,0:T(8,128)(2,1)} collective-permute-done((bf16[128,1920]{1,0:T(8,128)(2,1)}, bf16[128,1920]{1,0:T(8,128)(2,1)}, u32[]{:S(2)}, u32[]{:S(2)}) %collective-permute-start.36) | collective-permute-done | bytes 491552 | tf_op jit(solution)/shard_map/ppermute | solution.py:871
  1000.8 33.9 %reduce-scatter.4.cloned.1.call-done = bf16[1,3200,512]{2,1,0:T(8,128)(2,1)} async-done(((bf16[8,3200,512]{2,1,0:T(8,128)(2,1)}), bf16[1,3200,512]{2,1,0:T(8,128)(2,1)}) %reduce-scatter.4.cloned.1.call-update) | async-done | bytes 3276816 | tf_op jit(solution)/shard_map/reduce_scatter | solution.py:1162
  1034.7 4.3 fusion
  1082.7 4.6 multiply_reduce_fusion.7
  1087.5 11.2 multiply_reduce_fusion
  1130.8 10.1 multiply_subtract_fusion
  (567 shorter events, 239.7 us)
Async XLA Ops:
  7.2 141.6 %all-gather.7.cloned.1.call-start = ((), (), s32[]{:S(2)}) async-start(), calls=%async_computation.6 | async-start | bytes 29491200 | tf_op jit(solution)/shard_map/all_gather | solution.py:1092
  16.1 210.6 %all-gather.9.cloned.1.call-start = ((), (), s32[]{:S(2)}) async-start(), calls=%async_computation.7 | async-start | bytes 15040512 | tf_op jit(solution)/shard_map/all_gather | solution.py:1094
  17.8 14.6 %collective-permute-start.7 = (bf16[192,1024]{1,0:T(8,128)(2,1)S(1)}, bf16[192,1024]{1,0:T(8,128)(2,1)S(1)}, u32[]{:S(2)}, u32[]{:S(2)}) collective-permute-start(bf16[192,1024]{1,0:T(8,128)(2,1)S(1)} %pad_maximum_fusion.17), channel_id=1, source_target_pairs={{0,3},{1,0},{2,1},{3,2},{4,7},{5,4},{6,5},{7,6},{8,11},{9,8},{10,9... | collective-permute-start | bytes 1179656 | tf_op jit(solution)/shard_map/ppermute | solution.py:871
  22.9 19.0 %collective-permute-start.5 = (bf16[192,1024]{1,0:T(8,128)(2,1)S(1)}, bf16[192,1024]{1,0:T(8,128)(2,1)S(1)}, u32[]{:S(2)}, u32[]{:S(2)}) collective-permute-start(bf16[192,1024]{1,0:T(8,128)(2,1)S(1)} %pad_maximum_fusion.17), channel_id=1, source_target_pairs={{0,1},{1,2},{2,3},{3,0},{4,5},{5,6},{6,7},{7,4},{8,9},{9,10},{10,1... | collective-permute-start | bytes 1179656 | tf_op jit(solution)/shard_map/ppermute | solution.py:871
  22.9 33.5 %collective-permute-start.6 = (bf16[192,1024]{1,0:T(8,128)(2,1)S(1)}, bf16[192,1024]{1,0:T(8,128)(2,1)S(1)}, u32[]{:S(2)}, u32[]{:S(2)}) collective-permute-start(bf16[192,1024]{1,0:T(8,128)(2,1)S(1)} %pad_maximum_fusion.17), channel_id=1, source_target_pairs={{0,2},{1,3},{2,0},{3,1},{4,6},{5,7},{6,4},{7,5},{8,10},{9,11},{10,... | collective-permute-start | bytes 1179656 | tf_op jit(solution)/shard_map/ppermute | solution.py:871
  58.1 246.0 %all-gather.11.cloned.1.call-start = ((), (), s32[]{:S(2)}) async-start(), calls=%async_computation.8 | async-start | bytes 15040512 | tf_op jit(solution)/shard_map/all_gather | solution.py:1094
  58.2 14.0 %collective-permute-start.13 = (bf16[192,1024]{1,0:T(8,128)(2,1)S(1)}, bf16[192,1024]{1,0:T(8,128)(2,1)S(1)}, u32[]{:S(2)}, u32[]{:S(2)}) collective-permute-start(bf16[192,1024]{1,0:T(8,128)(2,1)S(1)} %pad_maximum_fusion.18), channel_id=1, source_target_pairs={{0,1},{1,2},{2,3},{3,0},{4,5},{5,6},{6,7},{7,4},{8,9},{9,10},{10,1... | collective-permute-start | bytes 1179656 | tf_op jit(solution)/shard_map/ppermute | solution.py:871
  58.3 28.8 %collective-permute-start.14 = (bf16[192,1024]{1,0:T(8,128)(2,1)S(1)}, bf16[192,1024]{1,0:T(8,128)(2,1)S(1)}, u32[]{:S(2)}, u32[]{:S(2)}) collective-permute-start(bf16[192,1024]{1,0:T(8,128)(2,1)S(1)} %pad_maximum_fusion.18), channel_id=1, source_target_pairs={{0,2},{1,3},{2,0},{3,1},{4,6},{5,7},{6,4},{7,5},{8,10},{9,11},{10,... | collective-permute-start | bytes 1179656 | tf_op jit(solution)/shard_map/ppermute | solution.py:871
  61.5 25.6 %collective-permute-start.15 = (bf16[192,1024]{1,0:T(8,128)(2,1)S(1)}, bf16[192,1024]{1,0:T(8,128)(2,1)S(1)}, u32[]{:S(2)}, u32[]{:S(2)}) collective-permute-start(bf16[192,1024]{1,0:T(8,128)(2,1)S(1)} %pad_maximum_fusion.18), channel_id=1, source_target_pairs={{0,3},{1,0},{2,1},{3,2},{4,7},{5,4},{6,5},{7,6},{8,11},{9,8},{10,9... | collective-permute-start | bytes 1179656 | tf_op jit(solution)/shard_map/ppermute | solution.py:871
  88.8 818.2 %reduce-scatter.8.cloned.1.call-start = ((), (), s32[]{:S(2)}) async-start(), calls=%async_computation.5 | async-start | bytes 15335424 | tf_op jit(solution)/shard_map/reduce_scatter | solution.py:963
  88.9 17.1 %collective-permute-start.8 = (f32[2,9,512]{2,0,1:T(2,128)S(1)}, f32[2,9,512]{2,0,1:T(2,128)S(1)}, u32[]{:S(2)}, u32[]{:S(2)}) collective-permute-start(f32[2,9,512]{2,0,1:T(2,128)S(1)} %fusion.31), channel_id=1, source_target_pairs={{0,1},{1,2},{2,3},{3,0},{4,5},{5,6},{6,7},{7,4},{8,9},{9,10},{10,1... | collective-permute-start | bytes 110600 | tf_op jit(solution)/shard_map/ppermute | solution.py:871
  97.0 9.0 collective-permute-start.9
  97.0 9.0 collective-permute-start.10
  168.3 61.3 %collective-permute-start.1 = (bf16[512,1024]{1,0:T(8,128)(2,1)}, bf16[512,1024]{1,0:T(8,128)(2,1)S(1)}, u32[]{:S(2)}, u32[]{:S(2)}) collective-permute-start(bf16[512,1024]{1,0:T(8,128)(2,1)} %get-tuple-element.267), channel_id=1, source_target_pairs={{0,3},{1,0},{2,1},{3,2},{4,7},{5,4},{6,5},{7,6},{8,11},{9,8},{10,9... | collective-permute-start | bytes 3145736 | tf_op jit(solution)/shard_map/ppermute | solution.py:871
  174.9 83.8 %collective-permute-start.2 = (bf16[512,1024]{1,0:T(8,128)(2,1)}, bf16[512,1024]{1,0:T(8,128)(2,1)S(1)}, u32[]{:S(2)}, u32[]{:S(2)}) collective-permute-start(bf16[512,1024]{1,0:T(8,128)(2,1)} %get-tuple-element.269), channel_id=1, source_target_pairs={{0,2},{1,3},{2,0},{3,1},{4,6},{5,7},{6,4},{7,5},{8,10},{9,11},{10,... | collective-permute-start | bytes 3145736 | tf_op jit(solution)/shard_map/ppermute | solution.py:871
  174.9 84.8 %collective-permute-start.3 = (bf16[512,1024]{1,0:T(8,128)(2,1)}, bf16[512,1024]{1,0:T(8,128)(2,1)}, u32[]{:S(2)}, u32[]{:S(2)}) collective-permute-start(bf16[512,1024]{1,0:T(8,128)(2,1)} %get-tuple-element.268), channel_id=1, source_target_pairs={{0,1},{1,2},{2,3},{3,0},{4,5},{5,6},{6,7},{7,4},{8,9},{9,10},{10,1... | collective-permute-start | bytes 3145736 | tf_op jit(solution)/shard_map/ppermute | solution.py:871
  291.2 15.8 %collective-permute-start.11 = (f32[128,2048]{1,0:T(8,128)}, f32[128,2048]{1,0:T(8,128)S(1)}, u32[]{:S(2)}, u32[]{:S(2)}) collective-permute-start(f32[128,2048]{1,0:T(8,128)} %get-tuple-element.86), channel_id=1, source_target_pairs={{0,4},{1,5},{2,6},{3,7},{8,12},{9,13},{10,14},{11,15},{16,20},{17,... | collective-permute-start | bytes 3145736 | tf_op jit(solution)/shard_map/ppermute | solution.py:879
  354.6 4.5 collective-permute-start.16
  382.6 11.1 collective-permute-start.18
  384.2 20.2 %collective-permute-start.19 = (bf16[128,1024]{1,0:T(8,128)(2,1)S(1)}, bf16[128,1024]{1,0:T(8,128)(2,1)S(1)}, u32[]{:S(2)}, u32[]{:S(2)}) collective-permute-start(bf16[128,1024]{1,0:T(8,128)(2,1)S(1)} %fusion.7), channel_id=1, source_target_pairs={{0,2},{1,3},{2,0},{3,1},{4,6},{5,7},{6,4},{7,5},{8,10},{9,11},{10,... | collective-permute-start | bytes 786440 | tf_op jit(solution)/shard_map/ppermute | solution.py:871
  386.6 17.8 %collective-permute-start.20 = (bf16[128,1024]{1,0:T(8,128)(2,1)S(1)}, bf16[128,1024]{1,0:T(8,128)(2,1)S(1)}, u32[]{:S(2)}, u32[]{:S(2)}) collective-permute-start(bf16[128,1024]{1,0:T(8,128)(2,1)S(1)} %fusion.7), channel_id=1, source_target_pairs={{0,3},{1,0},{2,1},{3,2},{4,7},{5,4},{6,5},{7,6},{8,11},{9,8},{10,9... | collective-permute-start | bytes 786440 | tf_op jit(solution)/shard_map/ppermute | solution.py:871
  435.2 7.8 collective-permute-start.21
  443.0 4.6 collective-permute-start.22
  509.3 9.7 collective-permute-start.23
  512.3 21.3 %collective-permute-start.24 = (bf16[128,1024]{1,0:T(8,128)(2,1)S(1)}, bf16[128,1024]{1,0:T(8,128)(2,1)S(1)}, u32[]{:S(2)}, u32[]{:S(2)}) collective-permute-start(bf16[128,1024]{1,0:T(8,128)(2,1)S(1)} %get-tuple-element.284), channel_id=1, source_target_pairs={{0,2},{1,3},{2,0},{3,1},{4,6},{5,7},{6,4},{7,5},{8,10},{9,11},{10,... | collective-permute-start | bytes 786440 | tf_op jit(solution)/shard_map/ppermute | solution.py:871
  512.8 20.8 %collective-permute-start.25 = (bf16[128,1024]{1,0:T(8,128)(2,1)S(1)}, bf16[128,1024]{1,0:T(8,128)(2,1)S(1)}, u32[]{:S(2)}, u32[]{:S(2)}) collective-permute-start(bf16[128,1024]{1,0:T(8,128)(2,1)S(1)} %get-tuple-element.283), channel_id=1, source_target_pairs={{0,1},{1,2},{2,3},{3,0},{4,5},{5,6},{6,7},{7,4},{8,9},{9,10},{10,1... | collective-permute-start | bytes 786440 | tf_op jit(solution)/shard_map/ppermute | solution.py:871
  557.3 4.8 collective-permute-start.27
  612.9 4.6 collective-permute-start.28
  640.1 271.6 %reduce-scatter.6.cloned.1.call-start = ((), (), s32[]{:S(2)}) async-start(), calls=%async_computation.4 | async-start | bytes 15335424 | tf_op jit(solution)/shard_map/reduce_scatter | solution.py:963
  663.1 4.8 collective-permute-start.30
  718.5 4.6 collective-permute-start.31
  745.8 288.8 %reduce-scatter.4.cloned.1.call-start = ((), (), s32[]{:S(2)}) async-start(), calls=%async_computation.3 | async-start | bytes 29491200 | tf_op jit(solution)/shard_map/reduce_scatter | solution.py:1162
  747.5 28.0 %collective-permute-start.33 = (bf16[512,1024]{1,0:T(8,128)(2,1)S(1)}, bf16[512,1024]{1,0:T(8,128)(2,1)S(1)}, u32[]{:S(2)}, u32[]{:S(2)}) collective-permute-start(bf16[512,1024]{1,0:T(8,128)(2,1)S(1)} %convert_element_type.168), channel_id=1, source_target_pairs={{0,1},{1,2},{2,3},{3,0},{4,5},{5,6},{6,7},{7,4},{8,9},{9,10},{10,1... | collective-permute-start | bytes 3145736 | tf_op jit(solution)/shard_map/ppermute | solution.py:871
  747.6 71.9 %collective-permute-start.34 = (bf16[512,1024]{1,0:T(8,128)(2,1)S(1)}, bf16[512,1024]{1,0:T(8,128)(2,1)S(1)}, u32[]{:S(2)}, u32[]{:S(2)}) collective-permute-start(bf16[512,1024]{1,0:T(8,128)(2,1)S(1)} %convert_element_type.168), channel_id=1, source_target_pairs={{0,2},{1,3},{2,0},{3,1},{4,6},{5,7},{6,4},{7,5},{8,10},{9,11},{10,... | collective-permute-start | bytes 3145736 | tf_op jit(solution)/shard_map/ppermute | solution.py:871
  749.3 70.2 %collective-permute-start.35 = (bf16[512,1024]{1,0:T(8,128)(2,1)S(1)}, bf16[512,1024]{1,0:T(8,128)(2,1)S(1)}, u32[]{:S(2)}, u32[]{:S(2)}) collective-permute-start(bf16[512,1024]{1,0:T(8,128)(2,1)S(1)} %convert_element_type.168), channel_id=1, source_target_pairs={{0,3},{1,0},{2,1},{3,2},{4,7},{5,4},{6,5},{7,6},{8,11},{9,8},{10,9... | collective-permute-start | bytes 3145736 | tf_op jit(solution)/shard_map/ppermute | solution.py:871
  854.9 24.8 %collective-permute-start.43 = (f32[242,128]{1,0:T(8,128)S(1)}, f32[242,128]{1,0:T(8,128)S(1)}, u32[]{:S(2)}, u32[]{:S(2)}) collective-permute-start(f32[242,128]{1,0:T(8,128)S(1)} %fusion.62), channel_id=1, source_target_pairs={{0,1},{1,0},{2,3},{3,2},{4,5},{5,4},{6,7},{7,6},{8,9},{9,8},{10,11... | collective-permute-start | bytes 371720 | tf_op jit(solution)/shard_map/ppermute | solution.py:891
  879.8 10.1 collective-permute-start.44
  889.8 9.4 collective-permute-start.45
  899.3 5.0 collective-permute-start.46
  914.8 54.1 %collective-permute-start.39 = (bf16[128,1920]{1,0:T(8,128)(2,1)}, bf16[128,1920]{1,0:T(8,128)(2,1)}, u32[]{:S(2)}, u32[]{:S(2)}) collective-permute-start(bf16[128,1920]{1,0:T(8,128)(2,1)} %concatenate.166), channel_id=1, source_target_pairs={{0,2},{1,3},{2,0},{3,1},{4,6},{5,7},{6,4},{7,5},{8,10},{9,11},{10,... | collective-permute-start | bytes 1474568 | tf_op jit(solution)/shard_map/ppermute | solution.py:871
  915.6 53.4 %collective-permute-start.40 = (bf16[128,1920]{1,0:T(8,128)(2,1)}, bf16[128,1920]{1,0:T(8,128)(2,1)}, u32[]{:S(2)}, u32[]{:S(2)}) collective-permute-start(bf16[128,1920]{1,0:T(8,128)(2,1)} %concatenate.167), channel_id=1, source_target_pairs={{0,1},{1,2},{2,3},{3,0},{4,5},{5,6},{6,7},{7,4},{8,9},{9,10},{10,1... | collective-permute-start | bytes 1474568 | tf_op jit(solution)/shard_map/ppermute | solution.py:871
  920.0 49.0 %collective-permute-start.41 = (bf16[128,1920]{1,0:T(8,128)(2,1)}, bf16[128,1920]{1,0:T(8,128)(2,1)}, u32[]{:S(2)}, u32[]{:S(2)}) collective-permute-start(bf16[128,1920]{1,0:T(8,128)(2,1)} %concatenate.168), channel_id=1, source_target_pairs={{0,3},{1,0},{2,1},{3,2},{4,7},{5,4},{6,5},{7,6},{8,11},{9,8},{10,9... | collective-permute-start | bytes 1474568 | tf_op jit(solution)/shard_map/ppermute | solution.py:871
  925.2 66.6 %collective-permute-start.36 = (bf16[128,1920]{1,0:T(8,128)(2,1)}, bf16[128,1920]{1,0:T(8,128)(2,1)}, u32[]{:S(2)}, u32[]{:S(2)}) collective-permute-start(bf16[128,1920]{1,0:T(8,128)(2,1)} %concatenate.162), channel_id=1, source_target_pairs={{0,2},{1,3},{2,0},{3,1},{4,6},{5,7},{6,4},{7,5},{8,10},{9,11},{10,... | collective-permute-start | bytes 1474568 | tf_op jit(solution)/shard_map/ppermute | solution.py:871
  927.2 64.5 %collective-permute-start.37 = (bf16[128,1920]{1,0:T(8,128)(2,1)}, bf16[128,1920]{1,0:T(8,128)(2,1)}, u32[]{:S(2)}, u32[]{:S(2)}) collective-permute-start(bf16[128,1920]{1,0:T(8,128)(2,1)} %concatenate.163), channel_id=1, source_target_pairs={{0,1},{1,2},{2,3},{3,0},{4,5},{5,6},{6,7},{7,4},{8,9},{9,10},{10,1... | collective-permute-start | bytes 1474568 | tf_op jit(solution)/shard_map/ppermute | solution.py:871
  968.9 22.8 %collective-permute-start.38 = (bf16[128,1920]{1,0:T(8,128)(2,1)}, bf16[128,1920]{1,0:T(8,128)(2,1)}, u32[]{:S(2)}, u32[]{:S(2)}) collective-permute-start(bf16[128,1920]{1,0:T(8,128)(2,1)} %concatenate.164), channel_id=1, source_target_pairs={{0,3},{1,0},{2,1},{3,2},{4,7},{5,4},{6,5},{7,6},{8,11},{9,8},{10,9... | collective-permute-start | bytes 1474568 | tf_op jit(solution)/shard_map/ppermute | solution.py:871
  1047.7 4.4 collective-permute-start.49
  1056.2 5.1 collective-permute-start.51
  1112.3 6.4 collective-permute-start.56
  (104 other events, 1056.9 us)
Sparse Core Ops, SparseCore 0:
  16.3 132.4 all-gather.6
  151.2 75.4 all-gather.8
  228.6 75.4 all-gather.10
  640.2 95.8 reduce-scatter.7
  745.9 96.3 reduce-scatter.5
  848.0 186.5 reduce-scatter.3

commit v2 on v1

--- a/solution.py
+++ b/solution.py
@@ -23,9 +23,10 @@
 WIDTH = 512
 GROUPS = INNER // WIDTH
 LANES = 128
-TILE = 640
+TILE = 800
 CLASSES = 4
 PAST = 1 << 11
+CAP = 128
 
 norm_eps = 1e-05
 adam_eps = 1e-06
@@ -70,6 +71,11 @@
 
 def softplus(v):
     return jnp.maximum(v, 0.0) + jnp.log1p(jnp.exp(-jnp.abs(v)))
+
+
+def normed(values, gain):
+    inverse = lax.rsqrt(jnp.mean(values * values, axis=1, keepdims=True) + norm_eps)
+    return (values * inverse * gain).astype(bf16)
 
 
 def iota(shape, axis):
@@ -131,10 +137,20 @@
     return iota((BLOCK, BLOCK), 0) >= iota((BLOCK, BLOCK), 1)
 
 
+def expanded(values, marks, parts=3, by=nn):
+    result = None
+    for _ in range(parts):
+        part = values.astype(bf16)
+        values = values - part.astype(f32)
+        term = by(part, marks)
+        result = term if result is None else result + term
+    return result
+
+
 def spread(group):
     head = iota((LANES, WIDTH), 0)
     lane = iota((LANES, WIDTH), 1)
-    return (head == group * (WIDTH // HDIM) + lane // HDIM).astype(f32)
+    return (head == group * (WIDTH // HDIM) + lane // HDIM).astype(bf16)
 
 
 def small_parts(rows, bcdt, headp, bcv, s_b, s_c, s_dt, s_cum, s_cumt, s_g):
@@ -206,12 +222,12 @@
     pre = conv_rows(xraw_o, chan, rows, 0, WIDTH)
     xc = pre * sigmoid(pre)
     expand = spread(group)
-    u = xc * nn(s_dt[...], expand, full)
-    skip = nn(headp[...], expand, full)[2:3, :]
+    u = xc * expanded(s_dt[...], expand)
+    skip = expanded(headp[...], expand)[2:3, :]
     state = jnp.zeros((STATE, WIDTH), f32)
     for b in range(rows // BLOCK):
         r = slice(b * BLOCK, (b + 1) * BLOCK)
-        cum_e = nn(s_cum[r, :], expand, full)
+        cum_e = expanded(s_cum[r, :], expand)
         total = cum_e[BLOCK - 1 : BLOCK, :]
         keys, reads = s_b[r, :], s_c[r, :]
         y = jnp.exp(cum_e) * nn(reads, state.astype(bf16)) + skip * xc[r]
@@ -269,10 +285,11 @@
 
 
 def join_kernel(
-    y, gate, c, ecf, st, chan, wout, resid, yf_o, scaled_o, inv_o, res_o, s_gated, s_square
+    y, gate, c, ecf, st, chan, wout, resid, gain,
+    yf_o, scaled_o, inv_o, res_o, normed_o, s_gated, s_square,
 ):
     group = pl.program_id(0)
-    ecf_e = nn(ecf[...], spread(group), full)
+    ecf_e = expanded(ecf[...], spread(group))
     yf = y[...] + ecf_e * nn(c[...], st[...].astype(bf16))
     yf_o[...] = yf
     gated = yf * (gate[...] * sigmoid(gate[...]))
@@ -299,9 +316,10 @@
             height = D // wout.shape[0]
             res = res + nt(scaled, unpacked_out(wout, q * height // 2, height))
         res_o[...] = res
-
-
-def scan_join(y, gate, c, ecf, st, chan, packed, resid):
+        normed_o[...] = normed(res, gain[0:1, :])
+
+
+def scan_join(y, gate, c, ecf, st, chan, packed, resid, gain):
     rows = y.shape[0]
     height = D // packed.shape[0]
     return call(
@@ -316,18 +334,20 @@
             whole((8, INNER)),
             pl.BlockSpec((packed.shape[0], 2 * height, D), lambda g: (0, 2, 0)),
             whole((rows, D)),
+            whole((8, D)),
         ],
-        [columns(rows), whole((rows, INNER)), whole((rows, LANES)), whole((rows, D))],
+        [columns(rows), whole((rows, INNER)), whole((rows, LANES))] + [whole((rows, D))] * 2,
         [
             struct((rows, INNER)),
             struct((rows, INNER), bf16),
             struct((rows, LANES)),
             struct((rows, D)),
+            struct((rows, D), bf16),
         ],
         [pltpu.VMEM((GROUPS, rows, WIDTH), f32), pltpu.VMEM((rows, LANES), f32)],
         flops=2 * rows * D * INNER,
         bytes_moved=2 * D * INNER + 14 * rows * INNER,
-    )(y, gate, c, ecf, st, chan, packed, resid)
+    )(y, gate, c, ecf, st, chan, packed, resid, gain)
 
 
 def unjoin_kernel(
@@ -367,7 +387,7 @@
         dy = dgated * opened
         dy_o[...] = dy
         dgate_o[...] = (dgated * y[...] * (sig * (1.0 + raw * (1.0 - sig)))).astype(bf16)
-        ecf_e = nn(ecf[...], spread(group), full)
+        ecf_e = expanded(ecf[...], spread(group))
         ds_o[...] = tn(c[...], (ecf_e * dy).astype(bf16))
 
 
@@ -412,8 +432,8 @@
 
 def head_sums(values, expand):
     if values.shape[0] == 1:
-        return nt(jnp.broadcast_to(values, (8, values.shape[1])), expand, full)[0:1, :]
-    return nt(values, expand, full)
+        return head_sums(jnp.broadcast_to(values, (8, values.shape[1])), expand)[0:1, :]
+    return expanded(values, expand, by=nt)
 
 
 def conv_back(ref, taps, pad, rows, low, width, taps_o, main, halo):
@@ -433,7 +453,7 @@
     xraw, dy, bcdt, st, dst, chan, headp, bcv,
     dx_o, tail_o, halo_o, dchan_o, dbc_o, dbch_o, dheadp_o, dbcv_o,
     s_b, s_c, s_dt, s_cum, s_cumt, s_g,
-    s_db, s_dc, s_dcum, s_ddt, s_dtot, s_dg, s_skip, s_pad, s_state, s_bcpad,
+    s_db, s_dc, s_dcum, s_ddt, s_dtot, s_dg, s_skip, s_pad, s_state, s_bcpad, s_cume,
 ):
     rows = dy.shape[0]
     blocks = rows // BLOCK
@@ -449,15 +469,16 @@
     sig = sigmoid(pre)
     xc = pre * sig
     expand = spread(group)
-    dt_e = nn(s_dt[...], expand, full)
+    dt_e = expanded(s_dt[...], expand)
     u = xc * dt_e
-    skip = nn(headp[...], expand, full)[2:3, :]
+    skip = expanded(headp[...], expand)[2:3, :]
     state = st[...]
     for b in range(blocks):
         r = slice(b * BLOCK, (b + 1) * BLOCK)
         s_state[b] = state
+        cum_e = expanded(s_cum[r, :], expand)
+        s_cume[r, :] = cum_e
         if b < blocks - 1:
-            cum_e = nn(s_cum[r, :], expand, full)
             total = cum_e[BLOCK - 1 : BLOCK, :]
             fresh = tn(s_b[r, :], (u[r] * jnp.exp(total - cum_e)).astype(bf16))
             state = state * jnp.exp(total) + fresh
@@ -465,7 +486,7 @@
     dskip = jnp.zeros((1, WIDTH), f32)
     for b in reversed(range(blocks)):
         r = slice(b * BLOCK, (b + 1) * BLOCK)
-        cum_e = nn(s_cum[r, :], expand, full)
+        cum_e = s_cume[r, :]
         total = cum_e[BLOCK - 1 : BLOCK, :]
         keys, reads = s_b[r, :], s_c[r, :]
         to_here, to_end, passed = jnp.exp(cum_e), jnp.exp(total - cum_e), jnp.exp(total)
@@ -608,6 +629,7 @@
             pltpu.VMEM((rows + 2 * HALO, WIDTH), f32),
             pltpu.VMEM((blocks, STATE, WIDTH), f32),
             pltpu.VMEM((rows + 2 * HALO, 2 * STATE), f32),
+            pltpu.VMEM((rows, WIDTH), f32),
         ],
         flops=20 * rows * INNER * STATE,
         bytes_moved=12 * rows * INNER,
@@ -688,111 +710,210 @@
     )(normed, dout, dgate, dx, tail, back, dbcdt, bc_back, scaled, packed, wb, resid, dresid, gain)
 
 
-def lookup_kernel(keys, starts, table, out, s_rows):
+def lookup_kernel(keys, edges, first, second, out, s_rows):
     cls = pl.program_id(0)
-    parts, lines, width = table.shape[1:]
+    parts, lines, width = first.shape[1:]
 
     @pl.when(cls == 0)
     def _():
         s_rows[...] = jnp.zeros(s_rows.shape, f32)
 
     place = iota((16, width), 0)
-
-    def turn(i, carry):
-        key = keys[i]
-        at = key & (PAST - 1)
-        line = (key >> 11) - cls * lines
-        base = pl.multiple_of((line >> 4) << 4, 16)
-        found = []
-        for part in range(parts):
-            tile = table[0, part, pl.ds(base, 16), :].astype(f32)
-            found.append(
-                jnp.sum(jnp.where(place == (line & 15), tile, 0.0), axis=0, keepdims=True)
-            )
-        s_rows[pl.ds(at, 1), :] = jnp.concatenate(found, axis=1)
-        return carry
-
-    lax.fori_loop(starts[cls], starts[cls + 1], turn, 0)
+    for half, table in enumerate((first, second)):
+
+        def turn(i, carry, half=half, table=table):
+            key = keys[i]
+            at = key & (PAST - 1)
+            line = (key >> 11) - (2 * cls + half) * lines
+            base = pl.multiple_of((line >> 4) << 4, 16)
+            found = []
+            for part in range(parts):
+                tile = table[0, part, pl.ds(base, 16), :].astype(f32)
+                found.append(
+                    jnp.sum(jnp.where(place == (line & 15), tile, 0.0), axis=0, keepdims=True)
+                )
+            s_rows[pl.ds(at, 1), :] = jnp.concatenate(found, axis=1)
+            return carry
+
+        lax.fori_loop(edges[2 * cls + half], edges[2 * cls + half + 1], turn, 0)
 
     @pl.when(cls == CLASSES - 1)
     def _():
         out[...] = s_rows[...].astype(bf16)
 
 
-def lookup(keys, starts, table):
+def lookup(keys, edges, halves):
     count = keys.shape[0]
+    spec = pl.BlockSpec((1,) + halves[0].shape[1:], lambda c, *_: (c, 0, 0, 0))
     return call(
         lookup_kernel,
         (CLASSES,),
-        [pl.BlockSpec((1,) + table.shape[1:], lambda c, *_: (c, 0, 0, 0))],
+        [spec, spec],
         whole((count, D)),
         struct((count, D), bf16),
         [pltpu.VMEM((count, D), f32)],
         prefetch=2,
-        bytes_moved=2 * table.size,
-    )(keys, starts, table)
-
-
-def scatter_kernel(keys, starts, table, rows, out, s_rows, s_sum):
-    cls = pl.program_id(0)
-    piece = pl.program_id(1)
-    parts, lines, width = table.shape[1:]
-
-    @pl.when((cls == 0) & (piece == 0))
-    def _():
-        wide = rows[...].astype(f32)
-        for p in range(s_rows.shape[0]):
-            s_rows[p] = wide[:, p * WIDTH : (p + 1) * WIDTH]
-
-    for part in range(parts):
-        s_sum[:, part * width : (part + 1) * width] = table[0, part].astype(f32)
+        bytes_moved=4 * halves[0].size,
+    )(keys, edges, *halves)
+
+
+def place_kernel(spots, packed, *refs):
+    *before, gain, out, normed_o, s_packed = refs
+    cap = packed.shape[1]
+    for j in range(packed.shape[0]):
+        s_packed[j * cap : (j + 1) * cap, :] = packed[j].astype(f32)
+    s_packed[packed.shape[0] * cap :, :] = jnp.zeros((8, D), f32)
 
     def turn(i, carry):
-        key = keys[i]
-        at = key & (PAST - 1)
-        line = (key >> 11) - cls * lines
-        s_sum[pl.ds(line, 1), :] += s_rows[piece, pl.ds(at, 1), :]
+        out[pl.ds(i, 1), :] = s_packed[pl.ds(spots[i], 1), :]
         return carry
 
-    lax.fori_loop(starts[cls], starts[cls + 1], turn, 0)
-    for part in range(parts):
-        out[0, part] = s_sum[:, part * width : (part + 1) * width].astype(bf16)
-
-
-def scatter(keys, starts, table, rows):
+    lax.fori_loop(0, out.shape[0], turn, 0, unroll=8)
+    if before:
+        out[...] += before[0][...]
+    normed_o[...] = normed(out[...], gain[0:1, :])
+
+
+def place_rows(spots, packed, before, gain):
+    rows = spots.shape[0]
+    more = [] if before is None else [before]
+    return call(
+        place_kernel,
+        (1,),
+        [whole(packed.shape)] + [whole((rows, D)) for _ in more] + [whole((8, D))],
+        [whole((rows, D))] * 2,
+        [struct((rows, D)), struct((rows, D), bf16)],
+        [pltpu.VMEM((packed.shape[0] * packed.shape[1] + 8, D), f32)],
+        prefetch=1,
+        bytes_moved=4 * rows * D,
+    )(spots, packed, *more, gain)
+
+
+def send_kernel(spots, grads, out, s_packed):
+    cap = out.shape[1]
+    s_packed[...] = jnp.zeros(s_packed.shape, f32)
+
+    def turn(i, carry):
+        s_packed[pl.ds(spots[i], 1), :] += grads[pl.ds(i, 1), :]
+        return carry
+
+    lax.fori_loop(0, grads.shape[0], turn, 0, unroll=8)
+    for j in range(out.shape[0]):
+        out[j] = s_packed[j * cap : (j + 1) * cap, :].astype(bf16)
+
+
+def send_rows(spots, grads, n_tensor):
+    shape = (n_tensor, CAP, D)
+    return call(
+        send_kernel,
+        (1,),
+        [whole(grads.shape)],
+        whole(shape),
+        struct(shape, bf16),
+        [pltpu.VMEM((n_tensor * CAP + 8, D), f32)],
+        prefetch=1,
+        bytes_moved=8 * grads.size,
+    )(spots, grads)
+
+
+def pack_kernel(keys, ranks, starts, firsts, where, rows, out, s_rows, s_out):
+    own, offset = where[0], where[1]
+    cap, width = out.shape[1:]
+    parts = D // width
+    s_rows[...] = rows[...].astype(f32)
+    s_out[...] = jnp.zeros(s_out.shape, f32)
+    for cls in range(CLASSES):
+
+        def turn(i, carry, cls=cls):
+            row = s_rows[pl.ds(keys[i] & (PAST - 1), 1), :]
+            slot = ranks[i] - firsts[cls] - offset
+            slot = jnp.where((slot >= 0) & (slot < cap), slot, cap)
+            for part in range(parts):
+                piece = row[:, part * width : (part + 1) * width]
+                s_out[own ^ (cls * parts + part), pl.ds(slot, 1), :] += piece
+            return carry
+
+        lax.fori_loop(starts[2 * cls], starts[2 * cls + 2], turn, 0)
+    out[...] = s_out[:, :cap, :].astype(bf16)
+
+
+def pack_rows(keys, ranks, starts, firsts, where, rows, n_data):
     count = keys.shape[0]
-    lines, width = table.shape[2:]
-    spec = pl.BlockSpec((1, WIDTH // width, lines, width), lambda c, p, *_: (c, p, 0, 0))
+    shape = (n_data, CAP, D * CLASSES // n_data)
     return call(
-        scatter_kernel,
-        (CLASSES, D // WIDTH),
-        [spec, whole((count, D))],
-        spec,
-        struct(table.shape, bf16),
-        [pltpu.VMEM((D // WIDTH, count, WIDTH), f32), pltpu.VMEM((lines, WIDTH), f32)],
-        prefetch=2,
-        bytes_moved=4 * table.size,
-    )(keys, starts, table, rows)
-
-
-def tile_logits(table, chosen, real):
+        pack_kernel,
+        (1,),
+        [whole((count, D))],
+        whole(shape),
+        struct(shape, bf16),
+        [pltpu.VMEM((count, D), f32), pltpu.VMEM((n_data, CAP + 8, shape[2]), f32)],
+        prefetch=5,
+        bytes_moved=2 * count * D,
+    )(keys, ranks, starts, firsts, where, rows)
+
+
+def add_kernel(keys, starts, where, packed, base, out, square, s_packed):
+    cls, offset = where[0], where[1]
+    lines = base.shape[0]
+    count = keys.shape[0] // packed.shape[0]
+    cap = packed.shape[1]
+    s_packed[...] = packed[...].astype(f32)
+    out[...] = base[...].astype(f32)
+    for r in range(packed.shape[0]):
+        first = starts[8 * r + cls] + offset
+
+        def turn(i, carry):
+            line = keys[r * count + i] - cls * lines
+            out[pl.ds(line, 1), :] += s_packed[r, pl.ds(i - first, 1), :]
+            return carry
+
+        lax.fori_loop(first, jnp.minimum(starts[8 * r + cls + 1], first + cap), turn, 0)
+    square[...] = jnp.zeros(square.shape, f32)
+    for low in range(0, lines, TILE):
+        part = out[low : low + TILE, :]
+        square[0:1, :] += jnp.sum(part * part, axis=0, keepdims=True)
+
+
+def add_rows(keys, starts, where, packed, base):
+    return call(
+        add_kernel,
+        (1,),
+        [whole(packed.shape), whole(base.shape)],
+        [whole(base.shape), whole((8, base.shape[1]))],
+        [struct(base.shape), struct((8, base.shape[1]))],
+        [pltpu.VMEM(packed.shape, f32)],
+        prefetch=3,
+        bytes_moved=8 * base.size,
+    )(keys, starts, where, packed, base)
+
+
+def tile_lines(core, height):
+    return (core[0] * 2 + pl.program_id(1)) * height
+
+
+def tile_logits(core, table, chosen, real):
     parts, height, width = table.shape[1:]
     result = nt(table[0, 0], chosen[:, :width])
     for part in range(1, parts):
         result = result + nt(table[0, part], chosen[:, part * width : (part + 1) * width])
-    line = pl.program_id(1) * height + iota(result.shape, 0)
+    line = tile_lines(core, height) + iota(result.shape, 0)
     return jnp.where(line < real, result, -1e30)
 
 
-def tile_hit(table, lines, wanted):
+def tile_hit(core, table, lines, wanted):
     height = table.shape[2]
-    first = pl.program_id(0) * lines + pl.program_id(1) * height
+    first = pl.program_id(0) * lines + tile_lines(core, height)
     return first + iota((height, wanted.shape[1]), 0) == wanted[0:1, :]
 
 
-def measure_kernel(real, lines, table, chosen, wanted, out, s_stats):
-    logits = tile_logits(table, chosen, real)
-    hit = tile_hit(table, lines, wanted)
+def one_half(core, first, second):
+    return jnp.where(core[0] == 0, first[...], second[...])
+
+
+def measure_kernel(real, lines, core, first_half, second_half, chosen, wanted, out, s_stats):
+    table = one_half(core, first_half, second_half)
+    logits = tile_logits(core, table, chosen, real)
+    hit = tile_hit(core, table, lines, wanted)
     first = (pl.program_id(0) == 0) & (pl.program_id(1) == 0)
 
     @pl.when(first)
@@ -809,29 +930,41 @@
     out[...] = s_stats[...]
 
 
-def table_spec(table):
-    parts, width = table.shape[1], table.shape[3]
-    return pl.BlockSpec((1, parts, TILE, width), lambda c, i: (c, 0, i, 0))
-
-
-def vocab_measure(table, chosen, wanted, real):
+def table_specs(halves):
+    parts, width = halves[0].shape[1], halves[0].shape[3]
+
+    def spec(k):
+        def place(c, i, core):
+            mine = core[0] == k
+            return (jnp.where(mine, c, 0), 0, jnp.where(mine, i, 0), 0)
+
+        return pl.BlockSpec((1, parts, TILE, width), place)
+
+    return [spec(0), spec(1)]
+
+
+def vocab_measure(core, halves, chosen, wanted, real):
     count = chosen.shape[0]
-    lines = table.shape[2]
+    lines = 2 * halves[0].shape[2]
     return call(
         functools.partial(measure_kernel, real, lines),
-        (CLASSES, lines // TILE),
-        [table_spec(table), whole((count, D)), whole((8, count))],
+        (CLASSES, lines // TILE // 2),
+        table_specs(halves) + [whole((count, D)), whole((8, count))],
         whole((8, count)),
         struct((8, count)),
         [pltpu.VMEM((8, count), f32)],
-        flops=2 * count * table.size,
-        bytes_moved=2 * table.size,
-    )(table, chosen, wanted)
-
-
-def vocab_kernel(real, lines, table, chosen, wanted, stats, dtable, dchosen, s_sum):
-    logits = tile_logits(table, chosen, real)
-    hit = tile_hit(table, lines, wanted)
+        prefetch=1,
+        flops=2 * count * halves[0].size,
+        bytes_moved=2 * halves[0].size,
+    )(core, *halves, chosen, wanted)
+
+
+def vocab_kernel(
+    real, lines, core, first_half, second_half, chosen, wanted, stats, dtable, dchosen, s_sum
+):
+    table = one_half(core, first_half, second_half)
+    logits = tile_logits(core, table, chosen, real)
+    hit = tile_hit(core, table, lines, wanted)
     soft = jnp.exp(logits - stats[0:1, :])
     dlogits = (stats[1:2, :] * (soft - jnp.where(hit, 1.0, 0.0))).astype(bf16)
     step = pl.program_id(0) * pl.num_programs(1) + pl.program_id(1)
@@ -851,19 +984,23 @@
         dchosen[...] = s_sum[...].astype(bf16)
 
 
-def vocab_back(table, chosen, wanted, stats, real):
+def vocab_back(core, halves, chosen, wanted, stats, real):
     count = chosen.shape[0]
-    lines = table.shape[2]
+    parts, lines, width = halves[0].shape[1:]
     return call(
-        functools.partial(vocab_kernel, real, lines),
+        functools.partial(vocab_kernel, real, 2 * lines),
         (CLASSES, lines // TILE),
-        [table_spec(table), whole((count, D)), whole((8, count)), whole((8, count))],
-        [table_spec(table), whole((count, D))],
-        [struct(table.shape, bf16), struct((count, D), bf16)],
+        table_specs(halves) + [whole((count, D)), whole((8, count)), whole((8, count))],
+        [
+            pl.BlockSpec((1, parts, TILE, width), lambda c, i, core: (c, 0, i, 0)),
+            whole((count, D)),
+        ],
+        [struct(halves[0].shape, bf16), struct((count, D), bf16)],
         [pltpu.VMEM((count, D), f32)],
-        flops=6 * count * table.size,
-        bytes_moved=4 * table.size,
-    )(table, chosen, wanted, stats)
+        prefetch=1,
+        flops=6 * count * halves[0].size,
+        bytes_moved=4 * halves[0].size,
+    )(core, *halves, chosen, wanted, stats)
 
 
 def shifted(values, axis, by):
@@ -881,17 +1018,46 @@
 
 def to_earlier(values):
     return lax.ppermute(values, "core", [(1, 0)])
+
+
+def crossed(values, axis, by):
+    n = lax.axis_size(axis) if isinstance(axis, str) else axis_count(axis)
+    return lax.ppermute(values, axis, [(i, i ^ by) for i in range(n)])
+
+
+def axis_count(axes):
+    count = 1
+    for axis in axes:
+        count *= lax.axis_size(axis)
+    return count
 
 
 def everywhere(values, axes, combine=jnp.add):
     for axis in axes:
         reach = 1
         while reach < lax.axis_size(axis):
-            n = lax.axis_size(axis)
-            other = lax.ppermute(values, axis, [(i, i ^ reach) for i in range(n)])
-            values = combine(values, other)
+            if 2 * reach < lax.axis_size(axis):
+                one, two, three = (crossed(values, axis, by * reach) for by in (1, 2, 3))
+                values = combine(combine(values, one), combine(two, three))
+                reach *= 4
+            else:
+                values = combine(values, crossed(values, axis, reach))
+                reach *= 2
+    return values
+
+
+def relative(values):
+    values = values[None]
+    for axis in ("core", "chip"):
+        reach = 1
+        while reach < lax.axis_size(axis):
+            values = jnp.concatenate([values, crossed(values, axis, reach)], axis=0)
             reach *= 2
     return values
+
+
+def exchanged(blocks):
+    return jnp.stack([blocks[0]] + [crossed(blocks[r], DP, r) for r in range(1, blocks.shape[0])])
 
 
 def around(values, axis):
@@ -905,6 +1071,13 @@
     for by in range(1, n):
         result = result + shifted(blocks[by], axis, -by).astype(f32)
     return result
+
+
+def by_core(own, other, axis=0):
+    first = lax.axis_index("core") == 0
+    return jnp.concatenate(
+        [jnp.where(first, own, other), jnp.where(first, other, own)], axis=axis
+    )
 
 
 def inverse_rms(values):
@@ -958,9 +1131,8 @@
     return turn_heads(jnp.pad(part, ((0, 0), (0, 2 * STATE + LANES - width))))
 
 
-def reduce_layer(packed):
+def reduce_layer(mine):
     n_tensor = lax.axis_size("tensor")
-    mine = lax.psum_scatter(packed, DP, scatter_dimension=0, tiled=True)
     shares = [mine[:, j * SHARE : (j + 1) * SHARE] for j in range(n_tensor)]
     bcdt = turn_heads(jnp.concatenate([share[:, 3 * WIDTH :] for share in shares[:3]], axis=1))
     blocks = []
@@ -978,17 +1150,18 @@
     )
 
 
-def layer_forward(resid, gain, packed, wb, smalls):
+def layer_forward(resid, normed, next_gain, packed, wb, smalls):
     chan, headp, bcv = smalls
-    normed = (resid * inverse_rms(resid) * gain).astype(bf16)
     nx = jnp.concatenate([to_later(normed[-HALO:]), normed], axis=0)
     y, gate, xraw, st, bcdt, c, ecf = scan_front(nx, packed, wb, chan, headp, bcv)
     before = to_later(st)
-    y, scaled, inverse, out = scan_join(y, gate, c, ecf, before, chan, packed, resid)
-    return out, (resid, normed, y, gate, xraw, before, bcdt, c, ecf, scaled, inverse)
-
-
-def layer_backward(dresid, kept, gain, packed, wb, smalls):
+    y, scaled, inverse, out, following = scan_join(
+        y, gate, c, ecf, before, chan, packed, resid, next_gain
+    )
+    return out, following, (resid, normed, y, gate, xraw, before, bcdt, c, ecf, scaled, inverse)
+
+
+def layer_backward(dresid, kept, gain, packed, wb, smalls, done):
     resid, normed, y, gate, xraw, before, bcdt, c, ecf, scaled, inverse = kept
     chan, headp, bcv = smalls
     dout = dresid.astype(bf16)
@@ -997,15 +1170,41 @@
     dx, tail, halo, dchan, dbcdt, bc_halo, dheadp, dbcv = scan_back(
         xraw, dy, bcdt, before, after, chan, headp, bcv
     )
+    dx, done = lax.optimization_barrier((dx, done))
     back, bc_back = to_earlier(halo), to_earlier(bc_halo)
-    gain_rows = jnp.broadcast_to(gain[None, :], (8, D))
     grads, dresid, dnorm_gain = layer_grads(
         normed, dout, dgate, dx, tail, back, dbcdt, bc_back,
-        scaled, packed, wb, resid, dresid, gain_rows,
+        scaled, packed, wb, resid, dresid, gain,
     )
     dchan = jnp.concatenate([dchan[: CONV + 1], dgain[:1]], axis=0)
     smalls = (dnorm_gain[0], dchan, dheadp[:3, :HEADS], dbcv[: CONV + 1])
-    return dresid, reduce_layer(grads), smalls
+    return dresid, grads, smalls, done
+
+
+def flat_layer(parts, final_gain):
+    gain, chan, head, taps = parts
+    n_tensor = lax.axis_size("tensor")
+    chan = in_order(chan.reshape(CONV + 2, n_tensor, -1), 1)
+    head = in_order(head.reshape(3, n_tensor, -1), 1).reshape(3, HEADS)
+    rows = [gain.reshape(-1, LANES), chan.reshape(-1, LANES), taps.reshape(-1, LANES)]
+    rows.append(jnp.pad(head, ((0, 5), (0, LANES - HEADS))))
+    if final_gain is not None:
+        rows.append(final_gain.reshape(-1, LANES))
+    return jnp.concatenate(rows)
+
+
+def unflat_layer(flat):
+    n_tensor = lax.axis_size("tensor")
+    z = lax.axis_index("tensor")
+    one, two = D // LANES, (CONV + 2) * INNER // LANES
+    three = (CONV + 1) * 2 * STATE // LANES
+    gain = flat[:one].reshape(D)
+    chan = flat[one : one + two].reshape(CONV + 2, INNER)
+    chan = lax.dynamic_slice_in_dim(chan, z * (INNER // n_tensor), INNER // n_tensor, 1)
+    taps = flat[one + two : one + two + three].reshape(CONV + 1, 2 * STATE)
+    head = flat[one + two + three : one + two + three + 3, :HEADS]
+    head = lax.dynamic_slice_in_dim(head, z * (HEADS // n_tensor), HEADS // n_tensor, 1)
+    return (gain, chan, head, taps, flat[one + two + three + 8 :].reshape(-1))
 
 
 def lse_merge(first, second):
@@ -1030,6 +1229,56 @@
     if stacked:
         return jnp.sum(values * values, axis=tuple(range(1, values.ndim)))
     return jnp.sum(values * values)[None]
+
+
+def layer_marks(shape, axis, values):
+    result = jnp.full(shape, values[0], f32)
+    place = iota(shape, axis or 0)
+    for i in range(1, len(values)):
+        result = jnp.where(place == i, values[i], result)
+    return result
+
+
+def adapt_kernel(axes, scale, *refs):
+    count = len(axes)
+    inputs, outputs, squares = refs[: 4 * count], refs[4 * count : 7 * count], refs[-1]
+    at = 0
+    for k, axis in enumerate(axes):
+        weight, first, second, grad = (ref[...] for ref in inputs[4 * k : 4 * k + 4])
+        moved = adapt(weight, first, second, grad * scale[0])
+        for ref, value in zip(outputs[3 * k : 3 * k + 3], moved):
+            ref[...] = value
+        square = moved[2] * moved[2]
+        if axis is None:
+            squares[at] = jnp.sum(square)
+            at += 1
+        else:
+            for i in range(LAYERS):
+                squares[at] = jnp.sum(jnp.where(iota(square.shape, axis) == i, square, 0.0))
+                at += 1
+
+
+def step_kernel(axes, factors, *refs):
+    count = len(axes)
+    weights, changes, outputs = refs[:count], refs[count : 2 * count], refs[2 * count :]
+    at = 0
+    for k, axis in enumerate(axes):
+        values = [factors[at + i] for i in range(1 if axis is None else LAYERS)]
+        at += len(values)
+        marks = layer_marks(weights[k].shape, axis, values)
+        outputs[k][...] = weights[k][...] - marks * changes[k][...]
+
+
+def at_once(kernel, scalars, arrays, shapes, extra):
+    smem = pl.BlockSpec(memory_space=pltpu.SMEM)
+    vmem = pl.BlockSpec(memory_space=pltpu.VMEM)
+    return pl.pallas_call(
+        kernel,
+        in_specs=[smem] + [vmem] * len(arrays),
+        out_specs=[vmem] * len(shapes) + [smem] * len(extra),
+        out_shape=[struct(shape) for shape in shapes + extra],
+        compiler_params=pltpu.CompilerParams(vmem_limit_bytes=VMEM_BYTES),
+    )(scalars, *arrays)
 
 
 def body(
@@ -1072,7 +1321,10 @@
     length = meta[:, seq + 2 * scored :]
     live = core * rows + jnp.arange(rows)[None, :] < length
     positions = lax.dynamic_slice_in_dim(meta, seq + core * half, half, 1)
-    wanted = lax.dynamic_slice_in_dim(meta, seq + scored + core * half, half, 1)
+    all_positions = meta[:, seq : seq + scored].reshape(n_tensor, 2, half).transpose(1, 0, 2)
+    counted = (all_positions < length[None]).astype(f32).reshape(-1)
+    all_wanted = meta[:, seq + scored : seq + 2 * scored].reshape(n_tensor, 2, half)
+    all_wanted = all_wanted.transpose(1, 0, 2).reshape(1, -1)
     own_positions = meta[0, seq : seq + scored]
 
     def place(indices):
@@ -1081,17 +1333,51 @@
 
     key, inside = place(ids)
     count = n_tensor * rows
-    key = jnp.where(inside & live, key, CLASSES * padded).reshape(count)
-    key = key * PAST + jnp.arange(count)
+    order = jnp.arange(rows)
+    same = (ids[:, :, None] == ids[:, None, :]) & live[:, None, :]
+    opening = jnp.min(jnp.where(same, order[None, None, :], rows), axis=2)
+    fresh = live & (opening == order[None, :])
+    hits = fresh & inside
+    before = order[None, None, :] < opening[:, :, None]
+    slots = jnp.sum((hits[:, None, :] & before).astype(jnp.int32), axis=2)
+    fullest = jnp.max(jnp.sum(hits.astype(jnp.int32), axis=1))
+    key = key * PAST + jnp.arange(n_tensor)[:, None] * rows + slots
+    past = CLASSES * padded * PAST + jnp.arange(count)
+    key = jnp.where(hits.reshape(count), key.reshape(count), past)
+    owner = (ids[0] // vocab - z) % n_tensor
+    alike = (owner[:, None] == owner[None, :]) & fresh[0][None, :] & before[0]
+    spots = owner * rows + jnp.sum(alike.astype(jnp.int32), axis=1)
+
+    def spots_at(offset):
+        slot = spots % rows - offset
+        here = live[0] & (slot >= 0) & (slot < CAP)
+        return jnp.where(here, spots // rows * CAP + slot, n_tensor * CAP)
+
+    every = jnp.arange(count)
     rank = jnp.sum((key[None, :] < key[:, None]).astype(jnp.int32), axis=1)
-    keys = jnp.sum(jnp.where(rank[None, :] == jnp.arange(count)[:, None], key[None, :], 0), axis=1)
-    edges = jnp.arange(8) * (padded * PAST)
+    keys = jnp.sum(jnp.where(rank[None, :] == every[:, None], key[None, :], 0), axis=1)
+    edges = jnp.arange(16) * (padded // 2 * PAST)
     starts = jnp.sum((key[None, :] < edges[:, None]).astype(jnp.int32), axis=1)
+    line = keys >> 11
+    new = (every < starts[2 * CLASSES]) & (line != jnp.pad(line, (1, 0), constant_values=-1)[:-1])
+    ranks = jnp.sum((new[None, :] & (every[None, :] <= every[:, None])).astype(jnp.int32), axis=1)
+    ranks = ranks - 1
+    opens = new[None, :] & (ranks[None, :] == every[:, None])
+    distinct = jnp.sum(jnp.where(opens, line[None, :], 0), axis=1)
+    bounds = starts[0 : 2 * CLASSES + 1 : 2]
+    firsts = jnp.sum((new[None, :] & (every[None, :] < bounds[:, None])).astype(jnp.int32), axis=1)
+    firsts = jnp.pad(firsts, (0, 8 - firsts.shape[0]))
+
+    shared = relative(jnp.concatenate([distinct, firsts]))
+    all_lines, all_firsts = shared[:, :count].reshape(-1), shared[:, count:].reshape(-1)
+    most = jnp.max(firsts[1 : CLASSES + 1] - firsts[:CLASSES])
+    most = jnp.pad(jnp.stack([most, fullest]), (0, LANES - 2))
+    most = everywhere(most, ("core", "tensor", "chip"), jnp.maximum)
+    most, fullest = most[0], most[1]
 
     low = jnp.pad(embed.astype(bf16), ((0, padded - lines), (0, 0)))
-    table = lax.all_gather(low, DP).reshape(CLASSES, n_data // CLASSES, padded, -1)
+    halves = [lax.all_gather(low[: padded // 2], DP)]
     shares = [pack_layer(w_zx[i], w_bcdt[i], w_out[i]) for i in range(LAYERS)]
-    packed = [lax.all_gather(share, DP) for share in shares]
     inner = INNER // n_tensor
     heads = HEADS // n_tensor
     small = jnp.concatenate([channel, jnp.pad(per_head, ((0, 0), (0, 0), (0, inner - heads)))], 1)
@@ -1109,126 +1395,206 @@
             )
         )
 
-    found = lookup(keys, starts, table)
-    resid = sum_back(found.reshape(n_tensor, rows, D), "tensor")
+    ready = (shares[0], smalls, keys, starts, spots_at(0), ranks, all_lines, all_firsts, most, fullest)
+    second, ready = lax.optimization_barrier((low[padded // 2 :], ready))
+    share, smalls, keys, starts, spots_first, ranks, all_lines, all_firsts, most, fullest = ready
+    halves.append(lax.all_gather(second, DP))
+    share, _ = lax.optimization_barrier((share, halves))
+    packed = [lax.all_gather(share, DP)]
+    halves = [half.reshape(CLASSES, n_data // CLASSES, padded // 2, -1) for half in halves]
+    found = lookup(keys, starts, halves)
+    found = found.reshape(n_tensor, rows, D)
+    gain_rows = [jnp.broadcast_to(gains[i][None, :], (8, D)) for i in range(LAYERS + 1)]
+
+    def rows_in(offset, before):
+        part = found[:, offset : offset + CAP]
+        part = [part[0]] + [shifted(part[by], "tensor", -by) for by in range(1, n_tensor)]
+        return place_rows(
+            spots_at(offset) if offset else spots_first, jnp.stack(part), before, gain_rows[0]
+        )
+
+    resid, normed = rows_in(0, None)
+    for offset in range(CAP, rows, CAP):
+        resid, normed = lax.cond(
+            fullest > offset,
+            lambda so_far, offset=offset: tuple(rows_in(offset, so_far[0])),
+            lambda so_far: so_far,
+            (resid, normed),
+        )
+    for share in shares[1:]:
+        share = lax.optimization_barrier((share, packed[-1], resid))[0]
+        packed.append(lax.all_gather(share, DP))
     w_small = [unpack_bcdt(packed[depth]) for depth in range(LAYERS)]
     kept = []
     for depth in range(LAYERS):
-        resid, saved = layer_forward(
-            resid, gains[depth], packed[depth], w_small[depth], smalls[depth]
+        resid, normed, saved = layer_forward(
+            resid, normed, gain_rows[depth + 1], packed[depth], w_small[depth], smalls[depth]
         )
         kept.append(saved)
 
-    final = (resid * inverse_rms(resid) * gains[LAYERS]).astype(bf16)
-    other = swapped(final)
-    both = jnp.concatenate(
-        [jnp.where(core == 0, final, other), jnp.where(core == 0, other, final)], axis=0
-    )
+    both = by_core(normed, swapped(normed))
     pick = (positions[0][:, None] == jnp.arange(seq)[None, :]).astype(bf16)
     chosen = around(nn(pick, both).astype(bf16), "tensor").reshape(n_tensor * half, D)
-    want, known = place(wanted)
-    want = jnp.where(known, want, -1).reshape(1, -1)
-    want = jnp.broadcast_to(want, (8, n_tensor * half))
-    stats = vocab_measure(table, chosen, want, lines)[:3]
-    stats = stats.reshape(3, n_tensor, half)
-
-    ordered = everywhere(in_order(stats, 1), ("tensor",), lse_merge)
-    stats = in_order(ordered, 1).reshape(3, -1)
+    chosen = by_core(chosen, swapped(chosen))
+    want, known = place(all_wanted)
+    want = jnp.broadcast_to(jnp.where(known, want, -1), (8, n_tensor * scored))
+    which = core[None]
+    stats = vocab_measure(which, halves, chosen, want, lines)[:3]
+    ordered = in_order(stats.reshape(3, 2, n_tensor, half), 2)
+    ordered = everywhere(ordered, ("core", "tensor"), lse_merge)
+    stats = in_order(ordered, 2).reshape(3, -1)
     log_total = stats[0] + jnp.log(stats[1])
-    counted = (positions < length).astype(f32).reshape(-1)
-    losses = (counted * (log_total - stats[2])).reshape(n_tensor, half).sum(axis=1)
-    loss_sum = jnp.sum(in_order(losses, 0))
+    losses = (counted * (log_total - stats[2])).reshape(2, n_tensor, half).sum(axis=2)
+    loss_sum = jnp.sum(in_order(losses, 1))
     loss_count = jnp.sum(counted)
     info = jnp.pad(jnp.stack([log_total, counted]), ((0, 6), (0, 0)))
-    dtable, dchosen = vocab_back(table, chosen, want, info, lines)
-    dpicked = sum_back(dchosen.reshape(n_tensor, half, D), "tensor").astype(bf16)
-    other = swapped(dpicked)
-    dpicked = jnp.concatenate(
-        [jnp.where(core == 0, dpicked, other), jnp.where(core == 0, other, dpicked)], axis=0
-    )
-    spots = (core * rows + jnp.arange(rows)[:, None] == own_positions[None, :]).astype(bf16)
-    dresid, dfinal_gain = rms_back(nn(spots, dpicked), resid, gains[LAYERS])
-
-    grads = [None] * LAYERS
-    small_grads = [None] * LAYERS
+    dtable, dchosen = vocab_back(which, halves, chosen, want, info, lines)
+    dtable = dtable.reshape((-1, 2) + dtable.shape[2:])
+    table_part = lax.psum_scatter(dtable, "chip", scatter_dimension=0)
+
+    dchosen = dchosen.reshape(2, n_tensor * half, D)
+    mine = jnp.where(core == 0, dchosen[0], dchosen[1])
+    other = jnp.where(core == 0, dchosen[1], dchosen[0])
+    dchosen = mine.astype(f32) + swapped(other).astype(f32)
+    dpicked = sum_back(dchosen.astype(bf16).reshape(n_tensor, half, D), "tensor").astype(bf16)
+    dpicked = by_core(dpicked, swapped(dpicked))
+    onto = (core * rows + jnp.arange(rows)[:, None] == own_positions[None, :]).astype(bf16)
+    dresid, dfinal_gain = rms_back(nn(onto, dpicked), resid, gains[LAYERS])
+
+    shares = [None] * LAYERS
+    parts = [None] * LAYERS
+    flats = []
     for depth in reversed(range(LAYERS)):
-        dresid, grads[depth], small_grads[depth] = layer_backward(
-            dresid, kept[depth], gains[depth], packed[depth], w_small[depth], smalls[depth]
+        dresid, grad, parts[depth], flats = layer_backward(
+            dresid, kept[depth], gain_rows[depth], packed[depth], w_small[depth], smalls[depth],
+            flats,
         )
-
-    arrived = around(dresid.astype(bf16), "tensor").reshape(count, D)
-    dtable = scatter(keys, starts, dtable, arrived)
-    dtable = dtable.reshape(n_data, padded, -1)
-    grad_table = lax.psum_scatter(dtable, DP, scatter_dimension=0)[:lines].astype(f32)
-
+        grad, table_part, dresid = lax.optimization_barrier((grad, table_part, dresid))
+        shares[depth] = lax.psum_scatter(grad, DP, scatter_dimension=0, tiled=True)
+        if depth > 0:
+            flat = flat_layer(parts[depth], dfinal_gain if depth == LAYERS - 1 else None)
+            flats = [everywhere(flat, ("core", "tensor", "chip"))] + flats
+
+    def rows_out(part):
+        return jnp.stack(
+            [part[0]] + [shifted(part[by], "tensor", by) for by in range(1, n_tensor)]
+        )
+
+    sent = send_rows(spots_first, dresid, n_tensor)
+    sent, table_part = lax.optimization_barrier((sent, table_part))
+    arrived = jnp.pad(rows_out(sent), ((0, 0), (0, rows - CAP), (0, 0)))
+    for offset in range(CAP, rows, CAP):
+        arrived = lax.cond(
+            fullest > offset,
+            lambda so_far, offset=offset: lax.dynamic_update_slice(
+                so_far,
+                rows_out(send_rows(spots_at(offset), dresid, n_tensor)),
+                (0, offset, 0),
+            ),
+            lambda so_far: so_far,
+            arrived,
+        )
+    arrived = arrived.reshape(count, D)
+    keep = jnp.where(core == 0, table_part[0], table_part[1])
+    give = jnp.where(core == 0, table_part[1], table_part[0])
+    table_part = by_core(keep, swapped(give))
+    own = lax.axis_index(DP)
+    cls = own // (n_data // CLASSES)
+
+    def pack_round(offset):
+        where = jnp.stack([own, offset])
+        return pack_rows(keys, ranks, starts, firsts, where, arrived, n_data)
+
+    def add_round(offset, recv, total):
+        return tuple(add_rows(all_lines, all_firsts, jnp.stack([cls, offset]), recv, total))
+
+    stacked = (False, True, True, True, True, True, True, False)
+    everyone = n_tensor * n_data
+    copies = (1, 1, n_tensor, 1, n_data, n_data, everyone, everyone)
+    weights = (embed, w_zx, w_bcdt, w_out, channel, per_head, bc_conv, gains)
+    outgoing, shares[1:], parts[0], late = lax.optimization_barrier(
+        (pack_round(0), shares[1:], parts[0], weights)
+    )
+    recv = exchanged(outgoing)
+    grads = [None] + [reduce_layer(share) for share in shares[1:]]
+    flats = [everywhere(flat_layer(parts[0], None), ("core", "tensor", "chip"))] + flats
+    weight_sq = jnp.concatenate(
+        [group_squares(*pair) / shared_by for *pair, shared_by in zip(late, stacked, copies)]
+    )
+    recv, table_part, grads[1:], flats[0], weight_sq = lax.optimization_barrier(
+        (recv, table_part, grads[1:], flats[0], weight_sq)
+    )
+    added = add_round(0, recv, table_part)
+    added = lax.while_loop(
+        lambda carry: carry[0] < most,
+        lambda carry: (carry[0] + CAP, add_round(carry[0], exchanged(pack_round(carry[0])), carry[1][0])),
+        (jnp.int32(CAP), added),
+    )[1]
+    grad_table, table_sq = added[0][:lines], jnp.sum(added[1])
+
+    grads[0] = reduce_layer(shares[0])
     grad_zx, grad_out, grad_bcdt = (jnp.stack(parts) for parts in zip(*grads))
-    grad_gains = jnp.stack([small_grads[depth][0] for depth in range(LAYERS)] + [dfinal_gain])
-    grad_channel = jnp.stack([part[1] for part in small_grads])
-    grad_channel = in_order(grad_channel.reshape(LAYERS, CONV + 2, n_tensor, inner), 2)
-    grad_channel = grad_channel.reshape(LAYERS, CONV + 2, INNER)
-    grad_head = jnp.stack([part[2] for part in small_grads])
-    grad_head = in_order(grad_head.reshape(LAYERS, 3, n_tensor, heads), 2)
-    grad_bc_conv = jnp.stack([part[3] for part in small_grads])
-    flat = jnp.concatenate(
-        [
-            grad_gains.reshape(-1, LANES),
-            grad_channel.reshape(-1, LANES),
-            grad_bc_conv.reshape(-1, LANES),
-            jnp.pad(grad_head.reshape(LAYERS * 3, HEADS), ((0, 0), (0, LANES - HEADS))),
-        ]
-    )
-    flat = everywhere(flat, ("core", "tensor", "chip"))
-    sizes = [grad.size // LANES for grad in (grad_gains, grad_channel, grad_bc_conv)]
-    edges = [sizes[0], sizes[0] + sizes[1], sum(sizes)]
-    grad_gains = flat[: edges[0]].reshape(grad_gains.shape)
-    grad_channel = flat[edges[0] : edges[1]].reshape(grad_channel.shape)
-    grad_bc_conv = flat[edges[1] : edges[2]].reshape(grad_bc_conv.shape)
-    grad_head = flat[edges[2] :, :HEADS].reshape(LAYERS, 3, HEADS)
-    grad_channel = lax.dynamic_slice_in_dim(grad_channel, z * inner, inner, 2)
-    grad_head = lax.dynamic_slice_in_dim(grad_head, z * heads, heads, 2)
-
-    everyone = n_tensor * n_data
+    small_grads = [unflat_layer(flat) for flat in flats]
+    grad_gains = jnp.stack([part[0] for part in small_grads] + [small_grads[-1][4]])
+    grad_channel, grad_head, grad_bc_conv = (
+        jnp.stack([part[k] for part in small_grads]) for k in (1, 2, 3)
+    )
+
     kinds = (
-        (embed, embed_m, embed_v, grad_table, False, 1),
-        (w_zx, w_zx_m, w_zx_v, grad_zx, True, 1),
-        (w_bcdt, w_bcdt_m, w_bcdt_v, grad_bcdt, True, n_tensor),
-        (w_out, w_out_m, w_out_v, grad_out, True, 1),
-        (channel, channel_m, channel_v, grad_channel, True, n_data),
-        (per_head, per_head_m, per_head_v, grad_head, True, n_data),
-        (bc_conv, bc_conv_m, bc_conv_v, grad_bc_conv, True, everyone),
-        (gains, gains_m, gains_v, grad_gains, False, everyone),
-    )
-    grad_sq = jnp.concatenate([group_squares(kind[3], kind[4]) / kind[5] for kind in kinds])
-    weight_sq = jnp.concatenate([group_squares(kind[0], kind[4]) / kind[5] for kind in kinds])
+        (embed, embed_m, embed_v, grad_table),
+        (w_zx, w_zx_m, w_zx_v, grad_zx),
+        (w_bcdt, w_bcdt_m, w_bcdt_v, grad_bcdt),
+        (w_out, w_out_m, w_out_v, grad_out),
+        (channel, channel_m, channel_v, grad_channel),
+        (per_head, per_head_m, per_head_v, grad_head),
+        (bc_conv, bc_conv_m, bc_conv_v, grad_bc_conv),
+        (gains, gains_m, gains_v, grad_gains),
+    )
+    kinds = [kind + pair for kind, pair in zip(kinds, zip(stacked, copies))]
+    grad_sq = jnp.concatenate(
+        [table_sq[None]] + [group_squares(kind[3], kind[4]) / kind[5] for kind in kinds[1:]]
+    )
     groups = grad_sq.shape[0]
     totals = jnp.concatenate(
-        [grad_sq, weight_sq, jnp.stack([loss_sum, loss_count]) / n_tensor]
+        [grad_sq, weight_sq, jnp.stack([loss_sum, loss_count]) / (2 * n_tensor)]
     )
     totals = everywhere(jnp.pad(totals, (0, LANES - totals.shape[0])), ("core", "tensor", "chip"))
     grad_sq, weight_sq = totals[:groups], totals[groups : 2 * groups]
     grad_norm = jnp.sqrt(jnp.sum(grad_sq))
     scale = jnp.minimum(1.0, clip_limit / grad_norm)
-    moved = [adapt(kind[0], kind[1], kind[2], kind[3] * scale) for kind in kinds]
+    rest = kinds[1:]
+    sizes = [LAYERS if kind[4] else 1 for kind in rest]
+    shares = [1.0 / kind[5] for kind, size in zip(rest, sizes) for _ in range(size)]
+    turns = [(0, 1, 2, 3), (0, 2, 1), (0, 1, 2), (1, 0, 2), (1, 0, 2), (1, 0, 2), (0, 1)]
+    axes = [0, 0, 0, 1, 1, 1, None]
+    arrays = [array.transpose(turn) for kind, turn in zip(rest, turns) for array in kind[:4]]
+    shapes = [arrays[4 * k].shape for k in range(len(rest))]
+    *moved, squares = at_once(
+        functools.partial(adapt_kernel, axes),
+        scale[None],
+        arrays,
+        [shape for shape in shapes for _ in range(3)],
+        [(groups - 1,)],
+    )
+    embed_moved = adapt(embed, embed_m, embed_v, grad_table * scale)
     step_sq = jnp.concatenate(
-        [group_squares(change[2], kind[4]) / kind[5] for change, kind in zip(moved, kinds)]
+        [group_squares(embed_moved[2], False), squares * jnp.array(shares, f32)]
     )
     step_sq = everywhere(jnp.pad(step_sq, (0, LANES - groups)), ("core", "tensor", "chip"))[:groups]
     weight_norm = jnp.sqrt(weight_sq)
     step_norm = jnp.sqrt(step_sq)
-    trust_all = weight_norm / step_norm
-    results = []
-    offset = 0
-    for kind, change in zip(kinds, moved):
-        weight = kind[0]
-        if kind[4]:
-            factor = trust_all[offset : offset + weight.shape[0]].reshape(
-                (weight.shape[0],) + (1,) * (weight.ndim - 1)
-            )
-            offset = offset + weight.shape[0]
-        else:
-            factor = trust_all[offset]
-            offset = offset + 1
-        results += [weight - learn_rate * factor * change[2], change[0], change[1]]
+    factors = learn_rate * (weight_norm / step_norm)
+    stepped = at_once(
+        functools.partial(step_kernel, axes),
+        factors[1:],
+        arrays[0::4] + moved[2::3],
+        shapes,
+        [],
+    )
+    results = [embed - factors[0] * embed_moved[2], embed_moved[0], embed_moved[1]]
+    for k, turn in enumerate(turns):
+        parts = (stepped[k], moved[3 * k], moved[3 * k + 1])
+        results += [part.transpose(turn) for part in parts]
     group_norms = jnp.stack([weight_norm, step_norm])
     return (totals[2 * groups], totals[2 * groups + 1], grad_norm, group_norms, *results)
 

time: 1160 us -> 1010 us (0.87)
  waiting for transfers between devices: 432 us -> 328 us
  Pallas kernels: 391 us -> 369 us
  local copies, waits for them, and re-layouts: 79.2 us -> 60.4 us
    ppermute x27, waiting for transfers between devices: 250 us -> 169 us  [shifted(): return lax.ppermute(values, axis, [(i, (i + by) % n) for i in range(n)])]
    reduce_scatter x3 -> x2, waiting for transfers between devices: 33.9 us -> 0.02 us  [body(): shares[depth] = lax.psum_scatter(grad, DP, scatter_dimension=0, tiled=True)]
    pallas_call x2, Pallas kernels: 99.6 us -> 79.1 us  [scan_back(): call(back_kernel, (GROUPS,), [columns(ext), columns(rows), whole((ext, 38...]
    unnamed x199 -> x179, local copies, waits for them, and re-layouts: 27.7 us -> 8.11 us
    reduce_sum x18 -> x7, other arithmetic: 18.2 us -> 2.86 us  [group_squares(): return jnp.sum(values * values, axis=tuple(range(1, values.ndim)))]
    ppermute x17 -> x49, waiting for transfers between devices: 29.7 us -> 44 us  [crossed(): return lax.ppermute(values, axis, [(i, i ^ by) for i in range(n)])]
    pallas_call x3 -> x8, Pallas kernels: 101 us -> 109 us  [the longest x1 57.2 us: vocab_back(): call(functools.partial(vocab_kernel, real, 2 * lines), (CLASSES, lines //...]
    ppermute x17 -> x49, starting transfers between devices: 50.6 us -> 57.9 us  [crossed(): return lax.ppermute(values, axis, [(i, i ^ by) for i in range(n)])]
  transfers between devices with their start and end apart: 63 -> 99, of which waited for: 40 -> 62; matrix products, arithmetic and copies ran while one was open for 7% -> 11% of each run, Pallas kernels for 14% -> 24%
where the time goes in v2:
time: 1010 us; the launch traced here: 1000 us
  Pallas kernels  369 us (37%)
  waiting for transfers between devices  328 us (32%)
  starting transfers between devices  117 us (12%)
  other arithmetic  104 us (10%)
  local copies, waits for them, and re-layouts  60.4 us (6%)
  between operations  24.4 us (2%)
    ppermute x27, waiting for transfers between devices, shifted(): return lax.ppermute(values, axis, [(i, (i + by) % n) for i in range(n)])  169 us
    pallas_call x2, Pallas kernels, scan_back(): call(back_kernel, (GROUPS,), [columns(ext), columns(rows), whole((ext, 38...  79.1 us
    ppermute x49, starting transfers between devices, crossed(): return lax.ppermute(values, axis, [(i, i ^ by) for i in range(n)])  57.9 us
    pallas_call x1, Pallas kernels, vocab_back(): call(functools.partial(vocab_kernel, real, 2 * lines), (CLASSES, lines //...  57.2 us
    pallas_call x2, Pallas kernels, scan_front(): call(scan_kernel, (GROUPS,), [whole((ext, D)), packed_zx(packed), whole(w...  45.5 us
    ppermute x49, waiting for transfers between devices, crossed(): return lax.ppermute(values, axis, [(i, i ^ by) for i in range(n)])  44 us
    pallas_call x2, Pallas kernels, layer_grads(): call(grads_kernel, (GROUPS,), [whole((rows, D)), whole((rows, D)), column...  43.3 us
    ppermute x27, starting transfers between devices, shifted(): return lax.ppermute(values, axis, [(i, (i + by) % n) for i in range(n)])  38.3 us
  transfers between devices with their start and end apart: 99, of which 62 were waited for; matrix products, arithmetic and copies ran while one was open for 11% of the time, Pallas kernels for 24%

profile of v2, /device:TPU:0, one launch (start us, length us, event | category | flops | bytes accessed | tf_op | source)
XLA Modules:
  0.0 1004.8 jit_solution(5520395139848646977)
XLA Ops:
  13.3 3.7 collective-permute-start.29
  33.5 3.5 select_reduce_fusion
  64.5 23.4 %collective-permute-done.26 = bf16[192,1024]{1,0:T(8,128)(2,1)S(1)} collective-permute-done((bf16[192,1024]{1,0:T(8,128)(2,1)S(1)}, bf16[192,1024]{1,0:T(8,128)(2,1)S(1)}, u32[]{:S(2)}, u32[]{:S(2)}) %collective-permute-start.26) | collective-permute-done | bytes 393248 | tf_op jit(solution)/shard_map/ppermute | solution.py:1008
  95.3 5.3 collective-permute-done.50
  100.6 26.4 %collective-permute-done.49 = bf16[192,1024]{1,0:T(8,128)(2,1)S(1)} collective-permute-done((bf16[192,1024]{1,0:T(8,128)(2,1)S(1)}, bf16[192,1024]{1,0:T(8,128)(2,1)S(1)}, u32[]{:S(2)}, u32[]{:S(2)}) %collective-permute-start.49) | collective-permute-done | bytes 393248 | tf_op jit(solution)/shard_map/ppermute | solution.py:1008
  129.2 38.2 %all-gather.11.cloned.1.call-done = bf16[12800,512]{1,0:T(8,128)(2,1)} async-done(((bf16[1600,512]{1,0:T(8,128)(2,1)}), bf16[12800,512]{1,0:T(8,128)(2,1)}) %all-gather.11.cloned.1.call-update) | async-done | bytes 13107216 | tf_op jit(solution)/shard_map/all_gather | solution.py:1401
  167.4 12.6 %shard_map.492 = bf16[2048,1024]{1,0:T(8,128)(2,1)S(1)} custom-call(s32[2048]{0:T(1024)S(1)} %select_reduce_fusion.1.keys, s32[16]{0:T(128)S(1)} %convert_reduce_fusion.4.edges.starts, bf16[4,2,1600,512]{3,2,1,0:T(8,128)(2,1)} %bitcast.411, bf16[4,2,1600,512]{3,2,1,0:T(8,128)(2,1)} %bitcast.414), custom_call_target="tpu_custom_call" | custom-call | bytes 26214400 | tf_op jit(solution)/shard_map/pallas_call | solution.py:748
  189.9 4.2 collective-permute-done.44
  194.2 7.9 collective-permute-done.43
  203.1 4.3 shard_map.493
  207.5 37.9 %all-gather.13.cloned.1.call-done = bf16[6528,1024]{1,0:T(8,128)(2,1)} async-done(((bf16[816,1024]{1,0:T(8,128)(2,1)}), bf16[6528,1024]{1,0:T(8,128)(2,1)}) %all-gather.13.cloned.1.call-update) | async-done | bytes 13369360 | tf_op jit(solution)/shard_map/all_gather | solution.py:1403
  255.9 23.0 %shard_map.494 = (f32[512,2048]{1,0:T(8,128)}, f32[512,2048]{1,0:T(8,128)}, f32[528,2048]{1,0:T(8,128)}, f32[128,2048]{1,0:T(8,128)}, f32[528,384]{1,0:T(8,128)}...) custom-call(bf16[528,1024]{1,0:T(8,128)(2,1)} %pad_maximum_fusion.9.nx, bf16[8,816,1024]{2,1,0:T(8,128)(2,1)} %bitcast.398, ...), custom_call_target="tpu_custom_call" | custom-call | flops 4429185024 | bytes 20971520 | tf_op jit(solution)/shard_map/pallas_call | solution.py:252
  284.6 13.8 %shard_map.495 = (f32[512,2048]{1,0:T(8,128)}, bf16[512,2048]{1,0:T(8,128)(2,1)}, f32[512,128]{1,0:T(8,128)}, f32[512,1024]{1,0:T(8,128)}, bf16[512,1024]{1,0:T(8,128)(2,1)}) custom-call(f32[512,2048]{1,0:T(8,128)} %get-tuple-element.366.y, f32[512,2048]{1,0:T(8,128)} %get-tuple-element.367.gate, bf16[512,128]{1,0:T(8,128)(2,1)} %get-tuple-element.368.c, ...), custom_call_target="tpu_custom_call" | custom-call | flops 2147483648 | bytes 18874368 | tf_op jit(solution)/shard_map/pallas_call | solution.py:325
  304.5 18.1 %all-gather.15.cloned.1.call-done = bf16[6528,1024]{1,0:T(8,128)(2,1)} async-done(((bf16[816,1024]{1,0:T(8,128)(2,1)}), bf16[6528,1024]{1,0:T(8,128)(2,1)}) %all-gather.15.cloned.1.call-update) | async-done | bytes 13369360 | tf_op jit(solution)/shard_map/all_gather | solution.py:1426
  325.7 22.5 %shard_map.496 = (f32[512,2048]{1,0:T(8,128)}, f32[512,2048]{1,0:T(8,128)}, f32[528,2048]{1,0:T(8,128)}, f32[128,2048]{1,0:T(8,128)}, f32[528,384]{1,0:T(8,128)}...) custom-call(bf16[528,1024]{1,0:T(8,128)(2,1)} %pad_maximum_fusion.10.nx, bf16[8,816,1024]{2,1,0:T(8,128)(2,1)} %bitcast.403, ...), custom_call_target="tpu_custom_call" | custom-call | flops 4429185024 | bytes 20971520 | tf_op jit(solution)/shard_map/pallas_call | solution.py:252
  353.9 14.4 %shard_map.497 = (f32[512,2048]{1,0:T(8,128)}, bf16[512,2048]{1,0:T(8,128)(2,1)}, f32[512,128]{1,0:T(8,128)}, f32[512,1024]{1,0:T(8,128)}, bf16[512,1024]{1,0:T(8,128)(2,1)}) custom-call(f32[512,2048]{1,0:T(8,128)} %get-tuple-element.377.y, f32[512,2048]{1,0:T(8,128)} %get-tuple-element.378.gate, bf16[512,128]{1,0:T(8,128)(2,1)} %get-tuple-element.379.c, ...), custom_call_target="tpu_custom_call" | custom-call | flops 2147483648 | bytes 18874368 | tf_op jit(solution)/shard_map/pallas_call | solution.py:325
  373.0 3.4 collective-permute-start.55
  377.7 5.4 collective-permute-done.55
  383.2 16.3 %collective-permute-done.54 = bf16[128,1024]{1,0:T(8,128)(2,1)S(1)} collective-permute-done((bf16[128,1024]{1,0:T(8,128)(2,1)S(1)}, bf16[128,1024]{1,0:T(8,128)(2,1)S(1)}, u32[]{:S(2)}, u32[]{:S(2)}) %collective-permute-start.54) | collective-permute-done | bytes 262176 | tf_op jit(solution)/shard_map/ppermute | solution.py:1008
  404.7 27.8 %shard_map.498 = f32[8,1024]{1,0:T(8,128)} custom-call(s32[1]{0:T(128)} %bitcast.128.core, bf16[4,2,1600,512]{3,2,1,0:T(8,128)(2,1)} %bitcast.412, bf16[4,2,1600,512]{3,2,1,0:T(8,128)(2,1)} %bitcast.415, bf16[1024,1024]{1,0:T(8,128)(2,1)} %pad_maximum_fusion.4.chosen, s32[8,1024]{1,0:T(8,128)} %broadcast_in_dim.136.wanted), custom_call_target="tpu_custom_call" | custom-call | flops 13421772800 | bytes 13107200 | tf_op jit(solution)/shard_map/pallas_call | solution.py:949
  442.6 57.2 %shard_map.499 = (bf16[4,2,1600,512]{3,2,1,0:T(8,128)(2,1)}, bf16[1024,1024]{1,0:T(8,128)(2,1)}) custom-call(s32[1]{0:T(128)} %bitcast.128.core, bf16[4,2,1600,512]{3,2,1,0:T(8,128)(2,1)} %bitcast.413, bf16[4,2,1600,512]{3,2,1,0:T(8,128)(2,1)} %bitcast.416, bf16[1024,1024]{1,0:T(8,128)(2,1)} %pad_maximum_fusion.4.chosen, ...), custom_call_target="tpu_custom_call" | custom-call | flops 40265318400 | bytes 26214400 | tf_op jit(solution)/shard_map/pallas_call | solution.py:990
  510.4 5.4 collective-permute-done.62
  515.9 6.2 collective-permute-done.64
  522.1 10.4 %collective-permute-done.63 = bf16[128,1024]{1,0:T(8,128)(2,1)} collective-permute-done((bf16[128,1024]{1,0:T(8,128)(2,1)}, bf16[128,1024]{1,0:T(8,128)(2,1)}, u32[]{:S(2)}, u32[]{:S(2)}) %collective-permute-start.63) | collective-permute-done | bytes 262176 | tf_op jit(solution)/shard_map/ppermute | solution.py:1008
  538.6 17.2 %shard_map.500 = (f32[512,2048]{1,0:T(8,128)}, bf16[512,2048]{1,0:T(8,128)(2,1)}, f32[8,2048]{1,0:T(8,128)}, f32[128,2048]{1,0:T(8,128)}) custom-call(bf16[512,1024]{1,0:T(8,128)(2,1)} %get-tuple-element.533.dout, bf16[8,816,1024]{2,1,0:T(8,128)(2,1)} %bitcast.405, f32[512,2048]{1,0:T(8,128)} %get-tuple-element.386.y, f32[512,2048]{1,0:T(8,128)} %get-tuple-element.378.gate, ...), custom_call_target="tpu_custom_call" | custom-call | flops 2147483648 | bytes 27262976 | tf_op jit(solution)/shard_map/pallas_call | solution.py:404
  561.6 39.5 %shard_map.501 = (bf16[512,2048]{1,0:T(8,128)(2,1)}, f32[16,2048]{1,0:T(8,128)}, f32[16,2048]{1,0:T(8,128)}, f32[8,2048]{1,0:T(8,128)}, f32[512,384]{1,0:T(8,128...) custom-call(f32[528,2048]{1,0:T(8,128)} %get-tuple-element.389.xraw, ...), custom_call_target="tpu_custom_call" | custom-call | flops 2684354560 | bytes 12582912 | tf_op jit(solution)/shard_map/pallas_call | solution.py:587
  606.4 22.2 %shard_map.502 = (bf16[1024,6656]{1,0:T(8,128)(2,1)}, f32[512,1024]{1,0:T(8,128)}, f32[8,1024]{1,0:T(8,128)}) custom-call(bf16[512,1024]{1,0:T(8,128)(2,1)} %get-tuple-element.372.normed, bf16[512,1024]{1,0:T(8,128)(2,1)} %get-tuple-element.533.dout, bf16[512,2048]{1,0:T(8,128)(2,1)} %get-tuple-element.388.dgate, bf16[512,2048]{1,0:T(8,128)(2,1)} %get-tuple-element.393.dx, ...), custom_call_target="tpu_custom_call" | custom-call | flops 10737418240 | bytes 54525952 | tf_op jit(solution)/shard_map/pallas_call | solution.py:686
  631.4 19.3 %shard_map.503 = (f32[512,2048]{1,0:T(8,128)}, bf16[512,2048]{1,0:T(8,128)(2,1)}, f32[8,2048]{1,0:T(8,128)}, f32[128,2048]{1,0:T(8,128)}) custom-call(bf16[512,1024]{1,0:T(8,128)(2,1)} %convert_element_type.181.dout, bf16[8,816,1024]{2,1,0:T(8,128)(2,1)} %bitcast.400, f32[512,2048]{1,0:T(8,128)} %get-tuple-element.403.y, ...), custom_call_target="tpu_custom_call" | custom-call | flops 2147483648 | bytes 27262976 | tf_op jit(solution)/shard_map/pallas_call | solution.py:404
  670.5 39.6 %shard_map.504 = (bf16[512,2048]{1,0:T(8,128)(2,1)}, f32[16,2048]{1,0:T(8,128)}, f32[16,2048]{1,0:T(8,128)}, f32[8,2048]{1,0:T(8,128)}, f32[512,384]{1,0:T(8,128...) custom-call(f32[528,2048]{1,0:T(8,128)} %get-tuple-element.406.xraw, ...), custom_call_target="tpu_custom_call" | custom-call | flops 2684354560 | bytes 12582912 | tf_op jit(solution)/shard_map/pallas_call | solution.py:587
  715.5 21.1 %shard_map.505 = (bf16[1024,6656]{1,0:T(8,128)(2,1)}, f32[512,1024]{1,0:T(8,128)}, f32[8,1024]{1,0:T(8,128)}) custom-call(bf16[512,1024]{1,0:T(8,128)(2,1)S(1)} %copy-done.25, bf16[512,1024]{1,0:T(8,128)(2,1)} %convert_element_type.181.dout, bf16[512,2048]{1,0:T(8,128)(2,1)} %get-tuple-element.405.dgate, bf16[512,2048]{1,0:T(8,128)(2,1)} %get-tuple-element.416.dx, ...), custom_call_target="tpu_custom_call" | custom-call | flops 10737418240 | bytes 54525952 | tf_op jit(solution)/shard_map/pallas_call | solution.py:686
  742.7 5.3 shard_map.506
  747.9 4.2 select_bitcast_fusion
  759.6 4.4 collective-permute-done.81
  764.0 14.8 %collective-permute-done.80 = bf16[128,1024]{1,0:T(8,128)(2,1)S(1)} collective-permute-done((bf16[128,1024]{1,0:T(8,128)(2,1)}, bf16[128,1024]{1,0:T(8,128)(2,1)S(1)}, u32[]{:S(2)}, u32[]{:S(2)}) %collective-permute-start.80) | collective-permute-done | bytes 262176 | tf_op jit(solution)/shard_map/ppermute | solution.py:1008
  781.8 8.1 shard_map.507
  810.3 6.3 multiply_reduce_fusion.1
  827.4 4.0 collective-permute-start.83
  832.7 3.3 collective-permute-done.83
  861.0 10.3 %shard_map.508 = (f32[3200,512]{1,0:T(8,128)}, f32[8,512]{1,0:T(8,128)}) custom-call(s32[16384]{0:T(1024)S(1)} %bitcast.432, s32[64]{0:T(128)S(1)} %copy-done.55, s32[2]{0:T(128)} %get-tuple-element.728.where, bf16[8,128,512]{2,1,0:T(8,128)(2,1)} %copy-done.23, bf16[3200,512]{1,0:T(8,128)(2,1)} %pad_maximum_fusion.3.base), custom_call_target="tpu_custom_call" | custom-call | bytes 13107200 | tf_op jit(solution)/shard_map/pallas_call | solution.py:878
  881.3 4.0 collective-permute-start.102
  889.2 8.2 collective-permute-done.101
  897.4 8.5 collective-permute-done.102
  905.9 21.0 %collective-permute-done.100 = bf16[128,1920]{1,0:T(8,128)(2,1)S(1)} collective-permute-done((bf16[128,1920]{1,0:T(8,128)(2,1)}, bf16[128,1920]{1,0:T(8,128)(2,1)S(1)}, u32[]{:S(2)}, u32[]{:S(2)}) %collective-permute-start.100) | collective-permute-done | bytes 491552 | tf_op jit(solution)/shard_map/ppermute | solution.py:1008
  932.3 4.3 collective-permute-start.104
  948.0 7.8 shard_map.509
  956.5 13.9 %multiply_reduce_fusion = (f32[]{:T(128)}, f32[3143,512]{1,0:T(8,128)S(1)}, f32[3143,512]{1,0:T(8,128)}) fusion(f32[3143,512]{1,0:T(8,128)} %param.47, f32[]{:T(128)} %min.3, f32[3200,512]{1,0:T(8,128)} %get-tuple-element.462, f32[3143,512]{1,0:T(8,128)} %param.48, f32[3143,512]{1,0:T(8,128)} %param.49), kind=kLoop, calls=%fused_computation.137 | loop fusion | flops 24138240 | bytes 38621192 | tf_op jit(solution)/shard_map/reduce_sum | solution.py:1231
  986.3 7.0 multiply_subtract_fusion
  993.3 3.3 shard_map.510
  (669 shorter events, 291.5 us)
Async XLA Ops:
  7.2 122.0 %all-gather.9.cloned.1.call-start = ((), (), s32[]{:S(2)}) async-start(), calls=%async_computation.5 | async-start | bytes 14745600 | tf_op jit(solution)/shard_map/all_gather | solution.py:1379
  12.5 154.9 %all-gather.11.cloned.1.call-start = ((), (), s32[]{:S(2)}) async-start(), calls=%async_computation.6 | async-start | bytes 14745600 | tf_op jit(solution)/shard_map/all_gather | solution.py:1401
  13.3 40.4 %collective-permute-start.29 = (f32[2,9,512]{2,0,1:T(2,128)S(1)}, f32[2,9,512]{2,0,1:T(2,128)S(1)}, u32[]{:S(2)}, u32[]{:S(2)}) collective-permute-start(f32[2,9,512]{2,0,1:T(2,128)S(1)} %fusion.74), channel_id=1, source_target_pairs={{0,2},{1,3},{2,0},{3,1},{4,6},{5,7},{6,4},{7,5},{8,10},{9,11},{10,... | collective-permute-start | bytes 110600 | tf_op jit(solution)/shard_map/ppermute | solution.py:1008
  47.2 7.1 collective-permute-start.28
  48.6 7.0 collective-permute-start.30
  51.7 12.8 %collective-permute-start.27 = (bf16[192,1024]{1,0:T(8,128)(2,1)S(1)}, bf16[192,1024]{1,0:T(8,128)(2,1)S(1)}, u32[]{:S(2)}, u32[]{:S(2)}) collective-permute-start(bf16[192,1024]{1,0:T(8,128)(2,1)S(1)} %pad_maximum_fusion.23), channel_id=1, source_target_pairs={{0,3},{1,0},{2,1},{3,2},{4,7},{5,4},{6,5},{7,6},{8,11},{9,8},{10,9... | collective-permute-start | bytes 1179656 | tf_op jit(solution)/shard_map/ppermute | solution.py:1008
  52.6 35.3 %collective-permute-start.26 = (bf16[192,1024]{1,0:T(8,128)(2,1)S(1)}, bf16[192,1024]{1,0:T(8,128)(2,1)S(1)}, u32[]{:S(2)}, u32[]{:S(2)}) collective-permute-start(bf16[192,1024]{1,0:T(8,128)(2,1)S(1)} %pad_maximum_fusion.23), channel_id=1, source_target_pairs={{0,2},{1,3},{2,0},{3,1},{4,6},{5,7},{6,4},{7,5},{8,10},{9,11},{10,... | collective-permute-start | bytes 1179656 | tf_op jit(solution)/shard_map/ppermute | solution.py:1008
  53.7 34.2 %collective-permute-start.25 = (bf16[192,1024]{1,0:T(8,128)(2,1)S(1)}, bf16[192,1024]{1,0:T(8,128)(2,1)S(1)}, u32[]{:S(2)}, u32[]{:S(2)}) collective-permute-start(bf16[192,1024]{1,0:T(8,128)(2,1)S(1)} %pad_maximum_fusion.23), channel_id=1, source_target_pairs={{0,1},{1,2},{2,3},{3,0},{4,5},{5,6},{6,7},{7,4},{8,9},{9,10},{10,1... | collective-permute-start | bytes 1179656 | tf_op jit(solution)/shard_map/ppermute | solution.py:1008
  89.5 155.9 %all-gather.13.cloned.1.call-start = ((), (), s32[]{:S(2)}) async-start(), calls=%async_computation.7 | async-start | bytes 15040512 | tf_op jit(solution)/shard_map/all_gather | solution.py:1403
  90.2 232.4 %all-gather.15.cloned.1.call-start = ((), (), s32[]{:S(2)}) async-start(), calls=%async_computation.8 | async-start | bytes 15040512 | tf_op jit(solution)/shard_map/all_gather | solution.py:1426
  90.4 10.2 %collective-permute-start.50 = (bf16[192,1024]{1,0:T(8,128)(2,1)S(1)}, bf16[192,1024]{1,0:T(8,128)(2,1)S(1)}, u32[]{:S(2)}, u32[]{:S(2)}) collective-permute-start(bf16[192,1024]{1,0:T(8,128)(2,1)S(1)} %pad_maximum_fusion.24), channel_id=1, source_target_pairs={{0,3},{1,0},{2,1},{3,2},{4,7},{5,4},{6,5},{7,6},{8,11},{9,8},{10,9... | collective-permute-start | bytes 1179656 | tf_op jit(solution)/shard_map/ppermute | solution.py:1008
  90.4 36.6 %collective-permute-start.49 = (bf16[192,1024]{1,0:T(8,128)(2,1)S(1)}, bf16[192,1024]{1,0:T(8,128)(2,1)S(1)}, u32[]{:S(2)}, u32[]{:S(2)}) collective-permute-start(bf16[192,1024]{1,0:T(8,128)(2,1)S(1)} %pad_maximum_fusion.24), channel_id=1, source_target_pairs={{0,2},{1,3},{2,0},{3,1},{4,6},{5,7},{6,4},{7,5},{8,10},{9,11},{10,... | collective-permute-start | bytes 1179656 | tf_op jit(solution)/shard_map/ppermute | solution.py:1008
  92.4 34.6 %collective-permute-start.48 = (bf16[192,1024]{1,0:T(8,128)(2,1)S(1)}, bf16[192,1024]{1,0:T(8,128)(2,1)S(1)}, u32[]{:S(2)}, u32[]{:S(2)}) collective-permute-start(bf16[192,1024]{1,0:T(8,128)(2,1)S(1)} %pad_maximum_fusion.24), channel_id=1, source_target_pairs={{0,1},{1,2},{2,3},{3,0},{4,5},{5,6},{6,7},{7,4},{8,9},{9,10},{10,1... | collective-permute-start | bytes 1179656 | tf_op jit(solution)/shard_map/ppermute | solution.py:1008
  182.8 11.3 %collective-permute-start.44 = (bf16[128,1024]{1,0:T(8,128)(2,1)}, bf16[128,1024]{1,0:T(8,128)(2,1)S(1)}, u32[]{:S(2)}, u32[]{:S(2)}) collective-permute-start(bf16[128,1024]{1,0:T(8,128)(2,1)} %get-tuple-element.589), channel_id=1, source_target_pairs={{0,1},{1,2},{2,3},{3,0},{4,5},{5,6},{6,7},{7,4},{8,9},{9,10},{10,1... | collective-permute-start | bytes 786440 | tf_op jit(solution)/shard_map/ppermute | solution.py:1008
  184.4 17.7 %collective-permute-start.43 = (bf16[128,1024]{1,0:T(8,128)(2,1)S(1)}, bf16[128,1024]{1,0:T(8,128)(2,1)S(1)}, u32[]{:S(2)}, u32[]{:S(2)}) collective-permute-start(bf16[128,1024]{1,0:T(8,128)(2,1)S(1)} %get-tuple-element.590), channel_id=1, source_target_pairs={{0,2},{1,3},{2,0},{3,1},{4,6},{5,7},{6,4},{7,5},{8,10},{9,11},{10,... | collective-permute-start | bytes 786440 | tf_op jit(solution)/shard_map/ppermute | solution.py:1008
  186.7 15.3 %collective-permute-start.42 = (bf16[128,1024]{1,0:T(8,128)(2,1)S(1)}, bf16[128,1024]{1,0:T(8,128)(2,1)S(1)}, u32[]{:S(2)}, u32[]{:S(2)}) collective-permute-start(bf16[128,1024]{1,0:T(8,128)(2,1)S(1)} %get-tuple-element.591), channel_id=1, source_target_pairs={{0,3},{1,0},{2,1},{3,2},{4,7},{5,4},{6,5},{7,6},{8,11},{9,8},{10,9... | collective-permute-start | bytes 786440 | tf_op jit(solution)/shard_map/ppermute | solution.py:1008
  245.4 383.1 %reduce-scatter.10.cloned.1.call-start = ((), (), s32[]{:S(2)}) async-start(), calls=%async_computation.9 | async-start | bytes 16384000
  373.0 10.1 %collective-permute-start.55 = (bf16[128,1024]{1,0:T(8,128)(2,1)S(1)}, bf16[128,1024]{1,0:T(8,128)(2,1)S(1)}, u32[]{:S(2)}, u32[]{:S(2)}) collective-permute-start(bf16[128,1024]{1,0:T(8,128)(2,1)S(1)} %fusion.50), channel_id=1, source_target_pairs={{0,3},{1,0},{2,1},{3,2},{4,7},{5,4},{6,5},{7,6},{8,11},{9,8},{10,9... | collective-permute-start | bytes 786440 | tf_op jit(solution)/shard_map/ppermute | solution.py:1008
  376.4 23.0 %collective-permute-start.54 = (bf16[128,1024]{1,0:T(8,128)(2,1)S(1)}, bf16[128,1024]{1,0:T(8,128)(2,1)S(1)}, u32[]{:S(2)}, u32[]{:S(2)}) collective-permute-start(bf16[128,1024]{1,0:T(8,128)(2,1)S(1)} %fusion.50), channel_id=1, source_target_pairs={{0,2},{1,3},{2,0},{3,1},{4,6},{5,7},{6,4},{7,5},{8,10},{9,11},{10,... | collective-permute-start | bytes 786440 | tf_op jit(solution)/shard_map/ppermute | solution.py:1008
  376.4 23.0 %collective-permute-start.53 = (bf16[128,1024]{1,0:T(8,128)(2,1)S(1)}, bf16[128,1024]{1,0:T(8,128)(2,1)S(1)}, u32[]{:S(2)}, u32[]{:S(2)}) collective-permute-start(bf16[128,1024]{1,0:T(8,128)(2,1)S(1)} %fusion.50), channel_id=1, source_target_pairs={{0,1},{1,2},{2,3},{3,0},{4,5},{5,6},{6,7},{7,4},{8,9},{9,10},{10,1... | collective-permute-start | bytes 786440 | tf_op jit(solution)/shard_map/ppermute | solution.py:1008
  499.8 293.7 %reduce-scatter.6.cloned.1.call-start = ((), (), s32[]{:S(2)}) async-start(), calls=%async_computation.3 | async-start | bytes 15335424 | tf_op jit(solution)/shard_map/reduce_scatter | solution.py:1473
  506.0 9.9 collective-permute-start.62
  508.8 13.3 %collective-permute-start.64 = (bf16[128,1024]{1,0:T(8,128)(2,1)}, bf16[128,1024]{1,0:T(8,128)(2,1)}, u32[]{:S(2)}, u32[]{:S(2)}) collective-permute-start(bf16[128,1024]{1,0:T(8,128)(2,1)} %get-tuple-element.621), channel_id=1, source_target_pairs={{0,1},{1,2},{2,3},{3,0},{4,5},{5,6},{6,7},{7,4},{8,9},{9,10},{10,1... | collective-permute-start | bytes 786440 | tf_op jit(solution)/shard_map/ppermute | solution.py:1008
  508.8 23.7 %collective-permute-start.63 = (bf16[128,1024]{1,0:T(8,128)(2,1)}, bf16[128,1024]{1,0:T(8,128)(2,1)}, u32[]{:S(2)}, u32[]{:S(2)}) collective-permute-start(bf16[128,1024]{1,0:T(8,128)(2,1)} %get-tuple-element.622), channel_id=1, source_target_pairs={{0,2},{1,3},{2,0},{3,1},{4,6},{5,7},{6,4},{7,5},{8,10},{9,11},{10,... | collective-permute-start | bytes 786440 | tf_op jit(solution)/shard_map/ppermute | solution.py:1008
  628.6 245.4 %reduce-scatter.8.cloned.1.call-start = ((), (), s32[]{:S(2)}) async-start(), calls=%async_computation.4 | async-start | bytes 15335424 | tf_op jit(solution)/shard_map/reduce_scatter | solution.py:1473
  650.6 18.8 %collective-permute-start.69 = (f32[128,2048]{1,0:T(8,128)}, f32[128,2048]{1,0:T(8,128)S(1)}, u32[]{:S(2)}, u32[]{:S(2)}) collective-permute-start(f32[128,2048]{1,0:T(8,128)} %get-tuple-element.409), channel_id=1, source_target_pairs={{4,0},{5,1},{6,2},{7,3},{12,8},{13,9},{14,10},{15,11},{20,16},{21,... | collective-permute-start | bytes 3145736 | tf_op jit(solution)/shard_map/ppermute | solution.py:1020
  658.2 7.7 collective-permute-start.72
  658.2 7.7 collective-permute-start.71
  665.9 47.2 %collective-permute-start.76 = (f32[130,128]{1,0:T(8,128)S(1)}, f32[130,128]{1,0:T(8,128)S(1)}, u32[]{:S(2)}, u32[]{:S(2)}) collective-permute-start(f32[130,128]{1,0:T(8,128)S(1)} %add_add_fusion.3), channel_id=1, source_target_pairs={{0,24},{8,16},{16,8},{24,0},{1,25},{9,17},{17,9},{25,1},{2,26},{10... | collective-permute-start | bytes 199688 | tf_op jit(solution)/shard_map/ppermute | solution.py:1025
  666.5 46.6 %collective-permute-start.75 = (f32[130,128]{1,0:T(8,128)S(1)}, f32[130,128]{1,0:T(8,128)S(1)}, u32[]{:S(2)}, u32[]{:S(2)}) collective-permute-start(f32[130,128]{1,0:T(8,128)S(1)} %add_add_fusion.3), channel_id=1, source_target_pairs={{0,16},{8,24},{16,0},{24,8},{1,17},{9,25},{17,1},{25,9},{2,18},{10... | collective-permute-start | bytes 199688 | tf_op jit(solution)/shard_map/ppermute | solution.py:1025
  668.5 44.7 %collective-permute-start.74 = (f32[130,128]{1,0:T(8,128)S(1)}, f32[130,128]{1,0:T(8,128)S(1)}, u32[]{:S(2)}, u32[]{:S(2)}) collective-permute-start(f32[130,128]{1,0:T(8,128)S(1)} %add_add_fusion.3), channel_id=1, source_target_pairs={{0,8},{8,0},{16,24},{24,16},{1,9},{9,1},{17,25},{25,17},{2,10},{10... | collective-permute-start | bytes 199688 | tf_op jit(solution)/shard_map/ppermute | solution.py:1025
  752.1 37.7 %collective-permute-start.89 = (bf16[1600,512]{1,0:T(8,128)(2,1)}, bf16[1600,512]{1,0:T(8,128)(2,1)}, u32[]{:S(2)}, u32[]{:S(2)}) collective-permute-start(bf16[1600,512]{1,0:T(8,128)(2,1)} %select_bitcast_fusion), channel_id=1, source_target_pairs={{0,4},{4,0},{1,5},{5,1},{2,6},{6,2},{3,7},{7,3},{8,12},{12,8},{9,1... | collective-permute-start | bytes 4915208 | tf_op jit(solution)/shard_map/ppermute | solution.py:1012
  754.7 9.4 collective-permute-start.81
  756.0 22.9 %collective-permute-start.80 = (bf16[128,1024]{1,0:T(8,128)(2,1)}, bf16[128,1024]{1,0:T(8,128)(2,1)S(1)}, u32[]{:S(2)}, u32[]{:S(2)}) collective-permute-start(bf16[128,1024]{1,0:T(8,128)(2,1)} %get-tuple-element.618), channel_id=1, source_target_pairs={{0,2},{1,3},{2,0},{3,1},{4,6},{5,7},{6,4},{7,5},{8,10},{9,11},{10,... | collective-permute-start | bytes 786440 | tf_op jit(solution)/shard_map/ppermute | solution.py:1008
  756.0 22.9 %collective-permute-start.79 = (bf16[128,1024]{1,0:T(8,128)(2,1)}, bf16[128,1024]{1,0:T(8,128)(2,1)S(1)}, u32[]{:S(2)}, u32[]{:S(2)}) collective-permute-start(bf16[128,1024]{1,0:T(8,128)(2,1)} %get-tuple-element.619), channel_id=1, source_target_pairs={{0,1},{1,2},{2,3},{3,0},{4,5},{5,6},{6,7},{7,4},{8,9},{9,10},{10,1... | collective-permute-start | bytes 786440 | tf_op jit(solution)/shard_map/ppermute | solution.py:1008
  796.8 19.9 %collective-permute-start.93 = (f32[122,128]{1,0:T(8,128)S(1)}, f32[122,128]{1,0:T(8,128)S(1)}, u32[]{:S(2)}, u32[]{:S(2)}) collective-permute-start(f32[122,128]{1,0:T(8,128)S(1)} %select_maximum_fusion), channel_id=1, source_target_pairs={{0,4},{4,0},{1,5},{5,1},{2,6},{6,2},{3,7},{7,3},{8,12},{12,8},{9,1... | collective-permute-start | bytes 187400 | tf_op jit(solution)/shard_map/ppermute | solution.py:1025
  805.9 52.3 %collective-permute-start.91 = (bf16[128,1920]{1,0:T(8,128)(2,1)}, bf16[128,1920]{1,0:T(8,128)(2,1)}, u32[]{:S(2)}, u32[]{:S(2)}) collective-permute-start(bf16[128,1920]{1,0:T(8,128)(2,1)} %concatenate.196), channel_id=1, source_target_pairs={{0,1},{1,2},{2,3},{3,0},{4,5},{5,6},{6,7},{7,4},{8,9},{9,10},{10,1... | collective-permute-start | bytes 1474568 | tf_op jit(solution)/shard_map/ppermute | solution.py:1008
  816.8 8.9 collective-permute-start.96
  819.2 8.2 collective-permute-start.95
  820.1 7.3 collective-permute-start.94
  823.2 34.9 %collective-permute-start.92 = (bf16[128,1920]{1,0:T(8,128)(2,1)S(1)}, bf16[128,1920]{1,0:T(8,128)(2,1)S(1)}, u32[]{:S(2)}, u32[]{:S(2)}) collective-permute-start(bf16[128,1920]{1,0:T(8,128)(2,1)S(1)} %copy-done.33), channel_id=1, source_target_pairs={{0,3},{1,0},{2,1},{3,2},{4,7},{5,4},{6,5},{7,6},{8,11},{9,8},{10,9... | collective-permute-start | bytes 1474568 | tf_op jit(solution)/shard_map/ppermute | solution.py:1008
  825.7 33.3 %collective-permute-start.90 = (bf16[128,1920]{1,0:T(8,128)(2,1)S(1)}, bf16[128,1920]{1,0:T(8,128)(2,1)S(1)}, u32[]{:S(2)}, u32[]{:S(2)}) collective-permute-start(bf16[128,1920]{1,0:T(8,128)(2,1)S(1)} %copy-done.32), channel_id=1, source_target_pairs={{0,2},{1,3},{2,0},{3,1},{4,6},{5,7},{6,4},{7,5},{8,10},{9,11},{10,... | collective-permute-start | bytes 1474568 | tf_op jit(solution)/shard_map/ppermute | solution.py:1008
  827.4 8.6 collective-permute-start.83
  831.5 7.0 collective-permute-start.84
  838.5 7.2 collective-permute-start.86
  881.2 16.2 %collective-permute-start.101 = (bf16[128,1920]{1,0:T(8,128)(2,1)}, bf16[128,1920]{1,0:T(8,128)(2,1)S(1)}, u32[]{:S(2)}, u32[]{:S(2)}) collective-permute-start(bf16[128,1920]{1,0:T(8,128)(2,1)} %concatenate.202), channel_id=1, source_target_pairs={{0,1},{1,2},{2,3},{3,0},{4,5},{5,6},{6,7},{7,4},{8,9},{9,10},{10,1... | collective-permute-start | bytes 1474568 | tf_op jit(solution)/shard_map/ppermute | solution.py:1008
  881.3 24.7 %collective-permute-start.102 = (bf16[128,1920]{1,0:T(8,128)(2,1)}, bf16[128,1920]{1,0:T(8,128)(2,1)S(1)}, u32[]{:S(2)}, u32[]{:S(2)}) collective-permute-start(bf16[128,1920]{1,0:T(8,128)(2,1)} %concatenate.203), channel_id=1, source_target_pairs={{0,3},{1,0},{2,1},{3,2},{4,7},{5,4},{6,5},{7,6},{8,11},{9,8},{10,9... | collective-permute-start | bytes 1474568 | tf_op jit(solution)/shard_map/ppermute | solution.py:1008
  885.3 41.7 %collective-permute-start.100 = (bf16[128,1920]{1,0:T(8,128)(2,1)}, bf16[128,1920]{1,0:T(8,128)(2,1)S(1)}, u32[]{:S(2)}, u32[]{:S(2)}) collective-permute-start(bf16[128,1920]{1,0:T(8,128)(2,1)} %concatenate.201), channel_id=1, source_target_pairs={{0,2},{1,3},{2,0},{3,1},{4,6},{5,7},{6,4},{7,5},{8,10},{9,11},{10,... | collective-permute-start | bytes 1474568 | tf_op jit(solution)/shard_map/ppermute | solution.py:1008
  (135 other events, 1915.4 us)
Sparse Core Ops, SparseCore 0:
  12.7 77.8 all-gather.8
  93.0 74.3 all-gather.10
  169.9 75.4 all-gather.12
  247.1 75.4 all-gather.14
  500.0 124.5 reduce-scatter.9
  628.7 100.2 reduce-scatter.5
  736.8 96.8 reduce-scatter.7

commit v3 on v2

--- a/solution.py
+++ b/solution.py
@@ -23,7 +23,7 @@
 WIDTH = 512
 GROUPS = INNER // WIDTH
 LANES = 128
-TILE = 800
+TILE = 1600
 CLASSES = 4
 PAST = 1 << 11
 CAP = 128
@@ -66,6 +66,10 @@
 
 
 def sigmoid(v):
+    return 0.5 * jnp.tanh(0.5 * v) + 0.5
+
+
+def small_sigmoid(v):
     return 1.0 / (1.0 + jnp.exp(-v))
 
 
@@ -559,7 +563,7 @@
             ddt = s_ddt[r, :] + da * rate
             rate_sum = rate_sum + jnp.sum(da * (rate * s_dt[r, :]), axis=0, keepdims=True)
             raw = bcdt[HALO + b * BLOCK : HALO + (b + 1) * BLOCK, 2 * STATE :] + headp[0:1, :]
-            ddt = ddt * sigmoid(raw)
+            ddt = ddt * small_sigmoid(raw)
             bias_sum = bias_sum + jnp.sum(ddt, axis=0, keepdims=True)
             dbc_o[r, 2 * STATE :] = ddt
         dheadp_o[...] = jnp.concatenate(
@@ -888,7 +892,7 @@
 
 
 def tile_lines(core, height):
-    return (core[0] * 2 + pl.program_id(1)) * height
+    return (core[0] * pl.num_programs(1) + pl.program_id(1)) * height
 
 
 def tile_logits(core, table, chosen, real):
@@ -903,7 +907,7 @@
 def tile_hit(core, table, lines, wanted):
     height = table.shape[2]
     first = pl.program_id(0) * lines + tile_lines(core, height)
-    return first + iota((height, wanted.shape[1]), 0) == wanted[0:1, :]
+    return iota((height, wanted.shape[1]), 0) == wanted[0:1, :] - first
 
 
 def one_half(core, first, second):
@@ -912,8 +916,6 @@
 
 def measure_kernel(real, lines, core, first_half, second_half, chosen, wanted, out, s_stats):
     table = one_half(core, first_half, second_half)
-    logits = tile_logits(core, table, chosen, real)
-    hit = tile_hit(core, table, lines, wanted)
     first = (pl.program_id(0) == 0) & (pl.program_id(1) == 0)
 
     @pl.when(first)
@@ -921,12 +923,14 @@
         s_stats[0:1, :] = jnp.full((1, s_stats.shape[1]), -1e30, f32)
         s_stats[1:8, :] = jnp.zeros((7, s_stats.shape[1]), f32)
 
-    old = s_stats[0:1, :]
+    old, total, picked = s_stats[0:1, :], s_stats[1:2, :], s_stats[2:3, :]
+    logits = tile_logits(core, table, chosen, real)
+    hit = tile_hit(core, table, lines, wanted)
     top = jnp.maximum(old, jnp.max(logits, axis=0, keepdims=True))
-    total = s_stats[1:2, :] * jnp.exp(old - top)
-    s_stats[1:2, :] = total + jnp.sum(jnp.exp(logits - top), axis=0, keepdims=True)
-    s_stats[2:3, :] += jnp.sum(jnp.where(hit, logits, 0.0), axis=0, keepdims=True)
-    s_stats[0:1, :] = top
+    total = total * jnp.exp(old - top)
+    total = total + jnp.sum(jnp.exp(logits - top), axis=0, keepdims=True)
+    picked = picked + jnp.sum(jnp.where(hit, logits, 0.0), axis=0, keepdims=True)
+    s_stats[0:1, :], s_stats[1:2, :], s_stats[2:3, :] = top, total, picked
     out[...] = s_stats[...]
 
 
@@ -963,10 +967,6 @@
     real, lines, core, first_half, second_half, chosen, wanted, stats, dtable, dchosen, s_sum
 ):
     table = one_half(core, first_half, second_half)
-    logits = tile_logits(core, table, chosen, real)
-    hit = tile_hit(core, table, lines, wanted)
-    soft = jnp.exp(logits - stats[0:1, :])
-    dlogits = (stats[1:2, :] * (soft - jnp.where(hit, 1.0, 0.0))).astype(bf16)
     step = pl.program_id(0) * pl.num_programs(1) + pl.program_id(1)
     parts, width = table.shape[1], table.shape[3]
 
@@ -974,10 +974,13 @@
     def _():
         s_sum[...] = jnp.zeros(s_sum.shape, f32)
 
+    soft = jnp.exp(tile_logits(core, table, chosen, real) - stats[0:1, :])
+    hit = tile_hit(core, table, lines, wanted)
+    dlogits = (stats[1:2, :] * jnp.where(hit, soft - 1.0, soft)).astype(bf16)
     for part in range(parts):
-        at = slice(part * width, (part + 1) * width)
-        dtable[0, part] = nn(dlogits, chosen[:, at]).astype(bf16)
-        s_sum[:, at] += tn(dlogits, table[0, part])
+        columns = slice(part * width, (part + 1) * width)
+        dtable[0, part] = nn(dlogits, chosen[:, columns]).astype(bf16)
+        s_sum[:, columns] += tn(dlogits, table[0, part])
 
     @pl.when(step == CLASSES * pl.num_programs(1) - 1)
     def _():
@@ -1131,14 +1134,40 @@
     return turn_heads(jnp.pad(part, ((0, 0), (0, 2 * STATE + LANES - width))))
 
 
-def reduce_layer(mine):
+def split_kernel(z, mine, *outs):
+    n = len(outs)
+    source, target = iota((LANES, LANES), 0), iota((LANES, LANES), 1)
+    heads = HEADS // n
+    group = (z[0] + n - target // heads) % n
+    turn = (source == group * heads + target % heads) & (target < HEADS)
+    steps = nn(mine[:, 2 * SHARE + 3 * WIDTH : 3 * SHARE], turn.astype(bf16)).astype(bf16)
+    for by, out in enumerate(outs):
+        at = (n - by) % n * SHARE
+        out[:, : 3 * WIDTH] = mine[:, at : at + 3 * WIDTH]
+        for part in range(2):
+            low = 3 * WIDTH + part * LANES
+            at = part * SHARE + 3 * WIDTH
+            out[:, low : low + LANES] = mine[:, at : at + LANES]
+        out[:, 3 * WIDTH + 2 * LANES :] = steps
+
+
+def exchange_layer(mine):
     n_tensor = lax.axis_size("tensor")
-    shares = [mine[:, j * SHARE : (j + 1) * SHARE] for j in range(n_tensor)]
-    bcdt = turn_heads(jnp.concatenate([share[:, 3 * WIDTH :] for share in shares[:3]], axis=1))
-    blocks = []
-    for by in range(n_tensor):
-        block = jnp.concatenate([shares[-by][:, : 3 * WIDTH], bcdt], axis=1)
-        blocks.append(block if by == 0 else shifted(block, "tensor", by))
+    shape = (mine.shape[0], 3 * WIDTH + 3 * LANES)
+    blocks = call(
+        split_kernel,
+        (1,),
+        [whole(mine.shape)],
+        [whole(shape)] * n_tensor,
+        [struct(shape, bf16)] * n_tensor,
+        [],
+        prefetch=1,
+        bytes_moved=4 * mine.size,
+    )(lax.axis_index("tensor")[None], mine)
+    return [blocks[0]] + [shifted(blocks[by], "tensor", by) for by in range(1, n_tensor)]
+
+
+def sum_layer(blocks):
     blocks = [block.astype(f32) for block in blocks]
     even = functools.reduce(jnp.add, blocks[0::2])
     odd = functools.reduce(jnp.add, blocks[1::2])
@@ -1161,7 +1190,7 @@
     return out, following, (resid, normed, y, gate, xraw, before, bcdt, c, ecf, scaled, inverse)
 
 
-def layer_backward(dresid, kept, gain, packed, wb, smalls, done):
+def layer_backward(dresid, kept, gain, packed, wb, smalls):
     resid, normed, y, gate, xraw, before, bcdt, c, ecf, scaled, inverse = kept
     chan, headp, bcv = smalls
     dout = dresid.astype(bf16)
@@ -1170,7 +1199,6 @@
     dx, tail, halo, dchan, dbcdt, bc_halo, dheadp, dbcv = scan_back(
         xraw, dy, bcdt, before, after, chan, headp, bcv
     )
-    dx, done = lax.optimization_barrier((dx, done))
     back, bc_back = to_earlier(halo), to_earlier(bc_halo)
     grads, dresid, dnorm_gain = layer_grads(
         normed, dout, dgate, dx, tail, back, dbcdt, bc_back,
@@ -1178,7 +1206,7 @@
     )
     dchan = jnp.concatenate([dchan[: CONV + 1], dgain[:1]], axis=0)
     smalls = (dnorm_gain[0], dchan, dheadp[:3, :HEADS], dbcv[: CONV + 1])
-    return dresid, grads, smalls, done
+    return dresid, grads, smalls
 
 
 def flat_layer(parts, final_gain):
@@ -1301,7 +1329,7 @@
     scored = loss_pos.shape[1]
     half = scored // 2
     lines = embed.shape[0]
-    padded = -(-lines // TILE) * TILE
+    padded = -(-lines // (2 * TILE)) * (2 * TILE)
     vocab = lines * CLASSES
 
     own_meta = jnp.concatenate([token_ids, loss_pos, targets, lengths], axis=1)
@@ -1403,6 +1431,14 @@
     packed = [lax.all_gather(share, DP)]
     halves = [half.reshape(CLASSES, n_data // CLASSES, padded // 2, -1) for half in halves]
     found = lookup(keys, starts, halves)
+    stacked = (False, True, True, True, True, True, True, False)
+    everyone = n_tensor * n_data
+    copies = (1, 1, n_tensor, 1, n_data, n_data, everyone, everyone)
+    weights = (embed, w_zx, w_bcdt, w_out, channel, per_head, bc_conv, gains)
+    found, late = lax.optimization_barrier((found, weights))
+    weight_sq = jnp.concatenate(
+        [group_squares(*pair) / shared_by for *pair, shared_by in zip(late, stacked, copies)]
+    )
     found = found.reshape(n_tensor, rows, D)
     gain_rows = [jnp.broadcast_to(gains[i][None, :], (8, D)) for i in range(LAYERS + 1)]
 
@@ -1421,6 +1457,7 @@
             lambda so_far: so_far,
             (resid, normed),
         )
+    resid, weight_sq = lax.optimization_barrier((resid, weight_sq))
     for share in shares[1:]:
         share = lax.optimization_barrier((share, packed[-1], resid))[0]
         packed.append(lax.all_gather(share, DP))
@@ -1432,9 +1469,11 @@
         )
         kept.append(saved)
 
-    both = by_core(normed, swapped(normed))
-    pick = (positions[0][:, None] == jnp.arange(seq)[None, :]).astype(bf16)
-    chosen = around(nn(pick, both).astype(bf16), "tensor").reshape(n_tensor * half, D)
+    pick = (own_positions[:, None] - core * rows == jnp.arange(rows)[None, :]).astype(bf16)
+    picked = nn(pick, normed).astype(bf16).reshape(2, half, D)
+    mine = jnp.where(core == 0, picked[0], picked[1])
+    other = jnp.where(core == 0, picked[1], picked[0])
+    chosen = around(mine + swapped(other), "tensor").reshape(n_tensor * half, D)
     chosen = by_core(chosen, swapped(chosen))
     want, known = place(all_wanted)
     want = jnp.broadcast_to(jnp.where(known, want, -1), (8, n_tensor * scored))
@@ -1463,17 +1502,12 @@
 
     shares = [None] * LAYERS
     parts = [None] * LAYERS
-    flats = []
     for depth in reversed(range(LAYERS)):
-        dresid, grad, parts[depth], flats = layer_backward(
-            dresid, kept[depth], gain_rows[depth], packed[depth], w_small[depth], smalls[depth],
-            flats,
+        dresid, grad, parts[depth] = layer_backward(
+            dresid, kept[depth], gain_rows[depth], packed[depth], w_small[depth], smalls[depth]
         )
         grad, table_part, dresid = lax.optimization_barrier((grad, table_part, dresid))
         shares[depth] = lax.psum_scatter(grad, DP, scatter_dimension=0, tiled=True)
-        if depth > 0:
-            flat = flat_layer(parts[depth], dfinal_gain if depth == LAYERS - 1 else None)
-            flats = [everywhere(flat, ("core", "tensor", "chip"))] + flats
 
     def rows_out(part):
         return jnp.stack(
@@ -1481,7 +1515,8 @@
         )
 
     sent = send_rows(spots_first, dresid, n_tensor)
-    sent, table_part = lax.optimization_barrier((sent, table_part))
+    sent, share = lax.optimization_barrier((sent, shares[1]))
+    last = exchange_layer(share)
     arrived = jnp.pad(rows_out(sent), ((0, 0), (0, rows - CAP), (0, 0)))
     for offset in range(CAP, rows, CAP):
         arrived = lax.cond(
@@ -1495,35 +1530,27 @@
             arrived,
         )
     arrived = arrived.reshape(count, D)
+    own = lax.axis_index(DP)
+    cls = own // (n_data // CLASSES)
+
+    def pack_round(offset):
+        where = jnp.stack([own, offset])
+        return pack_rows(keys, ranks, starts, firsts, where, arrived, n_data)
+
+    def add_round(offset, recv, total):
+        return tuple(add_rows(all_lines, all_firsts, jnp.stack([cls, offset]), recv, total))
+
+    outgoing, last, parts, table_part = lax.optimization_barrier(
+        (pack_round(0), last, parts, table_part)
+    )
+    recv = exchanged(outgoing)
+    blocks = [exchange_layer(shares[0]), last]
+    flat = jnp.concatenate([flat_layer(*pair) for pair in zip(parts, [None, dfinal_gain])])
+    flat = everywhere(flat, ("core", "tensor", "chip"))
     keep = jnp.where(core == 0, table_part[0], table_part[1])
     give = jnp.where(core == 0, table_part[1], table_part[0])
     table_part = by_core(keep, swapped(give))
-    own = lax.axis_index(DP)
-    cls = own // (n_data // CLASSES)
-
-    def pack_round(offset):
-        where = jnp.stack([own, offset])
-        return pack_rows(keys, ranks, starts, firsts, where, arrived, n_data)
-
-    def add_round(offset, recv, total):
-        return tuple(add_rows(all_lines, all_firsts, jnp.stack([cls, offset]), recv, total))
-
-    stacked = (False, True, True, True, True, True, True, False)
-    everyone = n_tensor * n_data
-    copies = (1, 1, n_tensor, 1, n_data, n_data, everyone, everyone)
-    weights = (embed, w_zx, w_bcdt, w_out, channel, per_head, bc_conv, gains)
-    outgoing, shares[1:], parts[0], late = lax.optimization_barrier(
-        (pack_round(0), shares[1:], parts[0], weights)
-    )
-    recv = exchanged(outgoing)
-    grads = [None] + [reduce_layer(share) for share in shares[1:]]
-    flats = [everywhere(flat_layer(parts[0], None), ("core", "tensor", "chip"))] + flats
-    weight_sq = jnp.concatenate(
-        [group_squares(*pair) / shared_by for *pair, shared_by in zip(late, stacked, copies)]
-    )
-    recv, table_part, grads[1:], flats[0], weight_sq = lax.optimization_barrier(
-        (recv, table_part, grads[1:], flats[0], weight_sq)
-    )
+    recv, table_part, blocks, flat = lax.optimization_barrier((recv, table_part, blocks, flat))
     added = add_round(0, recv, table_part)
     added = lax.while_loop(
         lambda carry: carry[0] < most,
@@ -1532,8 +1559,10 @@
     )[1]
     grad_table, table_sq = added[0][:lines], jnp.sum(added[1])
 
-    grads[0] = reduce_layer(shares[0])
-    grad_zx, grad_out, grad_bcdt = (jnp.stack(parts) for parts in zip(*grads))
+    grads = [sum_layer(block) for block in blocks]
+    grad_zx, grad_out, grad_bcdt = (jnp.stack(layers) for layers in zip(*grads))
+    height = (flat.shape[0] - D // LANES) // LAYERS
+    flats = [flat[:height], flat[height:]]
     small_grads = [unflat_layer(flat) for flat in flats]
     grad_gains = jnp.stack([part[0] for part in small_grads] + [small_grads[-1][4]])
     grad_channel, grad_head, grad_bc_conv = (

time: 1010 us -> 998 us (0.988)
  waiting for transfers between devices: 328 us -> 300 us
  starting transfers between devices: 117 us -> 133 us
    ppermute x27, waiting for transfers between devices: 169 us -> 130 us  [shifted(): return lax.ppermute(values, axis, [(i, (i + by) % n) for i in range(n)])]
    ppermute x27, starting transfers between devices: 38.3 us -> 55 us  [shifted(): return lax.ppermute(values, axis, [(i, (i + by) % n) for i in range(n)])]
    ppermute x49 -> x42, waiting for transfers between devices: 44 us -> 47.2 us  [crossed(): return lax.ppermute(values, axis, [(i, i ^ by) for i in range(n)])]
    ppermute x49 -> x42, starting transfers between devices: 57.9 us -> 58.3 us  [crossed(): return lax.ppermute(values, axis, [(i, i ^ by) for i in range(n)])]
  transfers between devices with their start and end apart: 99 -> 92, of which waited for: 62 -> 52; matrix products, arithmetic and copies ran while one was open for 11% -> 10% of each run, Pallas kernels for 24% -> 23%
where the time goes in v3:
time: 998 us; the launch traced here: 993 us
  Pallas kernels  374 us (37%)
  waiting for transfers between devices  300 us (30%)
  starting transfers between devices  133 us (13%)
  other arithmetic  106 us (11%)
  local copies, waits for them, and re-layouts  52.3 us (5%)
  between operations  24 us (2%)
    ppermute x27, waiting for transfers between devices, shifted(): return lax.ppermute(values, axis, [(i, (i + by) % n) for i in range(n)])  130 us
    pallas_call x2, Pallas kernels, scan_back(): call(back_kernel, (GROUPS,), [columns(ext), columns(rows), whole((ext, 38...  77.4 us
    ppermute x42, starting transfers between devices, crossed(): return lax.ppermute(values, axis, [(i, i ^ by) for i in range(n)])  58.3 us
    pallas_call x1, Pallas kernels, vocab_back(): call(functools.partial(vocab_kernel, real, 2 * lines), (CLASSES, lines //...  56 us
    ppermute x27, starting transfers between devices, shifted(): return lax.ppermute(values, axis, [(i, (i + by) % n) for i in range(n)])  55 us
    ppermute x42, waiting for transfers between devices, crossed(): return lax.ppermute(values, axis, [(i, i ^ by) for i in range(n)])  47.2 us
    pallas_call x2, Pallas kernels, scan_front(): call(scan_kernel, (GROUPS,), [whole((ext, D)), packed_zx(packed), whole(w...  45.1 us
    pallas_call x2, Pallas kernels, layer_grads(): call(grads_kernel, (GROUPS,), [whole((rows, D)), whole((rows, D)), column...  43.3 us
  transfers between devices with their start and end apart: 92, of which 52 were waited for; matrix products, arithmetic and copies ran while one was open for 10% of the time, Pallas kernels for 23%

profile of v3, /device:TPU:0, one launch (start us, length us, event | category | flops | bytes accessed | tf_op | source)
XLA Modules:
  0.0 993.4 jit_solution(8498666904076107547)
XLA Ops:
  36.0 3.5 select_reduce_fusion
  61.4 3.5 collective-permute-done.33
  73.0 11.9 %collective-permute-done.26 = bf16[192,1024]{1,0:T(8,128)(2,1)} collective-permute-done((bf16[192,1024]{1,0:T(8,128)(2,1)}, bf16[192,1024]{1,0:T(8,128)(2,1)}, u32[]{:S(2)}, u32[]{:S(2)}) %collective-permute-start.26) | collective-permute-done | bytes 393248 | tf_op jit(solution)/shard_map/ppermute | solution.py:1011
  90.4 8.8 collective-permute-start.48
  105.1 4.2 collective-permute-done.48
  109.3 15.7 %collective-permute-done.49 = bf16[192,1024]{1,0:T(8,128)(2,1)S(1)} collective-permute-done((bf16[192,1024]{1,0:T(8,128)(2,1)}, bf16[192,1024]{1,0:T(8,128)(2,1)S(1)}, u32[]{:S(2)}, u32[]{:S(2)}) %collective-permute-start.49) | collective-permute-done | bytes 393248 | tf_op jit(solution)/shard_map/ppermute | solution.py:1011
  128.7 41.0 %all-gather.11.cloned.1.call-done = bf16[12800,512]{1,0:T(8,128)(2,1)} async-done(((bf16[1600,512]{1,0:T(8,128)(2,1)}), bf16[12800,512]{1,0:T(8,128)(2,1)}) %all-gather.11.cloned.1.call-update) | async-done | bytes 13107216 | tf_op jit(solution)/shard_map/all_gather | solution.py:1429
  169.7 12.8 %shard_map.492 = bf16[2048,1024]{1,0:T(8,128)(2,1)S(1)} custom-call(s32[2048]{0:T(1024)S(1)} %select_reduce_fusion.1.keys, s32[16]{0:T(128)S(1)} %copy-done.45, bf16[4,2,1600,512]{3,2,1,0:T(8,128)(2,1)} %bitcast.407, bf16[4,2,1600,512]{3,2,1,0:T(8,128)(2,1)} %bitcast.410), custom_call_target="tpu_custom_call" | custom-call | bytes 26214400 | tf_op jit(solution)/shard_map/pallas_call | solution.py:752
  191.6 5.1 multiply_reduce_fusion.1
  199.3 3.4 collective-permute-done.43
  205.3 4.3 shard_map.493
  209.7 38.1 %all-gather.13.cloned.1.call-done = bf16[6528,1024]{1,0:T(8,128)(2,1)} async-done(((bf16[816,1024]{1,0:T(8,128)(2,1)}), bf16[6528,1024]{1,0:T(8,128)(2,1)}) %all-gather.13.cloned.1.call-update) | async-done | bytes 13369360 | tf_op jit(solution)/shard_map/all_gather | solution.py:1431
  258.2 22.8 %shard_map.494 = (f32[512,2048]{1,0:T(8,128)}, f32[512,2048]{1,0:T(8,128)}, f32[528,2048]{1,0:T(8,128)}, f32[128,2048]{1,0:T(8,128)}, f32[528,384]{1,0:T(8,128)}...) custom-call(bf16[528,1024]{1,0:T(8,128)(2,1)} %pad_maximum_fusion.9.nx, bf16[8,816,1024]{2,1,0:T(8,128)(2,1)} %bitcast.394, ...), custom_call_target="tpu_custom_call" | custom-call | flops 4429185024 | bytes 20971520 | tf_op jit(solution)/shard_map/pallas_call | solution.py:256
  286.8 13.7 %shard_map.495 = (f32[512,2048]{1,0:T(8,128)}, bf16[512,2048]{1,0:T(8,128)(2,1)}, f32[512,128]{1,0:T(8,128)}, f32[512,1024]{1,0:T(8,128)}, bf16[512,1024]{1,0:T(8,128)(2,1)}) custom-call(f32[512,2048]{1,0:T(8,128)} %get-tuple-element.388.y, f32[512,2048]{1,0:T(8,128)} %get-tuple-element.389.gate, bf16[512,128]{1,0:T(8,128)(2,1)} %get-tuple-element.390.c, ...), custom_call_target="tpu_custom_call" | custom-call | flops 2147483648 | bytes 18874368 | tf_op jit(solution)/shard_map/pallas_call | solution.py:329
  306.7 18.2 %all-gather.15.cloned.1.call-done = bf16[6528,1024]{1,0:T(8,128)(2,1)} async-done(((bf16[816,1024]{1,0:T(8,128)(2,1)}), bf16[6528,1024]{1,0:T(8,128)(2,1)}) %all-gather.15.cloned.1.call-update) | async-done | bytes 13369360 | tf_op jit(solution)/shard_map/all_gather | solution.py:1463
  328.0 22.3 %shard_map.496 = (f32[512,2048]{1,0:T(8,128)}, f32[512,2048]{1,0:T(8,128)}, f32[528,2048]{1,0:T(8,128)}, f32[128,2048]{1,0:T(8,128)}, f32[528,384]{1,0:T(8,128)}...) custom-call(bf16[528,1024]{1,0:T(8,128)(2,1)} %pad_maximum_fusion.10.nx, bf16[8,816,1024]{2,1,0:T(8,128)(2,1)} %bitcast.399, ...), custom_call_target="tpu_custom_call" | custom-call | flops 4429185024 | bytes 20971520 | tf_op jit(solution)/shard_map/pallas_call | solution.py:256
  356.0 14.3 %shard_map.497 = (f32[512,2048]{1,0:T(8,128)}, bf16[512,2048]{1,0:T(8,128)(2,1)}, f32[512,128]{1,0:T(8,128)}, f32[512,1024]{1,0:T(8,128)}, bf16[512,1024]{1,0:T(8,128)(2,1)}) custom-call(f32[512,2048]{1,0:T(8,128)} %get-tuple-element.408.y, f32[512,2048]{1,0:T(8,128)} %get-tuple-element.409.gate, bf16[512,128]{1,0:T(8,128)(2,1)} %get-tuple-element.410.c, ...), custom_call_target="tpu_custom_call" | custom-call | flops 2147483648 | bytes 18874368 | tf_op jit(solution)/shard_map/pallas_call | solution.py:329
  379.3 5.5 collective-permute-done.53
  384.8 10.6 %collective-permute-done.54 = bf16[128,1024]{1,0:T(8,128)(2,1)S(1)} collective-permute-done((bf16[128,1024]{1,0:T(8,128)(2,1)S(1)}, bf16[128,1024]{1,0:T(8,128)(2,1)S(1)}, u32[]{:S(2)}, u32[]{:S(2)}) %collective-permute-start.54) | collective-permute-done | bytes 262176 | tf_op jit(solution)/shard_map/ppermute | solution.py:1011
  400.6 29.0 %shard_map.498 = f32[8,1024]{1,0:T(8,128)} custom-call(s32[1]{0:T(128)} %bitcast.130.core, bf16[4,2,1600,512]{3,2,1,0:T(8,128)(2,1)} %bitcast.408, bf16[4,2,1600,512]{3,2,1,0:T(8,128)(2,1)} %bitcast.411, bf16[1024,1024]{1,0:T(8,128)(2,1)} %pad_maximum_fusion.4.chosen, s32[8,1024]{1,0:T(8,128)} %broadcast_in_dim.141.wanted), custom_call_target="tpu_custom_call" | custom-call | flops 13421772800 | bytes 13107200 | tf_op jit(solution)/shard_map/pallas_call | solution.py:953
  431.7 6.2 collective-permute-start.58
  446.4 56.0 %shard_map.499 = (bf16[4,2,1600,512]{3,2,1,0:T(8,128)(2,1)}, bf16[1024,1024]{1,0:T(8,128)(2,1)}) custom-call(s32[1]{0:T(128)} %bitcast.130.core, bf16[4,2,1600,512]{3,2,1,0:T(8,128)(2,1)} %bitcast.409, bf16[4,2,1600,512]{3,2,1,0:T(8,128)(2,1)} %bitcast.412, bf16[1024,1024]{1,0:T(8,128)(2,1)} %pad_maximum_fusion.4.chosen, ...), custom_call_target="tpu_custom_call" | custom-call | flops 40265318400 | bytes 26214400 | tf_op jit(solution)/shard_map/pallas_call | solution.py:993
  510.0 7.6 collective-permute-done.62
  517.6 13.3 %collective-permute-done.63 = bf16[128,1024]{1,0:T(8,128)(2,1)S(1)} collective-permute-done((bf16[128,1024]{1,0:T(8,128)(2,1)S(1)}, bf16[128,1024]{1,0:T(8,128)(2,1)S(1)}, u32[]{:S(2)}, u32[]{:S(2)}) %collective-permute-start.63) | collective-permute-done | bytes 262176 | tf_op jit(solution)/shard_map/ppermute | solution.py:1011
  536.1 18.0 %shard_map.500 = (f32[512,2048]{1,0:T(8,128)}, bf16[512,2048]{1,0:T(8,128)(2,1)}, f32[8,2048]{1,0:T(8,128)}, f32[128,2048]{1,0:T(8,128)}) custom-call(bf16[512,1024]{1,0:T(8,128)(2,1)} %get-tuple-element.573.dout, bf16[8,816,1024]{2,1,0:T(8,128)(2,1)} %bitcast.401, f32[512,2048]{1,0:T(8,128)} %get-tuple-element.417.y, f32[512,2048]{1,0:T(8,128)} %get-tuple-element.409.gate, ...), custom_call_target="tpu_custom_call" | custom-call | flops 2147483648 | bytes 27262976 | tf_op jit(solution)/shard_map/pallas_call | solution.py:408
  555.4 3.5 collective-permute-done.66.dst
  559.8 38.7 %shard_map.501 = (bf16[512,2048]{1,0:T(8,128)(2,1)}, f32[16,2048]{1,0:T(8,128)}, f32[16,2048]{1,0:T(8,128)}, f32[8,2048]{1,0:T(8,128)}, f32[512,384]{1,0:T(8,128...) custom-call(f32[528,2048]{1,0:T(8,128)} %get-tuple-element.420.xraw, ...), custom_call_target="tpu_custom_call" | custom-call | flops 2684354560 | bytes 12582912 | tf_op jit(solution)/shard_map/pallas_call | solution.py:591
  603.7 22.1 %shard_map.502 = (bf16[1024,6656]{1,0:T(8,128)(2,1)}, f32[512,1024]{1,0:T(8,128)}, f32[8,1024]{1,0:T(8,128)}) custom-call(bf16[512,1024]{1,0:T(8,128)(2,1)} %get-tuple-element.403.normed, bf16[512,1024]{1,0:T(8,128)(2,1)} %get-tuple-element.573.dout, bf16[512,2048]{1,0:T(8,128)(2,1)} %get-tuple-element.419.dgate, bf16[512,2048]{1,0:T(8,128)(2,1)} %get-tuple-element.424.dx, ...), custom_call_target="tpu_custom_call" | custom-call | flops 10737418240 | bytes 54525952 | tf_op jit(solution)/shard_map/pallas_call | solution.py:690
  628.7 18.5 %shard_map.503 = (f32[512,2048]{1,0:T(8,128)}, bf16[512,2048]{1,0:T(8,128)(2,1)}, f32[8,2048]{1,0:T(8,128)}, f32[128,2048]{1,0:T(8,128)}) custom-call(bf16[512,1024]{1,0:T(8,128)(2,1)} %convert_element_type.181.dout, bf16[8,816,1024]{2,1,0:T(8,128)(2,1)} %bitcast.396, f32[512,2048]{1,0:T(8,128)} %get-tuple-element.434.y, ...), custom_call_target="tpu_custom_call" | custom-call | flops 2147483648 | bytes 27262976 | tf_op jit(solution)/shard_map/pallas_call | solution.py:408
  652.9 38.7 %shard_map.504 = (bf16[512,2048]{1,0:T(8,128)(2,1)}, f32[16,2048]{1,0:T(8,128)}, f32[16,2048]{1,0:T(8,128)}, f32[8,2048]{1,0:T(8,128)}, f32[512,384]{1,0:T(8,128...) custom-call(f32[528,2048]{1,0:T(8,128)} %get-tuple-element.437.xraw, ...), custom_call_target="tpu_custom_call" | custom-call | flops 2684354560 | bytes 12582912 | tf_op jit(solution)/shard_map/pallas_call | solution.py:591
  696.9 21.2 %shard_map.505 = (bf16[1024,6656]{1,0:T(8,128)(2,1)}, f32[512,1024]{1,0:T(8,128)}, f32[8,1024]{1,0:T(8,128)}) custom-call(bf16[512,1024]{1,0:T(8,128)(2,1)S(1)} %copy-done.17, bf16[512,1024]{1,0:T(8,128)(2,1)} %convert_element_type.181.dout, bf16[512,2048]{1,0:T(8,128)(2,1)} %get-tuple-element.436.dgate, bf16[512,2048]{1,0:T(8,128)(2,1)} %get-tuple-element.441.dx, ...), custom_call_target="tpu_custom_call" | custom-call | flops 10737418240 | bytes 54525952 | tf_op jit(solution)/shard_map/pallas_call | solution.py:690
  719.8 5.5 shard_map.506
  742.4 8.8 collective-permute-done.73
  753.5 7.0 collective-permute-start.77
  765.2 8.3 shard_map.507
  773.5 14.0 %collective-permute-done.76 = bf16[128,1920]{1,0:T(8,128)(2,1)} collective-permute-done((bf16[128,1920]{1,0:T(8,128)(2,1)}, bf16[128,1920]{1,0:T(8,128)(2,1)}, u32[]{:S(2)}, u32[]{:S(2)}) %collective-permute-start.76) | collective-permute-done | bytes 491552 | tf_op jit(solution)/shard_map/ppermute | solution.py:1011
  787.5 10.4 %collective-permute-done.77 = bf16[128,1920]{1,0:T(8,128)(2,1)} collective-permute-done((bf16[128,1920]{1,0:T(8,128)(2,1)}, bf16[128,1920]{1,0:T(8,128)(2,1)}, u32[]{:S(2)}, u32[]{:S(2)}) %collective-permute-start.77) | collective-permute-done | bytes 491552 | tf_op jit(solution)/shard_map/ppermute | solution.py:1011
  813.0 4.0 collective-permute-done.79
  830.8 5.9 collective-permute-done.91
  859.2 5.8 collective-permute-done.86
  865.0 18.5 %collective-permute-done.87 = bf16[128,1920]{1,0:T(8,128)(2,1)S(1)} collective-permute-done((bf16[128,1920]{1,0:T(8,128)(2,1)}, bf16[128,1920]{1,0:T(8,128)(2,1)S(1)}, u32[]{:S(2)}, u32[]{:S(2)}) %collective-permute-start.87) | collective-permute-done | bytes 491552 | tf_op jit(solution)/shard_map/ppermute | solution.py:1011
  893.2 10.4 %shard_map.510 = (f32[3200,512]{1,0:T(8,128)}, f32[8,512]{1,0:T(8,128)}) custom-call(s32[16384]{0:T(1024)S(1)} %bitcast.426, s32[64]{0:T(128)S(1)} %copy-done.50, s32[2]{0:T(128)} %get-tuple-element.755.where, bf16[8,128,512]{2,1,0:T(8,128)(2,1)} %bitcast_dynamic-update-slice_fusion.7.packed, bf16[3200,512]{1,0:T(8,128)(2,1)} %pad_maximum_fusion.3.base), custom_call_target="tpu_custom_call" | custom-call | bytes 13107200 | tf_op jit(solution)/shard_map/pallas_call | solution.py:882
  909.6 10.6 %collective-permute-start.97 = (f32[128]{0:T(128)S(1)}, f32[128]{0:T(128)S(1)}, u32[]{:S(2)}, u32[]{:S(2)}) collective-permute-start(f32[128]{0:T(128)S(1)} %pad_add_fusion.12), channel_id=1, source_target_pairs={{0,1},{1,0},{2,3},{3,2},{4,5},{5,4},{6,7},{7,6},{8,9},{9,8},{10,11... | collective-permute-start | bytes 1544 | tf_op jit(solution)/shard_map/ppermute | solution.py:1028
  924.6 3.8 collective-permute-done.99
  937.1 7.8 shard_map.511
  945.6 13.8 %multiply_reduce_fusion = (f32[]{:T(128)}, f32[3143,512]{1,0:T(8,128)S(1)}, f32[3143,512]{1,0:T(8,128)}) fusion(f32[3143,512]{1,0:T(8,128)} %param.47, f32[]{:T(128)} %min.3, f32[3200,512]{1,0:T(8,128)} %get-tuple-element.504, f32[3143,512]{1,0:T(8,128)} %param.48, f32[3143,512]{1,0:T(8,128)} %param.49), kind=kLoop, calls=%fused_computation.137 | loop fusion | flops 24138240 | bytes 38621192 | tf_op jit(solution)/shard_map/reduce_sum | solution.py:1259
  962.6 3.8 collective-permute-start.106
  974.8 7.0 multiply_subtract_fusion
  (601 shorter events, 291.3 us)
Async XLA Ops:
  7.2 121.5 %all-gather.9.cloned.1.call-start = ((), (), s32[]{:S(2)}) async-start(), calls=%async_computation.5 | async-start | bytes 14745600 | tf_op jit(solution)/shard_map/all_gather | solution.py:1407
  12.5 157.2 %all-gather.11.cloned.1.call-start = ((), (), s32[]{:S(2)}) async-start(), calls=%async_computation.6 | async-start | bytes 14745600 | tf_op jit(solution)/shard_map/all_gather | solution.py:1429
  12.7 8.7 collective-permute-start.31
  13.9 44.7 %collective-permute-start.28 = (f32[2,9,512]{2,0,1:T(2,128)}, f32[2,9,512]{2,0,1:T(2,128)S(1)}, u32[]{:S(2)}, u32[]{:S(2)}) collective-permute-start(f32[2,9,512]{2,0,1:T(2,128)} %fusion.67), channel_id=1, source_target_pairs={{0,1},{1,2},{2,3},{3,0},{4,5},{5,6},{6,7},{7,4},{8,9},{9,10},{10,1... | collective-permute-start | bytes 110600 | tf_op jit(solution)/shard_map/ppermute | solution.py:1011
  51.3 9.2 collective-permute-start.29
  51.4 9.6 collective-permute-start.30
  55.8 17.2 %collective-permute-start.25 = (bf16[192,1024]{1,0:T(8,128)(2,1)}, bf16[192,1024]{1,0:T(8,128)(2,1)S(1)}, u32[]{:S(2)}, u32[]{:S(2)}) collective-permute-start(bf16[192,1024]{1,0:T(8,128)(2,1)} %pad_maximum_fusion.22), channel_id=1, source_target_pairs={{0,1},{1,2},{2,3},{3,0},{4,5},{5,6},{6,7},{7,4},{8,9},{9,10},{10,1... | collective-permute-start | bytes 1179656 | tf_op jit(solution)/shard_map/ppermute | solution.py:1011
  56.5 28.4 %collective-permute-start.26 = (bf16[192,1024]{1,0:T(8,128)(2,1)}, bf16[192,1024]{1,0:T(8,128)(2,1)}, u32[]{:S(2)}, u32[]{:S(2)}) collective-permute-start(bf16[192,1024]{1,0:T(8,128)(2,1)} %pad_maximum_fusion.22), channel_id=1, source_target_pairs={{0,2},{1,3},{2,0},{3,1},{4,6},{5,7},{6,4},{7,5},{8,10},{9,11},{10,... | collective-permute-start | bytes 1179656 | tf_op jit(solution)/shard_map/ppermute | solution.py:1011
  58.6 26.4 %collective-permute-start.27 = (bf16[192,1024]{1,0:T(8,128)(2,1)}, bf16[192,1024]{1,0:T(8,128)(2,1)}, u32[]{:S(2)}, u32[]{:S(2)}) collective-permute-start(bf16[192,1024]{1,0:T(8,128)(2,1)} %pad_maximum_fusion.22), channel_id=1, source_target_pairs={{0,3},{1,0},{2,1},{3,2},{4,7},{5,4},{6,5},{7,6},{8,11},{9,8},{10,9... | collective-permute-start | bytes 1179656 | tf_op jit(solution)/shard_map/ppermute | solution.py:1011
  88.7 159.0 %all-gather.13.cloned.1.call-start = ((), (), s32[]{:S(2)}) async-start(), calls=%async_computation.7 | async-start | bytes 15040512 | tf_op jit(solution)/shard_map/all_gather | solution.py:1431
  89.5 235.5 %all-gather.15.cloned.1.call-start = ((), (), s32[]{:S(2)}) async-start(), calls=%async_computation.8 | async-start | bytes 15040512 | tf_op jit(solution)/shard_map/all_gather | solution.py:1463
  90.4 19.0 %collective-permute-start.48 = (bf16[192,1024]{1,0:T(8,128)(2,1)}, bf16[192,1024]{1,0:T(8,128)(2,1)S(1)}, u32[]{:S(2)}, u32[]{:S(2)}) collective-permute-start(bf16[192,1024]{1,0:T(8,128)(2,1)} %pad_maximum_fusion.23), channel_id=1, source_target_pairs={{0,1},{1,2},{2,3},{3,0},{4,5},{5,6},{6,7},{7,4},{8,9},{9,10},{10,1... | collective-permute-start | bytes 1179656 | tf_op jit(solution)/shard_map/ppermute | solution.py:1011
  99.2 25.8 %collective-permute-start.49 = (bf16[192,1024]{1,0:T(8,128)(2,1)}, bf16[192,1024]{1,0:T(8,128)(2,1)S(1)}, u32[]{:S(2)}, u32[]{:S(2)}) collective-permute-start(bf16[192,1024]{1,0:T(8,128)(2,1)} %pad_maximum_fusion.23), channel_id=1, source_target_pairs={{0,2},{1,3},{2,0},{3,1},{4,6},{5,7},{6,4},{7,5},{8,10},{9,11},{10,... | collective-permute-start | bytes 1179656 | tf_op jit(solution)/shard_map/ppermute | solution.py:1011
  99.5 25.5 %collective-permute-start.50 = (bf16[192,1024]{1,0:T(8,128)(2,1)}, bf16[192,1024]{1,0:T(8,128)(2,1)}, u32[]{:S(2)}, u32[]{:S(2)}) collective-permute-start(bf16[192,1024]{1,0:T(8,128)(2,1)} %pad_maximum_fusion.23), channel_id=1, source_target_pairs={{0,3},{1,0},{2,1},{3,2},{4,7},{5,4},{6,5},{7,6},{8,11},{9,8},{10,9... | collective-permute-start | bytes 1179656 | tf_op jit(solution)/shard_map/ppermute | solution.py:1011
  183.7 19.1 %collective-permute-start.43 = (bf16[128,1024]{1,0:T(8,128)(2,1)}, bf16[128,1024]{1,0:T(8,128)(2,1)}, u32[]{:S(2)}, u32[]{:S(2)}) collective-permute-start(bf16[128,1024]{1,0:T(8,128)(2,1)} %get-tuple-element.630), channel_id=1, source_target_pairs={{0,2},{1,3},{2,0},{3,1},{4,6},{5,7},{6,4},{7,5},{8,10},{9,11},{10,... | collective-permute-start | bytes 786440 | tf_op jit(solution)/shard_map/ppermute | solution.py:1011
  186.4 16.3 %collective-permute-start.44 = (bf16[128,1024]{1,0:T(8,128)(2,1)}, bf16[128,1024]{1,0:T(8,128)(2,1)}, u32[]{:S(2)}, u32[]{:S(2)}) collective-permute-start(bf16[128,1024]{1,0:T(8,128)(2,1)} %get-tuple-element.629), channel_id=1, source_target_pairs={{0,1},{1,2},{2,3},{3,0},{4,5},{5,6},{6,7},{7,4},{8,9},{9,10},{10,1... | collective-permute-start | bytes 786440 | tf_op jit(solution)/shard_map/ppermute | solution.py:1011
  187.1 15.9 %collective-permute-start.42 = (bf16[128,1024]{1,0:T(8,128)(2,1)}, bf16[128,1024]{1,0:T(8,128)(2,1)}, u32[]{:S(2)}, u32[]{:S(2)}) collective-permute-start(bf16[128,1024]{1,0:T(8,128)(2,1)} %get-tuple-element.631), channel_id=1, source_target_pairs={{0,3},{1,0},{2,1},{3,2},{4,7},{5,4},{6,5},{7,6},{8,11},{9,8},{10,9... | collective-permute-start | bytes 786440 | tf_op jit(solution)/shard_map/ppermute | solution.py:1011
  247.7 378.1 %reduce-scatter.10.cloned.1.call-start = ((), (), s32[]{:S(2)}) async-start(), calls=%async_computation.9 | async-start | bytes 16384000
  373.7 11.1 %collective-permute-start.53 = (bf16[128,1024]{1,0:T(8,128)(2,1)S(1)}, bf16[128,1024]{1,0:T(8,128)(2,1)S(1)}, u32[]{:S(2)}, u32[]{:S(2)}) collective-permute-start(bf16[128,1024]{1,0:T(8,128)(2,1)S(1)} %select_add_fusion), channel_id=1, source_target_pairs={{0,1},{1,2},{2,3},{3,0},{4,5},{5,6},{6,7},{7,4},{8,9},{9,10},{10,1... | collective-permute-start | bytes 786440 | tf_op jit(solution)/shard_map/ppermute | solution.py:1011
  375.2 20.2 %collective-permute-start.54 = (bf16[128,1024]{1,0:T(8,128)(2,1)S(1)}, bf16[128,1024]{1,0:T(8,128)(2,1)S(1)}, u32[]{:S(2)}, u32[]{:S(2)}) collective-permute-start(bf16[128,1024]{1,0:T(8,128)(2,1)S(1)} %select_add_fusion), channel_id=1, source_target_pairs={{0,2},{1,3},{2,0},{3,1},{4,6},{5,7},{6,4},{7,5},{8,10},{9,11},{10,... | collective-permute-start | bytes 786440 | tf_op jit(solution)/shard_map/ppermute | solution.py:1011
  377.6 17.8 %collective-permute-start.55 = (bf16[128,1024]{1,0:T(8,128)(2,1)S(1)}, bf16[128,1024]{1,0:T(8,128)(2,1)S(1)}, u32[]{:S(2)}, u32[]{:S(2)}) collective-permute-start(bf16[128,1024]{1,0:T(8,128)(2,1)S(1)} %select_add_fusion), channel_id=1, source_target_pairs={{0,3},{1,0},{2,1},{3,2},{4,7},{5,4},{6,5},{7,6},{8,11},{9,8},{10,9... | collective-permute-start | bytes 786440 | tf_op jit(solution)/shard_map/ppermute | solution.py:1011
  431.7 8.6 collective-permute-start.58
  502.4 224.2 %reduce-scatter.6.cloned.1.call-start = ((), (), s32[]{:S(2)}) async-start(), calls=%async_computation.3 | async-start | bytes 15335424 | tf_op jit(solution)/shard_map/reduce_scatter | solution.py:1510
  507.8 9.8 collective-permute-start.62
  508.7 22.1 %collective-permute-start.63 = (bf16[128,1024]{1,0:T(8,128)(2,1)S(1)}, bf16[128,1024]{1,0:T(8,128)(2,1)S(1)}, u32[]{:S(2)}, u32[]{:S(2)}) collective-permute-start(bf16[128,1024]{1,0:T(8,128)(2,1)S(1)} %get-tuple-element.650), channel_id=1, source_target_pairs={{0,2},{1,3},{2,0},{3,1},{4,6},{5,7},{6,4},{7,5},{8,10},{9,11},{10,... | collective-permute-start | bytes 786440 | tf_op jit(solution)/shard_map/ppermute | solution.py:1011
  508.8 22.1 %collective-permute-start.64 = (bf16[128,1024]{1,0:T(8,128)(2,1)S(1)}, bf16[128,1024]{1,0:T(8,128)(2,1)S(1)}, u32[]{:S(2)}, u32[]{:S(2)}) collective-permute-start(bf16[128,1024]{1,0:T(8,128)(2,1)S(1)} %get-tuple-element.649), channel_id=1, source_target_pairs={{0,1},{1,2},{2,3},{3,0},{4,5},{5,6},{6,7},{7,4},{8,9},{9,10},{10,1... | collective-permute-start | bytes 786440 | tf_op jit(solution)/shard_map/ppermute | solution.py:1011
  625.9 219.9 %reduce-scatter.8.cloned.1.call-start = ((), (), s32[]{:S(2)}) async-start(), calls=%async_computation.4 | async-start | bytes 15335424 | tf_op jit(solution)/shard_map/reduce_scatter | solution.py:1510
  728.6 13.7 %collective-permute-start.72 = (bf16[128,1024]{1,0:T(8,128)(2,1)}, bf16[128,1024]{1,0:T(8,128)(2,1)S(1)}, u32[]{:S(2)}, u32[]{:S(2)}) collective-permute-start(bf16[128,1024]{1,0:T(8,128)(2,1)} %get-tuple-element.647), channel_id=1, source_target_pairs={{0,1},{1,2},{2,3},{3,0},{4,5},{5,6},{6,7},{7,4},{8,9},{9,10},{10,1... | collective-permute-start | bytes 786440 | tf_op jit(solution)/shard_map/ppermute | solution.py:1011
  730.1 21.1 %collective-permute-start.73 = (bf16[128,1024]{1,0:T(8,128)(2,1)}, bf16[128,1024]{1,0:T(8,128)(2,1)S(1)}, u32[]{:S(2)}, u32[]{:S(2)}) collective-permute-start(bf16[128,1024]{1,0:T(8,128)(2,1)} %get-tuple-element.646), channel_id=1, source_target_pairs={{0,2},{1,3},{2,0},{3,1},{4,6},{5,7},{6,4},{7,5},{8,10},{9,11},{10,... | collective-permute-start | bytes 786440 | tf_op jit(solution)/shard_map/ppermute | solution.py:1011
  732.5 18.7 %collective-permute-start.74 = (bf16[128,1024]{1,0:T(8,128)(2,1)S(1)}, bf16[128,1024]{1,0:T(8,128)(2,1)S(1)}, u32[]{:S(2)}, u32[]{:S(2)}) collective-permute-start(bf16[128,1024]{1,0:T(8,128)(2,1)S(1)} %get-tuple-element.645), channel_id=1, source_target_pairs={{0,3},{1,0},{2,1},{3,2},{4,7},{5,4},{6,5},{7,6},{8,11},{9,8},{10,9... | collective-permute-start | bytes 786440 | tf_op jit(solution)/shard_map/ppermute | solution.py:1011
  741.2 32.2 %collective-permute-start.75 = (bf16[128,1920]{1,0:T(8,128)(2,1)}, bf16[128,1920]{1,0:T(8,128)(2,1)}, u32[]{:S(2)}, u32[]{:S(2)}) collective-permute-start(bf16[128,1920]{1,0:T(8,128)(2,1)} %get-tuple-element.455), channel_id=1, source_target_pairs={{0,1},{1,2},{2,3},{3,0},{4,5},{5,6},{6,7},{7,4},{8,9},{9,10},{10,1... | collective-permute-start | bytes 1474568 | tf_op jit(solution)/shard_map/ppermute | solution.py:1011
  741.4 46.1 %collective-permute-start.76 = (bf16[128,1920]{1,0:T(8,128)(2,1)}, bf16[128,1920]{1,0:T(8,128)(2,1)}, u32[]{:S(2)}, u32[]{:S(2)}) collective-permute-start(bf16[128,1920]{1,0:T(8,128)(2,1)} %get-tuple-element.456), channel_id=1, source_target_pairs={{0,2},{1,3},{2,0},{3,1},{4,6},{5,7},{6,4},{7,5},{8,10},{9,11},{10,... | collective-permute-start | bytes 1474568 | tf_op jit(solution)/shard_map/ppermute | solution.py:1011
  753.5 44.3 %collective-permute-start.77 = (bf16[128,1920]{1,0:T(8,128)(2,1)}, bf16[128,1920]{1,0:T(8,128)(2,1)}, u32[]{:S(2)}, u32[]{:S(2)}) collective-permute-start(bf16[128,1920]{1,0:T(8,128)(2,1)} %get-tuple-element.457), channel_id=1, source_target_pairs={{0,3},{1,0},{2,1},{3,2},{4,7},{5,4},{6,5},{7,6},{8,11},{9,8},{10,9... | collective-permute-start | bytes 1474568 | tf_op jit(solution)/shard_map/ppermute | solution.py:1011
  807.8 47.7 %collective-permute-start.85 = (bf16[1600,512]{1,0:T(8,128)(2,1)}, bf16[1600,512]{1,0:T(8,128)(2,1)}, u32[]{:S(2)}, u32[]{:S(2)}) collective-permute-start(bf16[1600,512]{1,0:T(8,128)(2,1)} %select_bitcast_fusion), channel_id=1, source_target_pairs={{0,4},{4,0},{1,5},{5,1},{2,6},{6,2},{3,7},{7,3},{8,12},{12,8},{9,1... | collective-permute-start | bytes 4915208 | tf_op jit(solution)/shard_map/ppermute | solution.py:1015
  807.9 9.1 collective-permute-start.79
  809.2 12.8 %collective-permute-start.80 = (bf16[128,512]{1,0:T(8,128)(2,1)S(1)}, bf16[128,512]{1,0:T(8,128)(2,1)S(1)}, u32[]{:S(2)}, u32[]{:S(2)}) collective-permute-start(bf16[128,512]{1,0:T(8,128)(2,1)S(1)} %get-tuple-element.640), channel_id=1, source_target_pairs={{0,12},{4,8},{8,4},{12,0},{16,28},{20,24},{24,20},{28,16},{1,13},{... | collective-permute-start | bytes 393224 | tf_op jit(solution)/shard_map/ppermute | solution.py:1028
  810.6 12.6 %collective-permute-start.81 = (bf16[128,512]{1,0:T(8,128)(2,1)S(1)}, bf16[128,512]{1,0:T(8,128)(2,1)S(1)}, u32[]{:S(2)}, u32[]{:S(2)}) collective-permute-start(bf16[128,512]{1,0:T(8,128)(2,1)S(1)} %get-tuple-element.639), channel_id=1, source_target_pairs={{0,16},{4,20},{8,24},{12,28},{16,0},{20,4},{24,8},{28,12},{1,17},{... | collective-permute-start | bytes 393224 | tf_op jit(solution)/shard_map/ppermute | solution.py:1028
  812.6 13.6 %collective-permute-start.82 = (bf16[128,512]{1,0:T(8,128)(2,1)S(1)}, bf16[128,512]{1,0:T(8,128)(2,1)S(1)}, u32[]{:S(2)}, u32[]{:S(2)}) collective-permute-start(bf16[128,512]{1,0:T(8,128)(2,1)S(1)} %get-tuple-element.638), channel_id=1, source_target_pairs={{0,20},{4,16},{8,28},{12,24},{16,4},{20,0},{24,12},{28,8},{1,21},{... | collective-permute-start | bytes 393224 | tf_op jit(solution)/shard_map/ppermute | solution.py:1028
  817.7 12.5 %collective-permute-start.83 = (bf16[128,512]{1,0:T(8,128)(2,1)S(1)}, bf16[128,512]{1,0:T(8,128)(2,1)S(1)}, u32[]{:S(2)}, u32[]{:S(2)}) collective-permute-start(bf16[128,512]{1,0:T(8,128)(2,1)S(1)} %get-tuple-element.637), channel_id=1, source_target_pairs={{0,24},{4,28},{8,16},{12,20},{16,8},{20,12},{24,0},{28,4},{1,25},{... | collective-permute-start | bytes 393224 | tf_op jit(solution)/shard_map/ppermute | solution.py:1028
  822.6 8.2 collective-permute-start.90
  823.9 12.8 %collective-permute-start.91 = (f32[252,128]{1,0:T(8,128)S(1)}, f32[252,128]{1,0:T(8,128)S(1)}, u32[]{:S(2)}, u32[]{:S(2)}) collective-permute-start(f32[252,128]{1,0:T(8,128)S(1)} %add.542), channel_id=1, source_target_pairs={{0,2},{1,3},{2,0},{3,1},{4,6},{5,7},{6,4},{7,5},{8,10},{9,11},{10,... | collective-permute-start | bytes 387080 | tf_op jit(solution)/shard_map/ppermute | solution.py:1028
  826.9 9.9 collective-permute-start.92
  830.8 9.5 collective-permute-start.84
  838.2 7.5 collective-permute-start.94
  848.7 16.3 %collective-permute-start.86 = (bf16[128,1920]{1,0:T(8,128)(2,1)}, bf16[128,1920]{1,0:T(8,128)(2,1)S(1)}, u32[]{:S(2)}, u32[]{:S(2)}) collective-permute-start(bf16[128,1920]{1,0:T(8,128)(2,1)} %get-tuple-element.473), channel_id=1, source_target_pairs={{0,1},{1,2},{2,3},{3,0},{4,5},{5,6},{6,7},{7,4},{8,9},{9,10},{10,1... | collective-permute-start | bytes 1474568 | tf_op jit(solution)/shard_map/ppermute | solution.py:1011
  851.9 31.6 %collective-permute-start.87 = (bf16[128,1920]{1,0:T(8,128)(2,1)}, bf16[128,1920]{1,0:T(8,128)(2,1)S(1)}, u32[]{:S(2)}, u32[]{:S(2)}) collective-permute-start(bf16[128,1920]{1,0:T(8,128)(2,1)} %get-tuple-element.474), channel_id=1, source_target_pairs={{0,2},{1,3},{2,0},{3,1},{4,6},{5,7},{6,4},{7,5},{8,10},{9,11},{10,... | collective-permute-start | bytes 1474568 | tf_op jit(solution)/shard_map/ppermute | solution.py:1011
  852.6 30.9 %collective-permute-start.88 = (bf16[128,1920]{1,0:T(8,128)(2,1)}, bf16[128,1920]{1,0:T(8,128)(2,1)S(1)}, u32[]{:S(2)}, u32[]{:S(2)}) collective-permute-start(bf16[128,1920]{1,0:T(8,128)(2,1)} %get-tuple-element.475), channel_id=1, source_target_pairs={{0,3},{1,0},{2,1},{3,2},{4,7},{5,4},{6,5},{7,6},{8,11},{9,8},{10,9... | collective-permute-start | bytes 1474568 | tf_op jit(solution)/shard_map/ppermute | solution.py:1011
  909.6 13.5 %collective-permute-start.97 = (f32[128]{0:T(128)S(1)}, f32[128]{0:T(128)S(1)}, u32[]{:S(2)}, u32[]{:S(2)}) collective-permute-start(f32[128]{0:T(128)S(1)} %pad_add_fusion.12), channel_id=1, source_target_pairs={{0,1},{1,0},{2,3},{3,2},{4,5},{5,4},{6,7},{7,6},{8,9},{9,8},{10,11... | collective-permute-start | bytes 1544 | tf_op jit(solution)/shard_map/ppermute | solution.py:1028
  (114 other events, 1632.2 us)
Sparse Core Ops, SparseCore 0:
  12.6 77.8 all-gather.8
  93.0 76.6 all-gather.10
  172.2 75.4 all-gather.12
  249.5 75.4 all-gather.14
  502.5 122.6 reduce-scatter.9
  628.6 97.9 reduce-scatter.5
  730.1 107.3 reduce-scatter.7
